TPU v7x, 32 devices: a whole 2x2x4 slice. The times are simulated.
32 devices in a mesh: fsdp: 4 (over y, core), expert: 8 (over z, x).
Axes of the slice: x: 2, y: 2, z: 4, core: 2. Of those that a mesh axis runs over, the one named last changes fastest.
Arguments:
- tokens: bfloat16 [512, 4096], P(('fsdp', 'expert')), may hold values from -18 to 18
- learner_rows: bfloat16 [16, 3, 768, 4096], P(None, None, 'expert', 'fsdp'), may hold values from -0.25 to 0.25, as said below
- exponents: int32 [16, 3, 768, 128], P(None, None, 'expert', 'fsdp'), may hold values from -9 to -5
- expert_ids: int32 [512, 8], P(('fsdp', 'expert')), may hold values from 0 to 15, all different within a row; in each aligned block of 16 rows (0 to 15, 16 to 31, ...) at most 16 rows name the same one
- route_probs: float32 [512, 8], P(('fsdp', 'expert')), may hold values from 0.05 to 1
Outputs:
- rollout_elements: bfloat16 [16, 3, 768, 4096], P('expert', None, None, 'fsdp')
- mixed: bfloat16 [512, 4096], P(('fsdp', 'expert'))
Inputs may be any that keep to these rules, and one draw needn't show every extreme that they name: `expert_ids`: each row names 8 different experts. Among the rows of one device no expert is named more than 16 times, a bound that some block reaches. `learner_rows`: each entry is at most 8 times its block's scale 2 ** exponent in magnitude.
All inputs are finite; a program needn't handle non-finite values.
Results may differ from a plain program's by a relative error of at most 0.02.
Values may be sent and summed in bfloat16 or wider, within the bound.
No kernel may reach another device: no remote copies, remote signals or barrier semaphores. Data moves between devices by JAX's collectives and lax.ppermute only.
A program may use at most 128 MiB of HBM per device.

v0:
```python
import jax
import jax.numpy as jnp
from jax import lax
from jax.sharding import PartitionSpec as P

BLOCK = 32


def to_grid(ratio):
    clipped = jnp.clip(ratio.astype(jnp.float32), -6.0, 6.0)
    magnitude = jnp.abs(clipped)
    level = (
        0.5 * (magnitude > 0.25)
        + 0.5 * (magnitude >= 0.75)
        + 0.5 * (magnitude > 1.25)
        + 0.5 * (magnitude >= 1.75)
    )
    level = level + 1.0 * (magnitude > 2.5) + 1.0 * (magnitude >= 3.5) + 2.0 * (magnitude > 5.0)
    return (jnp.sign(clipped) * level.astype(jnp.float32)).astype(jnp.bfloat16)


def body(tokens, learner_rows, exponents, expert_ids, route_probs):
    experts, part_count, unit_rows, feat_cols = learner_rows.shape
    owners = lax.axis_size("expert")
    groups = lax.axis_size("fsdp")
    per_owner = experts // owners
    tok_rows, top_count = expert_ids.shape
    width = tokens.shape[1]
    capacity = 2 * tok_rows * top_count // experts
    scales = jnp.exp2(exponents.astype(jnp.float32)).astype(jnp.bfloat16)
    widened = jnp.repeat(scales, BLOCK, axis=3)
    elements = to_grid(learner_rows / widened)
    element_view = elements.reshape(owners, per_owner, part_count, unit_rows, feat_cols)
    scale_view = scales.reshape(owners, per_owner, part_count, unit_rows, feat_cols // BLOCK)
    flat_ids = expert_ids.reshape(-1)
    one_hot = (flat_ids[:, None] == jnp.arange(experts, dtype=jnp.int32)[None, :]).astype(jnp.int32)
    position = jnp.sum((jnp.cumsum(one_hot, axis=0) - one_hot) * one_hot, axis=1)
    slot_index = flat_ids * capacity + position
    picked = (
        slot_index[:, None] == jnp.arange(experts * capacity, dtype=jnp.int32)[None, :]
    ).astype(jnp.float32)
    picked = picked.reshape(tok_rows, top_count, experts * capacity)
    routing = jnp.sum(picked, axis=1).astype(jnp.bfloat16)
    route_share = route_probs / jnp.sum(route_probs, axis=1, keepdims=True)
    blend_table = jnp.sum(picked * route_share[:, :, None], axis=1)
    packed = lax.dot_general(
        routing, tokens, (((0,), (0,)), ((), ())), preferred_element_type=jnp.float32
    )
    packed_view = packed.astype(jnp.bfloat16).reshape(owners, per_owner, 1, capacity, width)
    element_got, scale_got = (
        lax.all_to_all(element_view, "expert", split_axis=0, concat_axis=3, tiled=True),
        lax.all_to_all(scale_view, "expert", split_axis=0, concat_axis=3, tiled=True),
    )
    slot_got = lax.all_to_all(
        lax.all_to_all(packed_view, "fsdp", split_axis=4, concat_axis=3, tiled=True),
        "expert",
        split_axis=0,
        concat_axis=3,
        tiled=True,
    )
    weights = element_got[0] * jnp.repeat(scale_got[0], BLOCK, axis=3)
    slot_rows = slot_got[0, :, 0]
    paired = weights[:, 0:2]
    down_rows = weights[:, 2]
    summed = lax.psum_scatter(
        jnp.einsum("ksd,kghd->skgh", slot_rows, paired, preferred_element_type=jnp.float32).astype(
            jnp.bfloat16
        ),
        "fsdp",
        scatter_dimension=0,
        tiled=True,
    ).astype(jnp.float32)
    hidden = (jax.nn.silu(summed[:, :, 0]) * summed[:, :, 1]).astype(jnp.bfloat16)
    result = jnp.einsum(
        "skh,khd->ksd",
        lax.all_gather(hidden, "fsdp", axis=0, tiled=True),
        down_rows,
        preferred_element_type=jnp.float32,
    )
    output = result.astype(jnp.bfloat16)
    served = output[None, :, None]
    served_rows = served[0, :, 0]
    back_view = served_rows.reshape(per_owner, owners, groups, capacity, served_rows.shape[2])
    returned = lax.all_to_all(
        lax.all_to_all(back_view, "fsdp", split_axis=2, concat_axis=4, tiled=True),
        "expert",
        split_axis=1,
        concat_axis=0,
        tiled=True,
    )
    gathered = returned.reshape(experts * capacity, width).astype(jnp.float32)
    mixed = jnp.dot(
        blend_table, gathered, precision=lax.Precision.HIGHEST, preferred_element_type=jnp.float32
    )
    return (element_got[0], mixed.astype(jnp.bfloat16))


def solution(mesh):
    return jax.shard_map(
        body,
        mesh=mesh,
        in_specs=(
            P(("fsdp", "expert"), None),
            P(None, None, "expert", "fsdp"),
            P(None, None, "expert", "fsdp"),
            P(("fsdp", "expert"), None),
            P(("fsdp", "expert"), None),
        ),
        out_specs=(P("expert", None, None, "fsdp"), P(("fsdp", "expert"), None)),
        check_vma=False,
    )
```

profile of v0, /device:TPU:8, one launch (start us, length us, event | category | flops | bytes accessed | tf_op | source)
XLA Modules:
  0.0 604.0 jit_solution(12376015859870750090)
XLA Ops:
  7.2 0.0 copy-start
  7.2 0.8 copy.45
  8.0 0.1 eq.29
  8.1 0.1 fusion.12
  8.2 0.2 reduce_window_sum.11
  8.3 0.2 select_reduce_fusion.1
  8.5 0.1 reduce_sum.39
  8.6 0.7 reduce_sum.40
  9.3 0.7 broadcast_divide_fusion
  10.0 0.1 copy.47
  10.1 0.2 convert_reduce_fusion
  10.2 0.0 copy-done
  10.3 0.7 convolution_convert_fusion
  11.0 27.8 %copy.50 = bf16[8,2,1,16,4096]{3,1,0,2,4:T(2,128)(2,1)} copy(bf16[8,2,1,16,4096]{4,3,1,0,2:T(8,128)(2,1)S(1)} %bitcast.77) | data formatting | bytes 4194304 | tf_op jit(solution)/shard_map/reshape | solution.py:49
  38.8 0.0 copy-start.4
  38.8 20.4 %reshape.57 = bf16[4,2,131072]{2,1,0:T(2,128)(2,1)} reshape(bf16[4096,1,8,2,16]{4,3,2,1,0:T(2,128)(2,1)} %bitcast.71) | data formatting | bytes 4194304
  59.2 3.6 all-to-all-start.2
  62.8 0.0 copy-done.4
  62.8 0.9 exponential_convert_fusion
  63.7 24.8 %all-to-all-done.2 = bf16[4,2,131072]{2,1,0:T(2,128)(2,1)S(1)} async-done(((bf16[4,2,131072]{2,1,0:T(2,128)(2,1)}), bf16[4,2,131072]{2,1,0:T(2,128)(2,1)S(1)}, u32[]{:S(2)}, u32[]{:S(2)}) %all-to-all-start.2) | async-done | bytes 2097184 | tf_op jit(solution)/shard_map/all_to_all | solution.py:55
  88.5 6.3 %all-to-all-start.1 = ((bf16[8,2,3,96,32]{3,4,2,1,0:T(8,128)(2,1)}), bf16[8,2,3,96,32]{3,4,2,1,0:T(8,128)(2,1)S(1)}, u32[]{:S(2)}, u32[]{:S(2)}) async-start(bf16[8,2,3,96,32]{3,4,2,1,0:T(8,128)(2,1)} %bitcast.5), calls=%async_computation.1 | async-start | bytes 786432 | tf_op jit(solution)/shard_map/all_to_all | solution.py:52
  94.7 13.5 %reshape.58 = bf16[4096,1,8,2,16]{4,3,2,1,0:T(2,128)(2,1)} reshape(bf16[4,2,131072]{2,1,0:T(2,128)(2,1)S(1)} %all-to-all-done.2) | data formatting | bytes 4194304
  108.2 37.7 %copy.51 = bf16[8,2,1,4,16,1024]{5,4,3,1,0,2:T(8,128)(2,1)} copy(bf16[8,2,1,4,16,1024]{4,1,0,5,3,2:T(2,128)(2,1)} %bitcast.72) | data formatting | bytes 4194304 | tf_op jit(solution)/shard_map/all_to_all | solution.py:55
  145.9 0.0 all-to-all-done.1
  145.9 6.0 all-to-all-start.3
  151.9 14.7 %copy.42 = bf16[16,3,96,1024]{2,3,1,0:T(8,128)(2,1)} copy(bf16[16,3,96,1024]{3,2,1,0:T(8,128)(2,1)} %param.6) | data formatting | bytes 18874368 | tf_op args[1]
  166.6 30.3 %multiply_convert_fusion = bf16[16,3,96,1024]{2,3,1,0:T(8,128)(2,1)} fusion(bf16[16,3,96,1024]{2,3,1,0:T(8,128)(2,1)} %copy.42, bf16[16,3,96,32]{2,3,1,0:T(8,128)(2,1)} %exponential_convert_fusion), kind=kLoop, calls=%fused_computation | loop fusion | flops 127401984 | bytes 19169280 | tf_op jit(solution)/shard_map/convert_element_type | solution.py:19
  196.8 14.7 %copy.43 = bf16[8,2,3,96,1024]{4,3,2,1,0:T(8,128)(2,1)} copy(bf16[8,2,3,96,1024]{3,4,2,1,0:T(8,128)(2,1)} %bitcast.73) | data formatting | bytes 18874368 | tf_op jit(solution)/shard_map/reshape | solution.py:33
  211.5 0.0 all-to-all-done.3
  211.5 6.0 all-to-all-start
  217.5 0.0 reduce-scatter.4.cloned.1.call-start
  217.5 0.3 copy.48
  217.8 0.3 squeeze.20
  218.1 4.4 broadcast_in_dim.5
  222.5 12.7 %copy.49 = bf16[2,3,768,1024]{3,2,1,0:T(8,128)(2,1)} copy(bf16[2,3,768,1024]{2,3,1,0:T(8,128)(2,1)} %bitcast.76) | data formatting | bytes 18874368 | tf_op jit(solution)/shard_map/reshape | solution.py:61
  235.2 1.6 copy.52
  236.7 182.5 %all-to-all-done = bf16[8,2,3,96,1024]{4,3,2,1,0:T(8,128)(2,1)} async-done(((bf16[8,2,3,96,1024]{4,3,2,1,0:T(8,128)(2,1)}), bf16[8,2,3,96,1024]{4,3,2,1,0:T(8,128)(2,1)}, u32[]{:S(2)}, u32[]{:S(2)}) %all-to-all-start) | async-done | bytes 9437216 | tf_op jit(solution)/shard_map/all_to_all | solution.py:51
  419.3 9.4 %copy.44 = bf16[1,2,3,8,96,1024]{5,4,3,2,1,0:T(8,128)(2,1)} copy(bf16[1,2,3,8,96,1024]{5,4,2,1,3,0:T(8,128)(2,1)} %bitcast.3) | data formatting | bytes 18874368 | tf_op jit(solution)/shard_map/all_to_all | solution.py:51
  428.6 0.0 copy-start.3
  428.6 8.8 %mul.64 = bf16[2,3,768,1024]{3,2,1,0:T(8,128)(2,1)S(1)} multiply(bf16[2,3,768,1024]{3,2,1,0:T(8,128)(2,1)} %bitcast.74, bf16[2,3,768,1024]{3,2,1,0:T(8,128)(2,1)} %copy.49) | non-fusion elementwise | flops 4718592 | bytes 28311552 | tf_op jit(solution)/shard_map/mul | solution.py:61
  437.5 0.0 copy-start.2
  437.5 0.0 copy-done.3
  437.5 3.7 convolution_convert_fusion.2
  441.2 0.0 copy-done.2
  441.2 3.1 copy.61
  444.3 0.0 reduce-scatter.4.cloned.1.call-update
  444.3 0.3 all-gather.2.cloned.1.call-start
  444.6 38.1 %reduce-scatter.4.cloned.1.call-done = bf16[128,3072]{1,0:T(8,128)(2,1)} async-done(((bf16[512,3072]{1,0:T(8,128)(2,1)}), bf16[128,3072]{1,0:T(8,128)(2,1)}) %reduce-scatter.4.cloned.1.call-update) | async-done | bytes 786448
  482.7 1.5 copy.62
  484.2 0.3 copy.53
  484.5 0.1 convert_element_type.67
  484.6 1.0 fusion.11
  485.6 0.0 all-gather.2.cloned.1.call-update
  485.6 19.8 %all-gather.2.cloned.1.call-done = bf16[512,2,768]{2,0,1:T(8,128)(2,1)} async-done(((bf16[128,2,768]{2,0,1:T(8,128)(2,1)}), bf16[512,2,768]{2,0,1:T(8,128)(2,1)}) %all-gather.2.cloned.1.call-update) | async-done | bytes 1572880 | tf_op jit(solution)/shard_map/all_gather | solution.py:76
  505.4 4.2 fusion.9
  509.6 0.0 copy-start.1
  509.6 0.2 copy.54
  509.8 28.2 %all_to_all.96 = bf16[2,8,4,16,1024]{4,3,1,0,2:T(8,128)(2,1)S(1)} all-to-all(bf16[2,8,4,16,1024]{4,3,1,0,2:T(8,128)(2,1)S(1)} %copy.54), channel_id=1, replica_groups=mesh['fsdp'=4,'expert'=8] {'fsdp'}, dimensions={2} | all-to-all | bytes 4194304 | tf_op jit(solution)/shard_map/all_to_all | solution.py:85
  538.0 1.8 copy.58
  539.7 2.8 reshape.54
  542.5 53.0 %all_to_all.97 = bf16[2,8,1,16,4096]{4,3,0,2,1:T(8,128)(2,1)S(1)} all-to-all(bf16[2,8,1,16,4096]{4,3,0,2,1:T(8,128)(2,1)} %reshape.54), channel_id=1, replica_groups=mesh['fsdp'=4,'expert'=8] {'expert'}, dimensions={1} | all-to-all | bytes 4194304 | tf_op jit(solution)/shard_map/all_to_all | solution.py:84
  595.5 1.6 convolution_convert_fusion.1
  597.1 0.0 copy-done.1
  (1 shorter events, 0.0 us)
Async XLA Ops:
  7.2 3.1 copy-start
  38.8 24.0 %copy-start.4 = (s32[16,3,96,32]{2,3,1,0:T(8,128)S(1)}, s32[16,3,96,32]{2,3,1,0:T(8,128)}, u32[]{:S(2)}) copy-start(s32[16,3,96,32]{2,3,1,0:T(8,128)} %param.7) | copy-start | bytes 1769476
  59.2 29.3 %all-to-all-start.2 = ((bf16[4,2,131072]{2,1,0:T(2,128)(2,1)}), bf16[4,2,131072]{2,1,0:T(2,128)(2,1)S(1)}, u32[]{:S(2)}, u32[]{:S(2)}) async-start(bf16[4,2,131072]{2,1,0:T(2,128)(2,1)} %reshape.57), calls=%async_computation.2 | async-start | bytes 4194304 | tf_op jit(solution)/shard_map/all_to_all | solution.py:55
  88.5 57.4 %all-to-all-start.1 = ((bf16[8,2,3,96,32]{3,4,2,1,0:T(8,128)(2,1)}), bf16[8,2,3,96,32]{3,4,2,1,0:T(8,128)(2,1)S(1)}, u32[]{:S(2)}, u32[]{:S(2)}) async-start(bf16[8,2,3,96,32]{3,4,2,1,0:T(8,128)(2,1)} %bitcast.5), calls=%async_computation.1 | async-start | bytes 786432 | tf_op jit(solution)/shard_map/all_to_all | solution.py:52
  145.9 65.6 %all-to-all-start.3 = ((bf16[8,2,1,64,1024]{4,3,1,2,0:T(8,128)(2,1)}), bf16[8,2,1,64,1024]{4,3,1,2,0:T(8,128)(2,1)S(1)}, u32[]{:S(2)}, u32[]{:S(2)}) async-start(bf16[8,2,1,64,1024]{4,3,1,2,0:T(8,128)(2,1)} %bitcast.12), calls=%async_computation.3 | async-start | bytes 4194304 | tf_op jit(solution)/shard_map/all_to_all | solution.py:54
  211.5 207.8 %all-to-all-start = ((bf16[8,2,3,96,1024]{4,3,2,1,0:T(8,128)(2,1)}), bf16[8,2,3,96,1024]{4,3,2,1,0:T(8,128)(2,1)}, u32[]{:S(2)}, u32[]{:S(2)}) async-start(bf16[8,2,3,96,1024]{4,3,2,1,0:T(8,128)(2,1)} %copy.43), calls=%async_computation | async-start | bytes 18874368 | tf_op jit(solution)/shard_map/all_to_all | solution.py:51
  217.5 265.2 %reduce-scatter.4.cloned.1.call-start = ((), (), s32[]{:S(2)}) async-start(), calls=%async_computation.8 | async-start | bytes 3932160
  428.6 8.9 %copy-start.3 = (bf16[1,2,1,8,64,1024]{5,4,3,1,2,0:T(8,128)(2,1)S(1)}, bf16[1,2,1,8,64,1024]{5,4,3,1,2,0:T(8,128)(2,1)}, u32[]{:S(2)}) copy-start(bf16[1,2,1,8,64,1024]{5,4,3,1,2,0:T(8,128)(2,1)} %copy.52) | copy-start | bytes 6291460
  437.5 3.7 copy-start.2
  444.3 61.1 %all-gather.2.cloned.1.call-start = ((), (), s32[]{:S(2)}) async-start(), calls=%async_computation.7 | async-start | bytes 1966080 | tf_op jit(solution)/shard_map/all_gather | solution.py:76
  509.6 87.5 %copy-start.1 = (bf16[16,4096]{1,0:T(8,128)(2,1)S(1)}, bf16[16,4096]{1,0:T(8,128)(2,1)}, u32[]{:S(2)}) copy-start(bf16[16,4096]{1,0:T(8,128)(2,1)} %param.5) | copy-start | bytes 393220
Sparse Core Ops, SparseCore 0:
  444.4 38.1 reduce-scatter.3
  485.7 19.6 all-gather.1
where the time goes:
time: 609 us; the launch traced here: 604 us
  waiting for transfers between devices  265 us (44%)
  local copies, waits for them, and re-layouts  168 us (28%)
  blocking collectives  81.2 us (13%)
  other arithmetic  43.1 us (7%)
  starting transfers between devices  22.1 us (4%)
  between operations  14.2 us (2%)
  matrix products  10.2 us (2%)
    all_to_all x1, waiting for transfers between devices, body(): lax.all_to_all(element_view, 'expert', split_axis=0, concat_axis=3, tiled...  183 us
    unnamed x16, local copies, waits for them, and re-layouts  53.9 us
    all_to_all x1, blocking collectives, body(): lax.all_to_all(lax.all_to_all(back_view, 'fsdp', split_axis=2, concat_axi...  53 us
    unnamed x3, waiting for transfers between devices  38.1 us
    all_to_all x1, local copies, waits for them, and re-layouts, body(): lax.all_to_all(packed_view, 'fsdp', split_axis=4, concat_axis=3, tiled=True)  37.7 us
    convert_element_type x1, other arithmetic, to_grid(): return (jnp.sign(clipped) * level.astype(jnp.float32)).astype(jnp.bfloat16)  30.3 us
    all_to_all x1, blocking collectives, body(): lax.all_to_all(back_view, 'fsdp', split_axis=2, concat_axis=4, tiled=True)  28.2 us
    reshape x1, local copies, waits for them, and re-layouts, body(): packed.astype(jnp.bfloat16).reshape(owners, per_owner, 1, capacity, width)  27.8 us
  transfers between devices with their start and end apart: 6, of which 4 were waited for; matrix products, arithmetic and copies ran while one was open for 22% of the time, Pallas kernels for 0%

commit v1 on v0

v1 whole, which is shorter than its diff:
```python
import functools

import jax
import jax.numpy as jnp
from jax import lax
from jax.experimental import pallas as pl
from jax.experimental.pallas import tpu as pltpu
from jax.sharding import PartitionSpec as P

HALVES, ONES, TWOS = 1.5 * 2.0**22, 1.5 * 2.0**23, 1.5 * 2.0**24


def spread(values, width):
    blocks = values.shape[1]
    shape = (blocks, width)
    feature = lax.broadcasted_iota(jnp.int32, shape, 1)
    block = lax.broadcasted_iota(jnp.int32, shape, 0)
    size = width // blocks
    inside = (feature >= block * size) & (feature < (block + 1) * size)
    table = inside.astype(jnp.float32).astype(jnp.bfloat16)
    return jnp.dot(values.astype(jnp.bfloat16), table, preferred_element_type=jnp.float32)


def to_grid(rows, exponent):
    one = jnp.ones_like(exponent)
    inverse = lax.shift_left(one, -exponent).astype(jnp.float32)
    ratio = rows.astype(jnp.float32) * spread(inverse, rows.shape[1])
    ratio = jnp.clip(ratio, -6.0, 6.0)
    magnitude = jnp.abs(ratio)
    magic = jnp.where(magnitude < 2.0, HALVES, jnp.where(magnitude < 4.0, ONES, TWOS))
    return (ratio + magic) - magic


def encode_kernel(places, rows_ref, exponent_ref, out_ref):
    for part in range(rows_ref.shape[1]):
        value = to_grid(rows_ref[0, part], exponent_ref[0, part])
        out_ref[0, part] = value.astype(out_ref.dtype)


def encode(learner_rows, exponents, dest, row_block, out_rows):
    experts, parts, unit_rows, width = learner_rows.shape
    blocks = exponents.shape[3]
    per_owner = experts // lax.axis_size("expert")
    places = jnp.stack([dest, row_block]).astype(jnp.int32)
    return pl.pallas_call(
        encode_kernel,
        out_shape=jax.ShapeDtypeStruct((per_owner, parts, out_rows, width), learner_rows.dtype),
        grid_spec=pltpu.PrefetchScalarGridSpec(
            num_scalar_prefetch=1,
            grid=(per_owner,),
            in_specs=[
                pl.BlockSpec(
                    (1, parts, unit_rows, width), lambda i, s: (s[0] * per_owner + i, 0, 0, 0)
                ),
                pl.BlockSpec(
                    (1, parts, unit_rows, blocks), lambda i, s: (s[0] * per_owner + i, 0, 0, 0)
                ),
            ],
            out_specs=pl.BlockSpec((1, parts, unit_rows, width), lambda i, s: (i, 0, s[1], 0)),
        ),
        cost_estimate=pl.CostEstimate(
            flops=40 * per_owner * parts * unit_rows * width,
            bytes_accessed=4 * per_owner * parts * unit_rows * width,
            transcendentals=0,
        ),
    )(places, learner_rows, exponents)


def weights_kernel(rows_ref, exponent_ref, gate_ref, up_ref, down_ref):
    for part, ref in enumerate((gate_ref, up_ref, down_ref)):
        exponent = exponent_ref[0, part]
        value = to_grid(rows_ref[0, part], exponent)
        scale = jnp.exp2(exponent.astype(jnp.float32))
        ref[0] = (value * spread(scale, value.shape[1])).astype(ref.dtype)


def dequantize(learner_rows, exponents):
    experts, parts, unit_rows, width = learner_rows.shape
    blocks = exponents.shape[3]
    shape = jax.ShapeDtypeStruct((experts, unit_rows, width), learner_rows.dtype)
    spec = pl.BlockSpec((1, unit_rows, width), lambda i: (i, 0, 0))
    return pl.pallas_call(
        weights_kernel,
        out_shape=(shape,) * parts,
        grid=(experts,),
        in_specs=[
            pl.BlockSpec((1, parts, unit_rows, width), lambda i: (i, 0, 0, 0)),
            pl.BlockSpec((1, parts, unit_rows, blocks), lambda i: (i, 0, 0, 0)),
        ],
        out_specs=(spec,) * parts,
        cost_estimate=pl.CostEstimate(
            flops=50 * learner_rows.size,
            bytes_accessed=4 * learner_rows.size,
            transcendentals=0,
        ),
    )(learner_rows, exponents)


def swap(value, axis, bit):
    return lax.ppermute(value, axis, [(i, i ^ bit) for i in range(lax.axis_size(axis))])


def body(tokens, learner_rows, exponents, expert_ids, route_probs):
    experts, parts, unit_rows, width = learner_rows.shape
    owners = lax.axis_size("expert")
    groups = lax.axis_size("fsdp")
    per_owner = experts // owners
    tok_rows, model = tokens.shape
    me = lax.axis_index("expert")

    bits = [1 << b for b in reversed(range(owners.bit_length() - 1))]
    half = bits[0]

    order = [half + d for d in range(half)] + list(range(1, half))
    arrived = {}
    for d in order:
        sent = encode(learner_rows, exponents, me ^ d, jnp.int32(0), unit_rows)
        arrived[d] = swap(sent, "expert", d)
    elements = encode(learner_rows, exponents, me, me, owners * unit_rows)
    for d in order:
        elements = lax.dynamic_update_slice(
            elements, arrived[d], (0, 0, (me ^ d) * unit_rows, 0)
        )

    held = tokens[None]
    z_bits = bits[: (len(bits) + 1) // 2]
    for bit in z_bits:
        held = jnp.concatenate([held, swap(held, "expert", bit)], axis=0)
    slots = held.shape[0]
    held = held.reshape(slots * tok_rows, groups, width).transpose(1, 0, 2)
    held = lax.all_to_all(held, "fsdp", split_axis=0, concat_axis=0, tiled=True)
    for bit in bits[len(z_bits) :]:
        held = jnp.concatenate([held, swap(held, "expert", bit)], axis=1)
    rows = held.reshape(-1, width)

    gate_w, up_w, down_w = dequantize(learner_rows, exponents)
    nt = (((1,), (1,)), ((), ()))
    partial = jnp.stack(
        [
            lax.dot_general(
                rows, w.reshape(-1, width), nt, preferred_element_type=jnp.float32
            ).astype(jnp.bfloat16)
            for w in (gate_w, up_w)
        ],
        axis=1,
    )
    partial = partial.reshape(groups, -1, 2 * experts * unit_rows)
    summed = lax.psum_scatter(partial, "fsdp", scatter_dimension=0, tiled=False)
    summed = summed.astype(jnp.float32).reshape(-1, 2, experts * unit_rows)
    hidden = jax.nn.silu(summed[:, 0]) * summed[:, 1]

    share = route_probs / jnp.sum(route_probs, axis=1, keepdims=True)
    named = expert_ids[:, :, None] == jnp.arange(experts, dtype=jnp.int32)[None, None, :]
    table = jnp.sum(jnp.where(named, share[:, :, None], 0.0), axis=1)
    tables = lax.all_gather(table, "expert", axis=0, tiled=False)
    slot_of = [0]
    for bit in bits:
        slot_of = slot_of + [s | bit for s in slot_of]
    table = jnp.concatenate(
        [lax.dynamic_index_in_dim(tables, me ^ s, 0, keepdims=False) for s in slot_of], axis=0
    )
    shared = hidden.reshape(-1, experts, unit_rows) * table[:, :, None]
    shared = shared.astype(jnp.bfloat16).reshape(-1, experts * unit_rows)
    shared = lax.all_gather(shared, "fsdp", axis=0, tiled=True)
    out = jnp.dot(shared, down_w.reshape(-1, width), preferred_element_type=jnp.float32)

    out = out.reshape(groups, owners, tok_rows, width)
    for bit in reversed(bits):
        slots = out.shape[1] // 2
        out = out[:, :slots] + swap(out[:, slots:].astype(jnp.bfloat16), "expert", bit)
    mixed = lax.all_to_all(
        out[:, 0].astype(jnp.bfloat16), "fsdp", split_axis=0, concat_axis=0, tiled=True
    )
    mixed = mixed.transpose(1, 0, 2).reshape(tok_rows, model)
    return elements, mixed


def solution(mesh):
    return jax.shard_map(
        body,
        mesh=mesh,
        in_specs=(
            P(("fsdp", "expert"), None),
            P(None, None, "expert", "fsdp"),
            P(None, None, "expert", "fsdp"),
            P(("fsdp", "expert"), None),
            P(("fsdp", "expert"), None),
        ),
        out_specs=(P("expert", None, None, "fsdp"), P(("fsdp", "expert"), None)),
        check_vma=False,
    )
```

time: 609 us -> 379 us (0.62)
  local copies, waits for them, and re-layouts: 168 us -> 31.2 us
  waiting for transfers between devices: 265 us -> 199 us
  Pallas kernels: 0 us -> 46.6 us
  blocking collectives: 81.2 us -> 40.3 us
  other arithmetic: 43.1 us -> 8.42 us
    all_to_all x4 -> x1, waiting for transfers between devices: 207 us -> 2.16 us  [body(): lax.all_to_all(out[:, 0].astype(jnp.bfloat16), 'fsdp', split_axis=0, conc...]
    ppermute x0 -> x13, waiting for transfers between devices: none -> 189 us  [swap(): lax.ppermute(value, axis, [(i, i ^ bit) for i in range(lax.axis_size(axis...]
    all_to_all x2 -> x1, blocking collectives: 81.2 us -> 11.4 us  [body(): held = lax.all_to_all(held, 'fsdp', split_axis=0, concat_axis=0, tiled=True)]
    all_to_all x6 -> x0, local copies, waits for them, and re-layouts: 53.4 us -> none  [the longest x1 37.7 us: body(): lax.all_to_all(packed_view, 'fsdp', split_axis=4, concat_axis=3, tiled=True)]
    reshape x3, local copies, waits for them, and re-layouts: 55.2 us -> 4.55 us  [the longest x1 3.5 us: body(): partial = partial.reshape(groups, -1, 2 * experts * unit_rows)]
    unnamed x16 -> x26, local copies, waits for them, and re-layouts: 53.9 us -> 4.69 us
    pallas_call x0 -> x9, Pallas kernels: none -> 46.6 us  [the longest x8 29.9 us: encode(): pl.pallas_call(encode_kernel, out_shape=jax.ShapeDtypeStruct((per_owner,...]
    unnamed x3 -> x2, waiting for transfers between devices: 38.1 us -> 0.03 us
  transfers between devices with their start and end apart: 6 -> 16, of which waited for: 4 -> 10; matrix products, arithmetic and copies ran while one was open for 22% -> 8% of each run, Pallas kernels for 0% -> 12%
where the time goes in v1:
time: 379 us; the launch traced here: 375 us
  waiting for transfers between devices  199 us (53%)
  Pallas kernels  46.6 us (12%)
  blocking collectives  40.3 us (11%)
  local copies, waits for them, and re-layouts  31.2 us (8%)
  starting transfers between devices  25.4 us (7%)
  between operations  14.3 us (4%)
  matrix products  9.44 us (2%)
  other arithmetic  8.42 us (2%)
    ppermute x13, waiting for transfers between devices, swap(): lax.ppermute(value, axis, [(i, i ^ bit) for i in range(lax.axis_size(axis...  189 us
    pallas_call x8, Pallas kernels, encode(): pl.pallas_call(encode_kernel, out_shape=jax.ShapeDtypeStruct((per_owner,...  29.9 us
    all_gather x1, blocking collectives, body(): tables = lax.all_gather(table, 'expert', axis=0, tiled=False)  28.9 us
    ppermute x13, starting transfers between devices, swap(): lax.ppermute(value, axis, [(i, i ^ bit) for i in range(lax.axis_size(axis...  22 us
    pallas_call x1, Pallas kernels, dequantize(): pl.pallas_call(weights_kernel, out_shape=(shape,) * parts, grid=(experts,...  16.7 us
    dynamic_update_slice x7, local copies, waits for them, and re-layouts, body(): lax.dynamic_update_slice(elements, arrived[d], (0, 0, (me ^ d) * unit_row...  14.4 us
    all_to_all x1, blocking collectives, body(): held = lax.all_to_all(held, 'fsdp', split_axis=0, concat_axis=0, tiled=True)  11.4 us
  transfers between devices with their start and end apart: 16, of which 10 were waited for; matrix products, arithmetic and copies ran while one was open for 8% of the time, Pallas kernels for 12%

profile of v1, /device:TPU:8, one launch (start us, length us, event | category | flops | bytes accessed | tf_op | source)
XLA Modules:
  0.0 374.6 jit_solution(16409114559843641088)
XLA Ops:
  7.2 2.7 collective-permute-start.7
  9.9 5.8 %collective-permute-done.7 = bf16[1,16,4096]{2,1,0:T(8,128)(2,1)S(1)} collective-permute-done((bf16[1,16,4096]{2,1,0:T(8,128)(2,1)}, bf16[1,16,4096]{2,1,0:T(8,128)(2,1)S(1)}, u32[]{:S(2)}, u32[]{:S(2)}) %collective-permute-start.7) | collective-permute-done | bytes 131104 | tf_op jit(solution)/shard_map/ppermute | solution.py:100
  15.6 0.9 pad_maximum_fusion.3
  16.6 1.3 collective-permute-start.8
  17.8 7.0 %collective-permute-done.8 = bf16[2,16,4096]{2,1,0:T(8,128)(2,1)S(1)} collective-permute-done((bf16[2,16,4096]{2,1,0:T(8,128)(2,1)S(1)}, bf16[2,16,4096]{2,1,0:T(8,128)(2,1)S(1)}, u32[]{:S(2)}, u32[]{:S(2)}) %collective-permute-start.8) | collective-permute-done | bytes 262176 | tf_op jit(solution)/shard_map/ppermute | solution.py:100
  24.9 1.0 pad_maximum_fusion.2
  25.8 0.4 reshape.43
  26.4 11.4 %all_to_all.10 = bf16[4,64,1024]{2,1,0:T(8,128)(2,1)S(1)} all-to-all(bf16[4,64,1024]{2,1,0:T(8,128)(2,1)S(1)} %copy.74), channel_id=1, replica_groups=mesh['fsdp'=4,'expert'=8] {'fsdp'}, dimensions={0} | all-to-all | bytes 1048576 | tf_op jit(solution)/shard_map/all_to_all | solution.py:131
  37.8 1.5 collective-permute-start.9
  39.3 2.1 copy.66.exponent_ref
  41.4 16.7 %shard_map.76 = (bf16[16,96,1024]{2,1,0:T(8,128)(2,1)}, bf16[16,96,1024]{2,1,0:T(8,128)(2,1)}, bf16[16,96,1024]{2,1,0:T(8,128)(2,1)}) custom-call(bf16[16,3,96,1024]{3,2,1,0:T(8,128)(2,1)} %rows_ref.17, s32[16,3,96,32]{3,2,1,0:T(8,128)} %copy.66.exponent_ref), custom_call_target="tpu_custom_call" | custom-call | flops 235929600 | bytes 18874368 | tf_op jit(solution)/shard_map/pallas_call | solution.py:82
  58.2 3.9 %fusion.1 = bf16[512,1,1536]{2,0,1:T(8,128)(2,1)S(1)} fusion(bf16[512,1024]{1,0:T(8,128)(2,1)S(1)} %bitcast.61, bf16[1536,1024]{1,0:T(8,128)(2,1)} %bitcast.79), kind=kOutput, calls=%fused_computation.4 | convolution fusion | flops 1611399168 | bytes 5767168 | tf_op jit(solution)/shard_map/dot_general | solution.py:140
  62.1 1.8 fusion
  64.3 3.2 copy.76
  67.5 3.5 reshape.47
  71.1 0.6 copy-done.5
  72.0 28.9 %all-gather = f32[128,16]{1,0:T(8,128)S(1)} all-gather(f32[16,16]{1,0:T(8,128)S(1)} %select_reduce_fusion), channel_id=2, replica_groups=mesh['fsdp'=4,'expert'=8] {'expert'}, dimensions={0}, use_global_device_ids=true | all-gather | bytes 9216 | tf_op jit(solution)/shard_map/all_gather | solution.py:155
  101.6 7.6 %reduce-scatter.2.cloned.1.call-done = bf16[1,128,3072]{2,1,0:T(8,128)(2,1)} async-done(((bf16[4,128,3072]{2,1,0:T(8,128)(2,1)}), bf16[1,128,3072]{2,1,0:T(8,128)(2,1)}) %reduce-scatter.2.cloned.1.call-update) | async-done | bytes 786448 | tf_op jit(solution)/shard_map/reduce_scatter | solution.py:148
  109.1 1.4 copy.77
  110.6 1.0 fusion.4
  111.6 0.6 pad_add_fusion.6.places
  112.2 3.7 shard_map.69
  115.9 2.4 collective-permute-start
  118.3 0.6 pad_add_fusion.4
  118.9 3.7 shard_map.70
  122.7 1.4 collective-permute-start.1
  124.1 3.7 shard_map.71
  127.8 1.5 collective-permute-start.2
  129.3 0.6 pad_add_fusion.2
  129.9 3.7 shard_map.72
  133.6 0.6 collective-permute-start.3
  134.2 3.7 shard_map.73
  137.9 1.5 collective-permute-start.4
  139.4 0.6 pad_add_fusion.7.places
  140.0 3.7 shard_map.68
  143.7 1.7 copy.81
  145.4 3.7 fusion.7
  149.1 1.3 copy-done.2
  150.5 0.9 slice.63
  151.3 93.7 %collective-permute-done = bf16[2,3,96,1024]{3,2,1,0:T(8,128)(2,1)} collective-permute-done((bf16[2,3,96,1024]{3,2,1,0:T(8,128)(2,1)}, bf16[2,3,96,1024]{3,2,1,0:T(8,128)(2,1)}, u32[]{:S(2)}, u32[]{:S(2)}) %collective-permute-start) | collective-permute-done | bytes 1179680 | tf_op jit(solution)/shard_map/ppermute | solution.py:100
  245.1 1.5 collective-permute-start.10
  246.5 0.6 pad_add_fusion
  247.2 3.7 shard_map.74
  250.9 3.9 %shard_map.75 = bf16[2,3,96,1024]{3,2,1,0:T(8,128)(2,1)} custom-call(s32[2]{0:T(128)} %get-tuple-element.16.places, bf16[16,3,96,1024]{3,2,1,0:T(8,128)(2,1)} %rows_ref.17, s32[16,3,96,32]{3,2,1,0:T(8,128)} %copy.66.exponent_ref), custom_call_target="tpu_custom_call" | custom-call | flops 23592960 | bytes 2359296 | tf_op jit(solution)/shard_map/pallas_call | solution.py:45
  254.8 15.6 %collective-permute-done.1 = bf16[2,3,96,1024]{3,2,1,0:T(8,128)(2,1)} collective-permute-done((bf16[2,3,96,1024]{3,2,1,0:T(8,128)(2,1)}, bf16[2,3,96,1024]{3,2,1,0:T(8,128)(2,1)}, u32[]{:S(2)}, u32[]{:S(2)}) %collective-permute-start.1) | collective-permute-done | bytes 1179680 | tf_op jit(solution)/shard_map/ppermute | solution.py:100
  270.4 3.4 collective-permute-start.5
  273.7 2.4 constant_dynamic-update-slice_fusion.6
  276.2 2.4 constant_dynamic-update-slice_fusion.5
  278.6 18.1 %collective-permute-done.2 = bf16[2,3,96,1024]{3,2,1,0:T(8,128)(2,1)} collective-permute-done((bf16[2,3,96,1024]{3,2,1,0:T(8,128)(2,1)}, bf16[2,3,96,1024]{3,2,1,0:T(8,128)(2,1)}, u32[]{:S(2)}, u32[]{:S(2)}) %collective-permute-start.2) | collective-permute-done | bytes 1179680 | tf_op jit(solution)/shard_map/ppermute | solution.py:100
  296.7 2.4 constant_dynamic-update-slice_fusion.4
  299.1 1.2 slice_add_fusion
  300.4 3.0 collective-permute-start.11
  303.4 41.1 %collective-permute-done.3 = bf16[2,3,96,1024]{3,2,1,0:T(8,128)(2,1)} collective-permute-done((bf16[2,3,96,1024]{3,2,1,0:T(8,128)(2,1)}, bf16[2,3,96,1024]{3,2,1,0:T(8,128)(2,1)}, u32[]{:S(2)}, u32[]{:S(2)}) %collective-permute-start.3) | collective-permute-done | bytes 1179680 | tf_op jit(solution)/shard_map/ppermute | solution.py:100
  344.4 2.4 constant_dynamic-update-slice_fusion.3
  346.8 1.1 constant_dynamic-update-slice_fusion.2
  347.9 3.7 collective-permute-done.11
  351.7 1.5 collective-permute-start.12
  353.2 1.1 constant_dynamic-update-slice_fusion.1
  354.3 4.2 %collective-permute-done.12 = bf16[4,1,16,1024]{3,2,1,0:T(8,128)(2,1)S(1)} collective-permute-done((bf16[4,1,16,1024]{3,2,1,0:T(8,128)(2,1)S(1)}, bf16[4,1,16,1024]{3,2,1,0:T(8,128)(2,1)S(1)}, u32[]{:S(2)}, u32[]{:S(2)}) %collective-permute-start.12) | collective-permute-done | bytes 131104 | tf_op jit(solution)/shard_map/ppermute | solution.py:100
  358.5 0.7 fusion.6
  359.2 3.3 all-to-all-start.1
  362.5 2.4 constant_dynamic-update-slice_fusion
  364.9 2.2 all-to-all-done.1
  367.1 0.7 copy.93
  (46 shorter events, 1.7 us)
Async XLA Ops:
  7.2 32.1 %copy-start.4 = (s32[16,3,96,32]{2,3,1,0:T(8,128)S(1)}, s32[16,3,96,32]{2,3,1,0:T(8,128)}, u32[]{:S(2)}) copy-start(s32[16,3,96,32]{2,3,1,0:T(8,128)} %param.7) | copy-start | bytes 1769476
  7.2 102.0 %reduce-scatter.2.cloned.1.call-start = ((), (), s32[]{:S(2)}) async-start(), calls=%async_computation.3 | async-start | bytes 3932160 | tf_op jit(solution)/shard_map/reduce_scatter | solution.py:148
  7.2 8.4 %collective-permute-start.7 = (bf16[1,16,4096]{2,1,0:T(8,128)(2,1)}, bf16[1,16,4096]{2,1,0:T(8,128)(2,1)S(1)}, u32[]{:S(2)}, u32[]{:S(2)}) collective-permute-start(bf16[1,16,4096]{2,1,0:T(8,128)(2,1)} %bitcast.64), channel_id=1, source_target_pairs={{0,4},{1,5},{2,6},{3,7},{4,0},{5,1},{6,2},{7,3},{8,12},{9,13},{10,... | collective-permute-start | bytes 393224 | tf_op jit(solution)/shard_map/ppermute | solution.py:100
  16.6 8.3 %collective-permute-start.8 = (bf16[2,16,4096]{2,1,0:T(8,128)(2,1)S(1)}, bf16[2,16,4096]{2,1,0:T(8,128)(2,1)S(1)}, u32[]{:S(2)}, u32[]{:S(2)}) collective-permute-start(bf16[2,16,4096]{2,1,0:T(8,128)(2,1)S(1)} %pad_maximum_fusion.3), channel_id=1, source_target_pairs={{0,2},{1,3},{2,0},{3,1},{4,6},{5,7},{6,4},{7,5},{8,10},{9,11},{10,... | collective-permute-start | bytes 786440 | tf_op jit(solution)/shard_map/ppermute | solution.py:100
  37.8 20.3 %collective-permute-start.9 = (bf16[4,64,1024]{2,1,0:T(8,128)(2,1)S(1)}, bf16[4,64,1024]{2,1,0:T(8,128)(2,1)S(1)}, u32[]{:S(2)}, u32[]{:S(2)}) collective-permute-start(bf16[4,64,1024]{2,1,0:T(8,128)(2,1)S(1)} %all_to_all.10), channel_id=1, source_target_pairs={{0,1},{1,0},{2,3},{3,2},{4,5},{5,4},{6,7},{7,6},{8,9},{9,8},{10,11... | collective-permute-start | bytes 1572872 | tf_op jit(solution)/shard_map/ppermute | solution.py:100
  58.2 3.9 %copy-start.7 = (bf16[16,96,1024]{2,1,0:T(8,128)(2,1)S(1)}, bf16[16,96,1024]{2,1,0:T(8,128)(2,1)}, u32[]{:S(2)}) copy-start(bf16[16,96,1024]{2,1,0:T(8,128)(2,1)} %get-tuple-element.5) | copy-start | bytes 9437188
  71.0 0.7 copy-start.5
  71.0 0.8 copy-start.6
  71.1 72.6 %all-gather.3.cloned.1.call-start = ((), (), s32[]{:S(2)}) async-start(), calls=%async_computation.4 | async-start | bytes 1966080 | tf_op jit(solution)/shard_map/all_gather | solution.py:164
  115.9 129.1 %collective-permute-start = (bf16[2,3,96,1024]{3,2,1,0:T(8,128)(2,1)}, bf16[2,3,96,1024]{3,2,1,0:T(8,128)(2,1)}, u32[]{:S(2)}, u32[]{:S(2)}) collective-permute-start(bf16[2,3,96,1024]{3,2,1,0:T(8,128)(2,1)} %shard_map.69), channel_id=1, source_target_pairs={{0,4},{1,5},{2,6},{3,7},{4,0},{5,1},{6,2},{7,3},{8,12},{9,13},{10,... | collective-permute-start | bytes 3538952 | tf_op jit(solution)/shard_map/ppermute | solution.py:100
  122.7 147.7 %collective-permute-start.1 = (bf16[2,3,96,1024]{3,2,1,0:T(8,128)(2,1)}, bf16[2,3,96,1024]{3,2,1,0:T(8,128)(2,1)}, u32[]{:S(2)}, u32[]{:S(2)}) collective-permute-start(bf16[2,3,96,1024]{3,2,1,0:T(8,128)(2,1)} %shard_map.70), channel_id=1, source_target_pairs={{0,5},{1,4},{2,7},{3,6},{4,1},{5,0},{6,3},{7,2},{8,13},{9,12},{10,... | collective-permute-start | bytes 3538952 | tf_op jit(solution)/shard_map/ppermute | solution.py:100
  127.8 168.8 %collective-permute-start.2 = (bf16[2,3,96,1024]{3,2,1,0:T(8,128)(2,1)}, bf16[2,3,96,1024]{3,2,1,0:T(8,128)(2,1)}, u32[]{:S(2)}, u32[]{:S(2)}) collective-permute-start(bf16[2,3,96,1024]{3,2,1,0:T(8,128)(2,1)} %shard_map.71), channel_id=1, source_target_pairs={{0,6},{1,7},{2,4},{3,5},{4,2},{5,3},{6,0},{7,1},{8,14},{9,15},{10,... | collective-permute-start | bytes 3538952 | tf_op jit(solution)/shard_map/ppermute | solution.py:100
  133.6 210.8 %collective-permute-start.3 = (bf16[2,3,96,1024]{3,2,1,0:T(8,128)(2,1)}, bf16[2,3,96,1024]{3,2,1,0:T(8,128)(2,1)}, u32[]{:S(2)}, u32[]{:S(2)}) collective-permute-start(bf16[2,3,96,1024]{3,2,1,0:T(8,128)(2,1)} %shard_map.72), channel_id=1, source_target_pairs={{0,7},{1,6},{2,5},{3,4},{4,3},{5,2},{6,1},{7,0},{8,15},{9,14},{10,... | collective-permute-start | bytes 3538952 | tf_op jit(solution)/shard_map/ppermute | solution.py:100
  137.9 208.9 %collective-permute-start.4 = (bf16[2,3,96,1024]{3,2,1,0:T(8,128)(2,1)}, bf16[2,3,96,1024]{3,2,1,0:T(8,128)(2,1)S(1)}, u32[]{:S(2)}, u32[]{:S(2)}) collective-permute-start(bf16[2,3,96,1024]{3,2,1,0:T(8,128)(2,1)} %shard_map.73), channel_id=1, source_target_pairs={{0,1},{1,0},{2,3},{3,2},{4,5},{5,4},{6,7},{7,6},{8,9},{9,8},{10,11... | collective-permute-start | bytes 3538952 | tf_op jit(solution)/shard_map/ppermute | solution.py:100
  149.1 1.3 copy-start.2
  245.1 54.0 %collective-permute-start.10 = (bf16[4,4,16,1024]{3,2,1,0:T(8,128)(2,1)}, bf16[4,4,16,1024]{3,2,1,0:T(8,128)(2,1)}, u32[]{:S(2)}, u32[]{:S(2)}) collective-permute-start(bf16[4,4,16,1024]{3,2,1,0:T(8,128)(2,1)} %slice.63), channel_id=1, source_target_pairs={{0,1},{1,0},{2,3},{3,2},{4,5},{5,4},{6,7},{7,6},{8,9},{9,8},{10,11... | collective-permute-start | bytes 1572872 | tf_op jit(solution)/shard_map/ppermute | solution.py:100
  250.9 19.5 %copy-start.1 = (bf16[2,3,96,1024]{3,2,1,0:T(8,128)(2,1)S(1)}, bf16[2,3,96,1024]{3,2,1,0:T(8,128)(2,1)}, u32[]{:S(2)}) copy-start(bf16[2,3,96,1024]{3,2,1,0:T(8,128)(2,1)} %shard_map.74) | copy-start | bytes 3538948
  254.8 41.9 %copy-start = (bf16[2,3,96,1024]{3,2,1,0:T(8,128)(2,1)S(1)}, bf16[2,3,96,1024]{3,2,1,0:T(8,128)(2,1)}, u32[]{:S(2)}) copy-start(bf16[2,3,96,1024]{3,2,1,0:T(8,128)(2,1)} %shard_map.75) | copy-start | bytes 3538948
  254.8 44.3 %copy-start.3 = (f32[4,8,16,1024]{3,2,1,0:T(8,128)S(1)}, f32[4,8,16,1024]{3,2,1,0:T(8,128)}, u32[]{:S(2)}) copy-start(f32[4,8,16,1024]{3,2,1,0:T(8,128)} %copy-done.2) | copy-start | bytes 6291460
  270.4 82.8 %collective-permute-start.5 = (bf16[2,3,96,1024]{3,2,1,0:T(8,128)(2,1)S(1)}, bf16[2,3,96,1024]{3,2,1,0:T(8,128)(2,1)S(1)}, u32[]{:S(2)}, u32[]{:S(2)}) collective-permute-start(bf16[2,3,96,1024]{3,2,1,0:T(8,128)(2,1)S(1)} %copy-done.1), channel_id=1, source_target_pairs={{0,2},{1,3},{2,0},{3,1},{4,6},{5,7},{6,4},{7,5},{8,10},{9,11},{10,... | collective-permute-start | bytes 3538952 | tf_op jit(solution)/shard_map/ppermute | solution.py:100
  296.7 65.8 %collective-permute-start.6 = (bf16[2,3,96,1024]{3,2,1,0:T(8,128)(2,1)S(1)}, bf16[2,3,96,1024]{3,2,1,0:T(8,128)(2,1)}, u32[]{:S(2)}, u32[]{:S(2)}) collective-permute-start(bf16[2,3,96,1024]{3,2,1,0:T(8,128)(2,1)S(1)} %copy-done), channel_id=1, source_target_pairs={{0,3},{1,2},{2,1},{3,0},{4,7},{5,6},{6,5},{7,4},{8,11},{9,10},{10,... | collective-permute-start | bytes 3538952 | tf_op jit(solution)/shard_map/ppermute | solution.py:100
  300.4 51.3 %collective-permute-start.11 = (bf16[4,2,16,1024]{3,2,1,0:T(8,128)(2,1)S(1)}, bf16[4,2,16,1024]{3,2,1,0:T(8,128)(2,1)S(1)}, u32[]{:S(2)}, u32[]{:S(2)}) collective-permute-start(bf16[4,2,16,1024]{3,2,1,0:T(8,128)(2,1)S(1)} %slice.64), channel_id=1, source_target_pairs={{0,2},{1,3},{2,0},{3,1},{4,6},{5,7},{6,4},{7,5},{8,10},{9,11},{10,... | collective-permute-start | bytes 786440 | tf_op jit(solution)/shard_map/ppermute | solution.py:100
  351.7 6.7 %collective-permute-start.12 = (bf16[4,1,16,1024]{3,2,1,0:T(8,128)(2,1)S(1)}, bf16[4,1,16,1024]{3,2,1,0:T(8,128)(2,1)S(1)}, u32[]{:S(2)}, u32[]{:S(2)}) collective-permute-start(bf16[4,1,16,1024]{3,2,1,0:T(8,128)(2,1)S(1)} %slice.65), channel_id=1, source_target_pairs={{0,4},{1,5},{2,6},{3,7},{4,0},{5,1},{6,2},{7,3},{8,12},{9,13},{10,... | collective-permute-start | bytes 393224 | tf_op jit(solution)/shard_map/ppermute | solution.py:100
  359.2 7.9 %all-to-all-start.1 = ((bf16[4,16,1024]{2,1,0:T(8,128)(2,1)}), bf16[4,16,1024]{2,1,0:T(8,128)(2,1)S(1)}, u32[]{:S(2)}, u32[]{:S(2)}) async-start(bf16[4,16,1024]{2,1,0:T(8,128)(2,1)} %fusion.6), calls=%async_computation.2 | async-start | bytes 262144 | tf_op jit(solution)/shard_map/all_to_all | solution.py:171
Sparse Core Ops, SparseCore 0:
  71.2 37.9 reduce-scatter.1
  111.7 19.8 all-gather.2

commit v2 on v1

v2 whole, which is shorter than its diff:
```python
import functools

import jax
import jax.numpy as jnp
from jax import lax
from jax.experimental import pallas as pl
from jax.experimental.pallas import tpu as pltpu
from jax.sharding import PartitionSpec as P

HALVES, ONES, TWOS = 1.5 * 2.0**22, 1.5 * 2.0**23, 1.5 * 2.0**24


def spread(values, width):
    blocks = values.shape[0]
    shape = (blocks, width)
    feature = lax.broadcasted_iota(jnp.int32, shape, 1)
    block = lax.broadcasted_iota(jnp.int32, shape, 0)
    size = width // blocks
    inside = (feature >= block * size) & (feature < (block + 1) * size)
    table = inside.astype(jnp.float32).astype(jnp.bfloat16)
    return lax.dot_general(
        values.astype(jnp.bfloat16),
        table,
        (((0,), (0,)), ((), ())),
        preferred_element_type=jnp.float32,
    )


def to_grid(rows, exponent):
    one = jnp.ones_like(exponent)
    inverse = lax.shift_left(one, -exponent).astype(jnp.float32)
    ratio = rows.astype(jnp.float32) * spread(inverse, rows.shape[1])
    ratio = jnp.clip(ratio, -6.0, 6.0)
    magnitude = jnp.abs(ratio)
    magic = jnp.where(magnitude < 2.0, HALVES, jnp.where(magnitude < 4.0, ONES, TWOS))
    return (ratio + magic) - magic


def encode_kernel(me, rows_ref, exponent_ref, out_ref):
    for part in range(rows_ref.shape[1]):
        value = to_grid(rows_ref[0, part], exponent_ref[0, part])
        out_ref[0, part] = value.astype(out_ref.dtype)


def encode(learner_rows, exponents, me, partner, first, count, out_rows, out_block):
    experts, parts, unit_rows, width = learner_rows.shape
    blocks = exponents.shape[2]
    per_owner = experts // lax.axis_size("expert")

    def place(i, s):
        return ((s[0] ^ partner) * per_owner + first + i, 0, 0, 0)

    return pl.pallas_call(
        encode_kernel,
        out_shape=jax.ShapeDtypeStruct((count, parts, out_rows, width), learner_rows.dtype),
        grid_spec=pltpu.PrefetchScalarGridSpec(
            num_scalar_prefetch=1,
            grid=(count,),
            in_specs=[
                pl.BlockSpec((1, parts, unit_rows, width), place),
                pl.BlockSpec((1, parts, blocks, unit_rows), place),
            ],
            out_specs=pl.BlockSpec(
                (1, parts, unit_rows, width), lambda i, s: (i, 0, out_block(s[0]), 0)
            ),
        ),
        cost_estimate=pl.CostEstimate(
            flops=20 * count * parts * unit_rows * width,
            bytes_accessed=4 * count * parts * unit_rows * width,
            transcendentals=0,
        ),
    )(me, learner_rows, exponents)


def weights_kernel(first, rows_ref, exponent_ref, out_ref):
    for part in range(out_ref.shape[0]):
        exponent = exponent_ref[0, part]
        value = to_grid(rows_ref[0, part], exponent)
        scale = jnp.exp2(exponent.astype(jnp.float32))
        out_ref[part, 0] = (value * spread(scale, value.shape[1])).astype(out_ref.dtype)


def dequantize(learner_rows, exponents, first, count):
    experts, parts, unit_rows, width = learner_rows.shape
    blocks = exponents.shape[2]
    size = count * experts * unit_rows * width
    return pl.pallas_call(
        functools.partial(weights_kernel, first),
        out_shape=jax.ShapeDtypeStruct((count, experts, unit_rows, width), learner_rows.dtype),
        grid=(experts,),
        in_specs=[
            pl.BlockSpec((1, count, unit_rows, width), lambda i: (i, first // count, 0, 0)),
            pl.BlockSpec((1, count, blocks, unit_rows), lambda i: (i, first // count, 0, 0)),
        ],
        out_specs=pl.BlockSpec((count, 1, unit_rows, width), lambda i: (0, i, 0, 0)),
        cost_estimate=pl.CostEstimate(
            flops=25 * size, bytes_accessed=4 * size, transcendentals=0
        ),
    )(learner_rows, exponents)


def place(elements, block, me, partner):
    row = (me[0] ^ partner) * block.shape[2]
    return lax.dynamic_update_slice(elements, block, (0, 0, row, 0))


def swap(value, axis, bit):
    return lax.ppermute(value, axis, [(i, i ^ bit) for i in range(lax.axis_size(axis))])


def together(*values):
    return lax.optimization_barrier(values)


def masks(axis):
    return [1 << b for b in reversed(range(lax.axis_size(axis).bit_length() - 1))]


def low_bits(axis):
    bits = masks(axis)
    return bits[len(bits) - len(bits) // 2 :]


def share_table(expert_ids, route_probs, experts):
    share = route_probs / jnp.sum(route_probs, axis=1, keepdims=True)
    named = expert_ids[:, :, None] == jnp.arange(experts, dtype=jnp.int32)[None, None, :]
    table = jnp.sum(jnp.where(named, share[:, :, None], 0.0), axis=1)
    pieces = []
    for _ in range(3):
        piece = lax.reduce_precision(table, 8, 7)
        table = table - piece
        pieces.append(piece.astype(jnp.bfloat16))
    pieces = jnp.concatenate(pieces, axis=1)
    return jnp.pad(pieces, ((0, 0), (0, -pieces.shape[1] % 128)))


def gather(value, axis, bits):
    for bit in bits:
        value = jnp.concatenate([value, swap(value, axis, bit)], axis=0)
    return value


def halve(value, axis, bits):
    for bit in reversed(bits):
        kept = value.shape[0] // 2
        got = swap(value[kept:].astype(jnp.bfloat16), axis, bit)
        value = value[:kept].astype(jnp.float32) + got.astype(jnp.float32)
    return value


def columns(value, bits):
    group = lax.axis_index("fsdp")
    for bit in bits:
        kept = value.shape[1] // 2
        low, high = value[:, :kept], value[:, kept:]
        upper = (group & bit) != 0
        mine, other = jnp.where(upper, high, low), jnp.where(upper, low, high)
        value = jnp.concatenate([mine, swap(other, "fsdp", bit)], axis=0)
    return value


def uncolumns(value, bits):
    group = lax.axis_index("fsdp")
    for bit in reversed(bits):
        kept = value.shape[0] // 2
        mine, other = value[:kept], swap(value[kept:], "fsdp", bit)
        upper = (group & bit) != 0
        value = jnp.concatenate(
            [jnp.where(upper, other, mine), jnp.where(upper, mine, other)], axis=1
        )
    return value


def layer(held, learner_rows, exponents, encode_more):
    experts, parts, unit_rows, width = learner_rows.shape
    groups = lax.axis_size("fsdp")
    x_bits, group_bits = low_bits("expert"), masks("fsdp")
    units = experts * unit_rows
    rows = held.shape[0]
    slots = rows << len(x_bits)

    table = held[:, groups * width :]
    held = columns(held[:, : groups * width], group_bits).reshape(groups, rows, width)
    pair = dequantize(learner_rows, exponents, 0, 2)
    for bit in x_bits:
        held = jnp.concatenate([held, swap(held, "expert", bit)], axis=1)
    held, pair, table = together(held, pair, table)
    table = gather(table, "expert", x_bits)
    partial = lax.dot_general(
        held.reshape(groups * slots, width),
        pair.reshape(-1, width),
        (((1,), (1,)), ((), ())),
        preferred_element_type=jnp.float32,
    ).astype(jnp.bfloat16)
    partial, table = together(partial, table)
    table = table[:, : 3 * experts].astype(jnp.float32).reshape(-1, 3, experts).sum(axis=1)

    down = dequantize(learner_rows, exponents, 2, 1)
    partial = halve(partial, "fsdp", group_bits)
    partial, down = together(partial, down)
    hidden = jax.nn.silu(partial[:, :units]) * partial[:, units:]
    shared = hidden.reshape(-1, experts, unit_rows) * table[:, :, None]
    shared = shared.astype(jnp.bfloat16).reshape(-1, units)
    middle = len(encode_more) // 2
    more = [make() for make in encode_more]
    shared, *first = together(gather(shared, "fsdp", group_bits), *more[:middle])
    out = jnp.dot(shared, down.reshape(-1, width), preferred_element_type=jnp.float32)
    out = out.reshape(groups, slots, width)
    for bit in reversed(x_bits):
        kept = out.shape[1] // 2
        out = out[:, :kept] + swap(out[:, kept:].astype(jnp.bfloat16), "expert", bit)
    out, *second = together(out, *more[middle:])
    return out, *first, *second


def body(tokens, learner_rows, exponents, expert_ids, route_probs):
    experts, parts, unit_rows, width = learner_rows.shape
    owners = lax.axis_size("expert")
    groups = lax.axis_size("fsdp")
    per_owner = experts // owners
    tok_rows = tokens.shape[0]
    bits, group_bits = masks("expert"), masks("fsdp")
    z_bits = bits[: len(bits) - len(low_bits("expert"))]
    me = lax.axis_index("expert").astype(jnp.int32).reshape(1)
    exponents = exponents.swapaxes(2, 3)

    half = bits[0]
    far, near = list(range(half, owners)), list(range(1, half))
    first, second, third, fourth = (far[i * half // 4 : (i + 1) * half // 4] for i in range(4))
    begin, rest = near[: (half - 1) // 3], near[(half - 1) // 3 :]
    late = rest + fourth

    def block(partner, learner_rows, exponents):
        return encode(
            learner_rows, exponents, me, partner, 0, per_owner, unit_rows, lambda m: 0
        )

    sent, arrived = {}, {}
    for d in first + second + third + begin:
        sent[d] = block(d, learner_rows, exponents)

    def after(value, keys, table):
        value, *blocks = together(value, *[table[key] for key in keys])
        table.update(zip(keys, blocks))
        return value

    def send(keys):
        for key in keys:
            arrived[key] = swap(sent[key], "expert", key)

    table = gather(share_table(expert_ids, route_probs, experts), "expert", z_bits[:1])
    held = gather(tokens, "expert", z_bits[:1])
    held = jnp.concatenate([held, table], axis=1)
    held = after(held, first + second, sent)
    send(first + second)
    held = gather(held, "expert", z_bits[1:])
    held = after(held, third + begin, sent)
    send(third + begin)

    def serve(held, learner_rows, exponents):
        makes = [functools.partial(block, d, learner_rows, exponents) for d in late]
        return layer(held, learner_rows, exponents, makes)

    def idle(held, learner_rows, exponents):
        out = jnp.zeros((groups, held.shape[0], width), jnp.float32)
        return out, *[block(d, learner_rows, exponents) for d in late]

    out, *blocks = lax.cond(
        expert_ids[0, 0] >= 0, serve, idle, held, learner_rows, exponents
    )
    sent.update(zip(late, blocks))
    out = after(out, first, arrived)

    out = out.reshape(groups, -1, tok_rows, width).swapaxes(0, 1)
    for bit, there in zip(reversed(z_bits), (second + begin, third, [], [])):
        out = halve(out, "expert", [bit])
        out = after(out, there, arrived)
    send(late)
    mixed = uncolumns(out.astype(jnp.bfloat16).reshape(groups * tok_rows, width), group_bits)

    elements = encode(
        learner_rows, exponents, me, 0, 0, per_owner, owners * unit_rows, lambda m: m
    )
    for key in first + second + begin + third + rest + fourth:
        elements = place(elements, arrived[key], me, key)
    return elements, mixed


def solution(mesh):
    return jax.shard_map(
        body,
        mesh=mesh,
        in_specs=(
            P(("fsdp", "expert"), None),
            P(None, None, "expert", "fsdp"),
            P(None, None, "expert", "fsdp"),
            P(("fsdp", "expert"), None),
            P(("fsdp", "expert"), None),
        ),
        out_specs=(P("expert", None, None, "fsdp"), P(("fsdp", "expert"), None)),
        check_vma=False,
    )
```

time: 379 us -> 265 us (0.70)
  waiting for transfers between devices: 199 us -> 140 us
  blocking collectives: 40.3 us -> 0 us
  between operations: 14.3 us -> 1.44 us
  local copies, waits for them, and re-layouts: 31.2 us -> 23 us
  Pallas kernels: 46.6 us -> 52.1 us
    ppermute x13 -> x23, waiting for transfers between devices: 189 us -> 140 us  [swap(): lax.ppermute(value, axis, [(i, i ^ bit) for i in range(lax.axis_size(axis...]
    all_gather x1 -> x0, blocking collectives: 28.9 us -> none  [body(): tables = lax.all_gather(table, 'expert', axis=0, tiled=False)]
    all_to_all x1 -> x0, blocking collectives: 11.4 us -> none  [body(): held = lax.all_to_all(held, 'fsdp', split_axis=0, concat_axis=0, tiled=True)]
    reduce_scatter x1 -> x0, waiting for transfers between devices: 7.56 us -> none  [body(): summed = lax.psum_scatter(partial, 'fsdp', scatter_dimension=0, tiled=False)]
    ppermute x13 -> x23, starting transfers between devices: 22 us -> 28.4 us  [swap(): lax.ppermute(value, axis, [(i, i ^ bit) for i in range(lax.axis_size(axis...]
    pallas_call x9 -> x10, Pallas kernels: 46.6 us -> 52.1 us  [the longest x2 27 us: dequantize(): pl.pallas_call(functools.partial(weights_kernel, first), out_shape=jax.Sh...]
    reshape x3 -> x1, local copies, waits for them, and re-layouts: 4.55 us -> 0.1 us  [body(): out = out.reshape(groups, -1, tok_rows, width).swapaxes(0, 1)]
    slice x3 -> x9, local copies, waits for them, and re-layouts: 0.92 us -> 5.13 us  [the longest x4 1.87 us: halve(): got = swap(value[kept:].astype(jnp.bfloat16), axis, bit)]
  transfers between devices with their start and end apart: 16 -> 23, of which waited for: 10 -> 10; matrix products, arithmetic and copies ran while one was open for 8% -> 14% of each run, Pallas kernels for 12% -> 20%
where the time goes in v2:
time: 265 us; the launch traced here: 263 us
  waiting for transfers between devices  140 us (53%)
  Pallas kernels  52.1 us (20%)
  starting transfers between devices  28.4 us (11%)
  local copies, waits for them, and re-layouts  23 us (9%)
  matrix products  9.57 us (4%)
  other arithmetic  8.17 us (3%)
    ppermute x23, waiting for transfers between devices, swap(): lax.ppermute(value, axis, [(i, i ^ bit) for i in range(lax.axis_size(axis...  140 us
    ppermute x23, starting transfers between devices, swap(): lax.ppermute(value, axis, [(i, i ^ bit) for i in range(lax.axis_size(axis...  28.4 us
    pallas_call x2, Pallas kernels, dequantize(): pl.pallas_call(functools.partial(weights_kernel, first), out_shape=jax.Sh...  27 us
    pallas_call x8, Pallas kernels, encode(): pl.pallas_call(encode_kernel, out_shape=jax.ShapeDtypeStruct((count, part...  25.1 us
    dynamic_update_slice x7, local copies, waits for them, and re-layouts, place(): return lax.dynamic_update_slice(elements, block, (0, 0, row, 0))  11.8 us
    dot_general x1, matrix products, layer(): lax.dot_general(held.reshape(groups * slots, width), pair.reshape(-1, wid...  6.46 us
  transfers between devices with their start and end apart: 23, of which 10 were waited for; matrix products, arithmetic and copies ran while one was open for 14% of the time, Pallas kernels for 20%

profile of v2, /device:TPU:8, one launch (start us, length us, event | category | flops | bytes accessed | tf_op | source)
XLA Modules:
  0.0 263.4 jit_solution(15588809024263946841)
XLA Ops:
  0.6 2.7 %collective-permute-start.9 = (bf16[16,4096]{1,0:T(8,128)(2,1)}, bf16[16,4096]{1,0:T(8,128)(2,1)S(1)}, u32[]{:S(2)}, u32[]{:S(2)}) collective-permute-start(bf16[16,4096]{1,0:T(8,128)(2,1)} %param.7), channel_id=1, source_target_pairs={{0,4},{1,5},{2,6},{3,7},{4,0},{5,1},{6,2},{7,3},{8,12},{9,13},{10,... | collective-permute-start | bytes 393224 | tf_op jit(solution)/shard_map/ppermute | solution.py:108
  3.3 0.7 reduce_sum.27
  4.0 0.7 broadcast_divide_fusion
  4.8 0.8 copy.23
  5.7 0.3 collective-permute-start.10
  6.1 3.2 %shard_map.69 = bf16[2,3,96,1024]{3,2,1,0:T(8,128)(2,1)} custom-call(s32[1]{0:T(128)} %bitcast.8.me, bf16[16,3,96,1024]{3,2,1,0:T(8,128)(2,1)} %rows_ref.9, s32[16,3,32,96]{3,2,1,0:T(8,128)} %bitcast.25), custom_call_target="tpu_custom_call" | custom-call | flops 11796480 | bytes 2359296 | tf_op jit(solution)/shard_map/pallas_call | solution.py:53
  9.2 3.1 %shard_map.70 = bf16[2,3,96,1024]{3,2,1,0:T(8,128)(2,1)} custom-call(s32[1]{0:T(128)} %bitcast.8.me, bf16[16,3,96,1024]{3,2,1,0:T(8,128)(2,1)} %rows_ref.9, s32[16,3,32,96]{3,2,1,0:T(8,128)S(1)} %bitcast.26), custom_call_target="tpu_custom_call" | custom-call | flops 11796480 | bytes 2359296 | tf_op jit(solution)/shard_map/pallas_call | solution.py:53
  12.7 3.1 %shard_map.71 = bf16[2,3,96,1024]{3,2,1,0:T(8,128)(2,1)} custom-call(s32[1]{0:T(128)} %bitcast.8.me, bf16[16,3,96,1024]{3,2,1,0:T(8,128)(2,1)} %rows_ref.9, s32[16,3,32,96]{3,2,1,0:T(8,128)S(1)} %bitcast.27), custom_call_target="tpu_custom_call" | custom-call | flops 11796480 | bytes 2359296 | tf_op jit(solution)/shard_map/pallas_call | solution.py:53
  15.8 3.1 %shard_map.72 = bf16[2,3,96,1024]{3,2,1,0:T(8,128)(2,1)} custom-call(s32[1]{0:T(128)} %bitcast.8.me, bf16[16,3,96,1024]{3,2,1,0:T(8,128)(2,1)} %rows_ref.9, s32[16,3,32,96]{3,2,1,0:T(8,128)S(1)} %bitcast.28), custom_call_target="tpu_custom_call" | custom-call | flops 11796480 | bytes 2359296 | tf_op jit(solution)/shard_map/pallas_call | solution.py:53
  18.9 2.9 %collective-permute-start.12 = (bf16[2,3,96,1024]{3,2,1,0:T(8,128)(2,1)}, bf16[2,3,96,1024]{3,2,1,0:T(8,128)(2,1)S(1)}, u32[]{:S(2)}, u32[]{:S(2)}) collective-permute-start(bf16[2,3,96,1024]{3,2,1,0:T(8,128)(2,1)} %shard_map.69), channel_id=1, source_target_pairs={{0,4},{1,5},{2,6},{3,7},{4,0},{5,1},{6,2},{7,3},{8,12},{9,13},{10,... | collective-permute-start | bytes 3538952 | tf_op jit(solution)/shard_map/ppermute | solution.py:108
  21.8 1.3 collective-permute-start.14
  23.4 3.0 %collective-permute-start.17 = (bf16[2,3,96,1024]{3,2,1,0:T(8,128)(2,1)}, bf16[2,3,96,1024]{3,2,1,0:T(8,128)(2,1)}, u32[]{:S(2)}, u32[]{:S(2)}) collective-permute-start(bf16[2,3,96,1024]{3,2,1,0:T(8,128)(2,1)} %shard_map.71), channel_id=1, source_target_pairs={{0,6},{1,7},{2,4},{3,5},{4,2},{5,3},{6,0},{7,1},{8,14},{9,15},{10,... | collective-permute-start | bytes 3538952 | tf_op jit(solution)/shard_map/ppermute | solution.py:108
  26.4 1.2 slice.82
  28.3 129.8 %conditional.1 = (f32[4,64,1024]{2,1,0:T(8,128)S(1)}, bf16[2,3,96,1024]{3,2,1,0:T(8,128)(2,1)}, bf16[2,3,96,1024]{3,2,1,0:T(8,128)(2,1)}, bf16[2,3,96,1024]{3,2,1,0:T(8,128)(2,1)}) conditional(s32[]{:T(128)} %bitcast.10, (s32[1]{0:T(128)}, bf16[16,3,96,1024]{3,2,1,0:T(8,128)(2,1)}, s32[16,3,32,96]{3,2,1,0:T(8,128)S(1)}) %tuple.43, ...), branch_computations={%region_2.3_spmd, %region_3.5_spmd} | conditional | flops 5003421696 | bytes 123851280 | solution.py:268
  28.5 1.6 collective-permute-start
  30.1 4.9 %collective-permute-done = bf16[64,2048]{1,0:T(8,128)(2,1)S(1)} collective-permute-done((bf16[64,2048]{1,0:T(8,128)(2,1)S(1)}, bf16[64,2048]{1,0:T(8,128)(2,1)S(1)}, u32[]{:S(2)}, u32[]{:S(2)}) %collective-permute-start) | collective-permute-done | bytes 262176 | tf_op jit(solution)/shard_map/cond/branch_1_fun/ppermute | solution.py:108
  35.2 1.5 collective-permute-done.1
  36.7 1.5 collective-permute-start.2
  38.3 1.4 copy.21
  39.6 0.8 slice.95
  40.4 14.7 %branch_1_fun.5 = bf16[2,16,96,1024]{3,2,1,0:T(8,128)(2,1)} custom-call(bf16[16,3,96,1024]{3,2,1,0:T(8,128)(2,1)} %get-tuple-element.18.rows_ref, s32[16,3,32,96]{3,2,1,0:T(8,128)S(1)} %get-tuple-element.19.exponent_ref), custom_call_target="tpu_custom_call" | custom-call | flops 78643200 | bytes 12582912 | tf_op jit(solution)/shard_map/cond/branch_1_fun/pallas_call | solution.py:87
  55.1 31.1 %collective-permute-done.2 = bf16[4,64,1024]{2,1,0:T(8,128)(2,1)S(1)} collective-permute-done((bf16[4,64,1024]{2,1,0:T(8,128)(2,1)S(1)}, bf16[4,64,1024]{2,1,0:T(8,128)(2,1)S(1)}, u32[]{:S(2)}, u32[]{:S(2)}) %collective-permute-start.2) | collective-permute-done | bytes 524320 | tf_op jit(solution)/shard_map/cond/branch_1_fun/ppermute | solution.py:108
  86.3 0.6 collective-permute-start.3
  86.9 6.5 %convolution_convert_fusion = bf16[512,3072]{1,0:T(8,128)(2,1)S(1)} fusion(bf16[512,1024]{1,0:T(8,128)(2,1)S(1)} %bitcast.41, bf16[3072,1024]{1,0:T(8,128)(2,1)} %bitcast.32), kind=kOutput, calls=%fused_computation | convolution fusion | flops 3222798336 | bytes 10485760 | tf_op jit(solution)/shard_map/cond/branch_1_fun/dot_general | solution.py:189
  93.6 3.4 %collective-permute-done.4 = bf16[256,3072]{1,0:T(8,128)(2,1)S(1)} collective-permute-done((bf16[256,3072]{1,0:T(8,128)(2,1)S(1)}, bf16[256,3072]{1,0:T(8,128)(2,1)S(1)}, u32[]{:S(2)}, u32[]{:S(2)}) %collective-permute-start.4) | collective-permute-done | bytes 1572896 | tf_op jit(solution)/shard_map/cond/branch_1_fun/ppermute | solution.py:108
  97.0 0.5 convert_add_fusion
  97.5 1.7 copy-done.1
  99.2 1.0 slice.142
  100.2 1.5 collective-permute-start.5
  101.7 12.3 %branch_1_fun.6 = bf16[1,16,96,1024]{3,2,1,0:T(8,128)(2,1)} custom-call(bf16[16,3,96,1024]{3,2,1,0:T(8,128)(2,1)} %get-tuple-element.18.rows_ref, s32[16,3,32,96]{3,2,1,0:T(8,128)S(1)} %get-tuple-element.19.exponent_ref), custom_call_target="tpu_custom_call" | custom-call | flops 39321600 | bytes 6291456 | tf_op jit(solution)/shard_map/cond/branch_1_fun/pallas_call | solution.py:87
  114.3 5.8 %collective-permute-done.5 = bf16[128,3072]{1,0:T(8,128)(2,1)} collective-permute-done((bf16[128,3072]{1,0:T(8,128)(2,1)}, bf16[128,3072]{1,0:T(8,128)(2,1)}, u32[]{:S(2)}, u32[]{:S(2)}) %collective-permute-start.5) | collective-permute-done | bytes 786464 | tf_op jit(solution)/shard_map/cond/branch_1_fun/ppermute | solution.py:108
  120.1 1.8 slice_add_fusion
  122.1 1.6 collective-permute-start.6
  123.7 8.8 %collective-permute-done.6 = bf16[128,1536]{1,0:T(8,128)(2,1)S(1)} collective-permute-done((bf16[128,1536]{1,0:T(8,128)(2,1)S(1)}, bf16[128,1536]{1,0:T(8,128)(2,1)S(1)}, u32[]{:S(2)}, u32[]{:S(2)}) %collective-permute-start.6) | collective-permute-done | bytes 393248 | tf_op jit(solution)/shard_map/cond/branch_1_fun/ppermute | solution.py:108
  132.7 3.1 %branch_1_fun.7 = bf16[2,3,96,1024]{3,2,1,0:T(8,128)(2,1)} custom-call(s32[1]{0:T(128)} %get-tuple-element.26.me, bf16[16,3,96,1024]{3,2,1,0:T(8,128)(2,1)} %get-tuple-element.18.rows_ref, s32[16,3,32,96]{3,2,1,0:T(8,128)S(1)} %get-tuple-element.19.exponent_ref), custom_call_target="tpu_custom_call" | custom-call | flops 11796480 | bytes 2359296 | tf_op jit(solution)/shard_map/cond/branch_1_fun/pallas_call | solution.py:53
  135.8 1.4 pad_maximum_fusion
  137.2 0.7 copy-done.2
  137.9 3.1 %fusion.10 = f32[4,128,1024]{2,1,0:T(8,128)} fusion(bf16[4,128,1536]{2,1,0:T(8,128)(2,1)S(1)} %bitcast.40, bf16[1536,1024,1]{1,0,2:T(8,128)(2,1)S(1)} %bitcast.37), kind=kOutput, calls=%fused_computation.60 | convolution fusion | flops 1610612736 | bytes 6815744 | tf_op jit(solution)/shard_map/cond/branch_1_fun/dot_general | solution.py:207
  141.0 1.3 slice.143
  142.3 1.6 collective-permute-start.8
  143.9 3.1 %branch_1_fun.8 = bf16[2,3,96,1024]{3,2,1,0:T(8,128)(2,1)} custom-call(s32[1]{0:T(128)} %get-tuple-element.26.me, bf16[16,3,96,1024]{3,2,1,0:T(8,128)(2,1)} %get-tuple-element.18.rows_ref, s32[16,3,32,96]{3,2,1,0:T(8,128)S(1)} %get-tuple-element.19.exponent_ref), custom_call_target="tpu_custom_call" | custom-call | flops 11796480 | bytes 2359296 | tf_op jit(solution)/shard_map/cond/branch_1_fun/pallas_call | solution.py:53
  147.0 3.1 %branch_1_fun.9 = bf16[2,3,96,1024]{3,2,1,0:T(8,128)(2,1)} custom-call(s32[1]{0:T(128)} %get-tuple-element.26.me, bf16[16,3,96,1024]{3,2,1,0:T(8,128)(2,1)} %get-tuple-element.18.rows_ref, s32[16,3,32,96]{3,2,1,0:T(8,128)S(1)} %get-tuple-element.19.exponent_ref), custom_call_target="tpu_custom_call" | custom-call | flops 11796480 | bytes 2359296 | tf_op jit(solution)/shard_map/cond/branch_1_fun/pallas_call | solution.py:53
  150.1 6.6 %collective-permute-done.8 = bf16[4,64,1024]{2,1,0:T(8,128)(2,1)S(1)} collective-permute-done((bf16[4,64,1024]{2,1,0:T(8,128)(2,1)S(1)}, bf16[4,64,1024]{2,1,0:T(8,128)(2,1)S(1)}, u32[]{:S(2)}, u32[]{:S(2)}) %collective-permute-start.8) | collective-permute-done | bytes 524320 | tf_op jit(solution)/shard_map/cond/branch_1_fun/ppermute | solution.py:108
  156.7 1.4 slice_add_fusion.1
  158.1 1.0 copy-done.3
  159.3 0.8 slice.144
  160.0 1.6 collective-permute-start.13
  161.6 3.2 %shard_map.68 = bf16[2,3,768,1024]{3,2,1,0:T(8,128)(2,1)} custom-call(s32[1]{0:T(128)} %bitcast.8.me, bf16[16,3,96,1024]{3,2,1,0:T(8,128)(2,1)} %rows_ref.9, s32[16,3,32,96]{3,2,1,0:T(8,128)S(1)} %bitcast.31), custom_call_target="tpu_custom_call" | custom-call | flops 11796480 | bytes 2359296 | tf_op jit(solution)/shard_map/pallas_call | solution.py:53
  164.8 0.4 collective-permute-start.18
  165.3 1.1 constant_dynamic-update-slice_fusion.6
  166.4 3.1 %collective-permute-done.13 = bf16[2,4,16,1024]{3,2,1,0:T(8,128)(2,1)S(1)} collective-permute-done((bf16[2,4,16,1024]{3,2,1,0:T(8,128)(2,1)}, bf16[2,4,16,1024]{3,2,1,0:T(8,128)(2,1)S(1)}, u32[]{:S(2)}, u32[]{:S(2)}) %collective-permute-start.13) | collective-permute-done | bytes 262176 | tf_op jit(solution)/shard_map/ppermute | solution.py:108
  169.4 2.5 collective-permute-start.19
  172.1 1.2 collective-permute-start.20
  173.3 1.7 collective-permute-start.16
  175.0 2.4 constant_dynamic-update-slice_fusion.5
  177.4 2.4 constant_dynamic-update-slice_fusion.4
  179.8 73.5 %collective-permute-done.16 = bf16[1,4,16,1024]{3,2,1,0:T(8,128)(2,1)S(1)} collective-permute-done((bf16[1,4,16,1024]{3,2,1,0:T(8,128)(2,1)S(1)}, bf16[1,4,16,1024]{3,2,1,0:T(8,128)(2,1)S(1)}, u32[]{:S(2)}, u32[]{:S(2)}) %collective-permute-start.16) | collective-permute-done | bytes 131104 | tf_op jit(solution)/shard_map/ppermute | solution.py:108
  253.4 2.4 constant_dynamic-update-slice_fusion.3
  255.9 1.1 constant_dynamic-update-slice_fusion.2
  257.0 1.1 constant_dynamic-update-slice_fusion.1
  258.2 1.6 collective-permute-start.22
  259.8 1.1 constant_dynamic-update-slice_fusion
  260.9 1.8 collective-permute-done.22
  262.8 0.7 pad_maximum_fusion.7
  (58 shorter events, 2.6 us)
Async XLA Ops:
  0.6 11.8 %collective-permute-start.9 = (bf16[16,4096]{1,0:T(8,128)(2,1)}, bf16[16,4096]{1,0:T(8,128)(2,1)S(1)}, u32[]{:S(2)}, u32[]{:S(2)}) collective-permute-start(bf16[16,4096]{1,0:T(8,128)(2,1)} %param.7), channel_id=1, source_target_pairs={{0,4},{1,5},{2,6},{3,7},{4,0},{5,1},{6,2},{7,3},{8,12},{9,13},{10,... | collective-permute-start | bytes 393224 | tf_op jit(solution)/shard_map/ppermute | solution.py:108
  5.7 6.7 %collective-permute-start.10 = (bf16[16,128]{1,0:T(8,128)(2,1)S(1)}, bf16[16,128]{1,0:T(8,128)(2,1)S(1)}, u32[]{:S(2)}, u32[]{:S(2)}) collective-permute-start(bf16[16,128]{1,0:T(8,128)(2,1)S(1)} %fusion.8), channel_id=1, source_target_pairs={{0,4},{1,5},{2,6},{3,7},{4,0},{5,1},{6,2},{7,3},{8,12},{9,13},{10,... | collective-permute-start | bytes 12296 | tf_op jit(solution)/shard_map/ppermute | solution.py:108
  6.1 3.2 %copy-start = (s32[16,3,96,32]{2,3,1,0:T(8,128)S(1)}, s32[16,3,96,32]{2,3,1,0:T(8,128)}, u32[]{:S(2)}) copy-start(s32[16,3,96,32]{2,3,1,0:T(8,128)} %param.9) | copy-start | bytes 1769476
  9.2 3.2 %copy-start.7 = (bf16[16,4096]{1,0:T(8,128)(2,1)S(1)}, bf16[16,4096]{1,0:T(8,128)(2,1)}, u32[]{:S(2)}) copy-start(bf16[16,4096]{1,0:T(8,128)(2,1)} %param.7) | copy-start | bytes 393220
  12.4 10.6 %collective-permute-start.11 = (bf16[32,4224]{1,0:T(8,128)(2,1)S(1)}, bf16[32,4224]{1,0:T(8,128)(2,1)S(1)}, u32[]{:S(2)}, u32[]{:S(2)}) collective-permute-start(bf16[32,4224]{1,0:T(8,128)(2,1)S(1)} %maximum_maximum_fusion), channel_id=1, source_target_pairs={{0,2},{1,3},{2,0},{3,1},{4,6},{5,7},{6,4},{7,5},{8,10},{9,11},{10,... | collective-permute-start | bytes 811016 | tf_op jit(solution)/shard_map/ppermute | solution.py:108
  18.9 139.2 %collective-permute-start.12 = (bf16[2,3,96,1024]{3,2,1,0:T(8,128)(2,1)}, bf16[2,3,96,1024]{3,2,1,0:T(8,128)(2,1)S(1)}, u32[]{:S(2)}, u32[]{:S(2)}) collective-permute-start(bf16[2,3,96,1024]{3,2,1,0:T(8,128)(2,1)} %shard_map.69), channel_id=1, source_target_pairs={{0,4},{1,5},{2,6},{3,7},{4,0},{5,1},{6,2},{7,3},{8,12},{9,13},{10,... | collective-permute-start | bytes 3538952 | tf_op jit(solution)/shard_map/ppermute | solution.py:108
  21.8 150.2 %collective-permute-start.14 = (bf16[2,3,96,1024]{3,2,1,0:T(8,128)(2,1)}, bf16[2,3,96,1024]{3,2,1,0:T(8,128)(2,1)}, u32[]{:S(2)}, u32[]{:S(2)}) collective-permute-start(bf16[2,3,96,1024]{3,2,1,0:T(8,128)(2,1)} %shard_map.70), channel_id=1, source_target_pairs={{0,5},{1,4},{2,7},{3,6},{4,1},{5,0},{6,3},{7,2},{8,13},{9,12},{10,... | collective-permute-start | bytes 3538952 | tf_op jit(solution)/shard_map/ppermute | solution.py:108
  23.1 150.2 %collective-permute-start.15 = (bf16[2,3,96,1024]{3,2,1,0:T(8,128)(2,1)}, bf16[2,3,96,1024]{3,2,1,0:T(8,128)(2,1)}, u32[]{:S(2)}, u32[]{:S(2)}) collective-permute-start(bf16[2,3,96,1024]{3,2,1,0:T(8,128)(2,1)} %shard_map.72), channel_id=1, source_target_pairs={{0,1},{1,0},{2,3},{3,2},{4,5},{5,4},{6,7},{7,6},{8,9},{9,8},{10,11... | collective-permute-start | bytes 3538952 | tf_op jit(solution)/shard_map/ppermute | solution.py:108
  23.4 229.9 %collective-permute-start.17 = (bf16[2,3,96,1024]{3,2,1,0:T(8,128)(2,1)}, bf16[2,3,96,1024]{3,2,1,0:T(8,128)(2,1)}, u32[]{:S(2)}, u32[]{:S(2)}) collective-permute-start(bf16[2,3,96,1024]{3,2,1,0:T(8,128)(2,1)} %shard_map.71), channel_id=1, source_target_pairs={{0,6},{1,7},{2,4},{3,5},{4,2},{5,3},{6,0},{7,1},{8,14},{9,15},{10,... | collective-permute-start | bytes 3538952 | tf_op jit(solution)/shard_map/ppermute | solution.py:108
  28.5 6.4 %collective-permute-start = (bf16[64,2048]{1,0:T(8,128)(2,1)S(1)}, bf16[64,2048]{1,0:T(8,128)(2,1)S(1)}, u32[]{:S(2)}, u32[]{:S(2)}) collective-permute-start(bf16[64,2048]{1,0:T(8,128)(2,1)S(1)} %get-tuple-element.70), channel_id=1, source_target_pairs={{0,16},{8,24},{16,0},{24,8},{1,17},{9,25},{17,1},{25,9},{2,18},{10... | collective-permute-start | bytes 786440 | tf_op jit(solution)/shard_map/cond/branch_1_fun/ppermute | solution.py:108
  35.1 1.6 collective-permute-start.1
  36.7 49.5 %collective-permute-start.2 = (bf16[4,64,1024]{2,1,0:T(8,128)(2,1)S(1)}, bf16[4,64,1024]{2,1,0:T(8,128)(2,1)S(1)}, u32[]{:S(2)}, u32[]{:S(2)}) collective-permute-start(bf16[4,64,1024]{2,1,0:T(8,128)(2,1)S(1)} %bitcast.38), channel_id=1, source_target_pairs={{0,1},{1,0},{2,3},{3,2},{4,5},{5,4},{6,7},{7,6},{8,9},{9,8},{10,11... | collective-permute-start | bytes 1572872 | tf_op jit(solution)/shard_map/cond/branch_1_fun/ppermute | solution.py:108
  86.3 7.0 %collective-permute-start.3 = (bf16[64,128]{0,1:T(8,128)(2,1)S(1)}, bf16[64,128]{0,1:T(8,128)(2,1)S(1)}, u32[]{:S(2)}, u32[]{:S(2)}) collective-permute-start(bf16[64,128]{0,1:T(8,128)(2,1)S(1)} %slice.95), channel_id=1, source_target_pairs={{0,1},{1,0},{2,3},{3,2},{4,5},{5,4},{6,7},{7,6},{8,9},{9,8},{10,11... | collective-permute-start | bytes 49160 | tf_op jit(solution)/shard_map/cond/branch_1_fun/ppermute | solution.py:108
  93.5 3.5 %collective-permute-start.4 = (bf16[256,3072]{1,0:T(8,128)(2,1)S(1)}, bf16[256,3072]{1,0:T(8,128)(2,1)S(1)}, u32[]{:S(2)}, u32[]{:S(2)}) collective-permute-start(bf16[256,3072]{1,0:T(8,128)(2,1)S(1)} %slice.63), channel_id=1, source_target_pairs={{0,8},{8,0},{16,24},{24,16},{1,9},{9,1},{17,25},{25,17},{2,10},{10... | collective-permute-start | bytes 4718600 | tf_op jit(solution)/shard_map/cond/branch_1_fun/ppermute | solution.py:108
  97.5 1.7 copy-start.1
  100.2 19.9 %collective-permute-start.5 = (bf16[128,3072]{1,0:T(8,128)(2,1)}, bf16[128,3072]{1,0:T(8,128)(2,1)}, u32[]{:S(2)}, u32[]{:S(2)}) collective-permute-start(bf16[128,3072]{1,0:T(8,128)(2,1)} %slice.142), channel_id=1, source_target_pairs={{0,16},{8,24},{16,0},{24,8},{1,17},{9,25},{17,1},{25,9},{2,18},{10... | collective-permute-start | bytes 2359304 | tf_op jit(solution)/shard_map/cond/branch_1_fun/ppermute | solution.py:108
  122.1 10.4 %collective-permute-start.6 = (bf16[128,1536]{1,0:T(8,128)(2,1)S(1)}, bf16[128,1536]{1,0:T(8,128)(2,1)S(1)}, u32[]{:S(2)}, u32[]{:S(2)}) collective-permute-start(bf16[128,1536]{1,0:T(8,128)(2,1)S(1)} %multiply_convert_fusion), channel_id=1, source_target_pairs={{0,16},{8,24},{16,0},{24,8},{1,17},{9,25},{17,1},{25,9},{2,18},{10... | collective-permute-start | bytes 1179656 | tf_op jit(solution)/shard_map/cond/branch_1_fun/ppermute | solution.py:108
  132.6 3.2 %collective-permute-start.7 = (bf16[256,1536]{1,0:T(8,128)(2,1)S(1)}, bf16[256,1536]{1,0:T(8,128)(2,1)}, u32[]{:S(2)}, u32[]{:S(2)}) collective-permute-start(bf16[256,1536]{1,0:T(8,128)(2,1)S(1)} %pad_maximum_fusion.2), channel_id=1, source_target_pairs={{0,8},{8,0},{16,24},{24,16},{1,9},{9,1},{17,25},{25,17},{2,10},{10... | collective-permute-start | bytes 2359304 | tf_op jit(solution)/shard_map/cond/branch_1_fun/ppermute | solution.py:108
  135.8 2.1 copy-start.2
  142.3 14.4 %collective-permute-start.8 = (bf16[4,64,1024]{2,1,0:T(8,128)(2,1)S(1)}, bf16[4,64,1024]{2,1,0:T(8,128)(2,1)S(1)}, u32[]{:S(2)}, u32[]{:S(2)}) collective-permute-start(bf16[4,64,1024]{2,1,0:T(8,128)(2,1)S(1)} %slice.143), channel_id=1, source_target_pairs={{0,1},{1,0},{2,3},{3,2},{4,5},{5,4},{6,7},{7,6},{8,9},{9,8},{10,11... | collective-permute-start | bytes 1572872 | tf_op jit(solution)/shard_map/cond/branch_1_fun/ppermute | solution.py:108
  158.1 1.0 copy-start.3
  160.0 9.4 %collective-permute-start.13 = (bf16[2,4,16,1024]{3,2,1,0:T(8,128)(2,1)}, bf16[2,4,16,1024]{3,2,1,0:T(8,128)(2,1)S(1)}, u32[]{:S(2)}, u32[]{:S(2)}) collective-permute-start(bf16[2,4,16,1024]{3,2,1,0:T(8,128)(2,1)} %slice.144), channel_id=1, source_target_pairs={{0,2},{1,3},{2,0},{3,1},{4,6},{5,7},{6,4},{7,5},{8,10},{9,11},{10,... | collective-permute-start | bytes 786440 | tf_op jit(solution)/shard_map/ppermute | solution.py:108
  161.6 3.7 %copy-start.4 = (bf16[2,3,96,1024]{3,2,1,0:T(8,128)(2,1)S(1)}, bf16[2,3,96,1024]{3,2,1,0:T(8,128)(2,1)}, u32[]{:S(2)}) copy-start(bf16[2,3,96,1024]{3,2,1,0:T(8,128)(2,1)} %copy-done.3) | copy-start | bytes 3538948
  164.8 4.6 %copy-start.5 = (bf16[2,3,96,1024]{3,2,1,0:T(8,128)(2,1)S(1)}, bf16[2,3,96,1024]{3,2,1,0:T(8,128)(2,1)}, u32[]{:S(2)}) copy-start(bf16[2,3,96,1024]{3,2,1,0:T(8,128)(2,1)} %get-tuple-element.66) | copy-start | bytes 3538948
  164.8 7.2 %copy-start.6 = (bf16[2,3,96,1024]{3,2,1,0:T(8,128)(2,1)S(1)}, bf16[2,3,96,1024]{3,2,1,0:T(8,128)(2,1)}, u32[]{:S(2)}) copy-start(bf16[2,3,96,1024]{3,2,1,0:T(8,128)(2,1)} %get-tuple-element.67) | copy-start | bytes 3538948
  164.8 91.1 %collective-permute-start.18 = (bf16[2,3,96,1024]{3,2,1,0:T(8,128)(2,1)}, bf16[2,3,96,1024]{3,2,1,0:T(8,128)(2,1)S(1)}, u32[]{:S(2)}, u32[]{:S(2)}) collective-permute-start(bf16[2,3,96,1024]{3,2,1,0:T(8,128)(2,1)} %get-tuple-element.65), channel_id=1, source_target_pairs={{0,2},{1,3},{2,0},{3,1},{4,6},{5,7},{6,4},{7,5},{8,10},{9,11},{10,... | collective-permute-start | bytes 3538952 | tf_op jit(solution)/shard_map/ppermute | solution.py:108
  169.4 87.6 %collective-permute-start.19 = (bf16[2,3,96,1024]{3,2,1,0:T(8,128)(2,1)S(1)}, bf16[2,3,96,1024]{3,2,1,0:T(8,128)(2,1)S(1)}, u32[]{:S(2)}, u32[]{:S(2)}) collective-permute-start(bf16[2,3,96,1024]{3,2,1,0:T(8,128)(2,1)S(1)} %copy-done.5), channel_id=1, source_target_pairs={{0,3},{1,2},{2,1},{3,0},{4,7},{5,6},{6,5},{7,4},{8,11},{9,10},{10,... | collective-permute-start | bytes 3538952 | tf_op jit(solution)/shard_map/ppermute | solution.py:108
  172.1 87.7 %collective-permute-start.20 = (bf16[2,3,96,1024]{3,2,1,0:T(8,128)(2,1)S(1)}, bf16[2,3,96,1024]{3,2,1,0:T(8,128)(2,1)S(1)}, u32[]{:S(2)}, u32[]{:S(2)}) collective-permute-start(bf16[2,3,96,1024]{3,2,1,0:T(8,128)(2,1)S(1)} %copy-done.6), channel_id=1, source_target_pairs={{0,7},{1,6},{2,5},{3,4},{4,3},{5,2},{6,1},{7,0},{8,15},{9,14},{10,... | collective-permute-start | bytes 3538952 | tf_op jit(solution)/shard_map/ppermute | solution.py:108
  173.3 80.0 %collective-permute-start.16 = (bf16[1,4,16,1024]{3,2,1,0:T(8,128)(2,1)S(1)}, bf16[1,4,16,1024]{3,2,1,0:T(8,128)(2,1)S(1)}, u32[]{:S(2)}, u32[]{:S(2)}) collective-permute-start(bf16[1,4,16,1024]{3,2,1,0:T(8,128)(2,1)S(1)} %slice.145), channel_id=1, source_target_pairs={{0,4},{1,5},{2,6},{3,7},{4,0},{5,1},{6,2},{7,3},{8,12},{9,13},{10,... | collective-permute-start | bytes 393224 | tf_op jit(solution)/shard_map/ppermute | solution.py:108
  253.3 4.8 %collective-permute-start.21 = (bf16[32,1024]{1,0:T(8,128)(2,1)S(1)}, bf16[32,1024]{1,0:T(8,128)(2,1)S(1)}, u32[]{:S(2)}, u32[]{:S(2)}) collective-permute-start(bf16[32,1024]{1,0:T(8,128)(2,1)S(1)} %bitcast.42), channel_id=1, source_target_pairs={{0,8},{8,0},{16,24},{24,16},{1,9},{9,1},{17,25},{25,17},{2,10},{10... | collective-permute-start | bytes 196616 | tf_op jit(solution)/shard_map/ppermute | solution.py:108
  258.2 4.6 %collective-permute-start.22 = (bf16[16,2048]{1,0:T(8,128)(2,1)S(1)}, bf16[16,2048]{1,0:T(8,128)(2,1)S(1)}, u32[]{:S(2)}, u32[]{:S(2)}) collective-permute-start(bf16[16,2048]{1,0:T(8,128)(2,1)S(1)} %fusion.1), channel_id=1, source_target_pairs={{0,16},{8,24},{16,0},{24,8},{1,17},{9,25},{17,1},{25,9},{2,18},{10... | collective-permute-start | bytes 196616 | tf_op jit(solution)/shard_map/ppermute | solution.py:108

commit v3 on v2

--- a/solution.py
+++ b/solution.py
@@ -99,9 +99,9 @@
     )(learner_rows, exponents)
 
 
-def place(elements, block, me, partner):
+def place(elements, block, me, partner, first):
     row = (me[0] ^ partner) * block.shape[2]
-    return lax.dynamic_update_slice(elements, block, (0, 0, row, 0))
+    return lax.dynamic_update_slice(elements, block, (first, 0, row, 0))
 
 
 def swap(value, axis, bit):
@@ -224,20 +224,20 @@
     me = lax.axis_index("expert").astype(jnp.int32).reshape(1)
     exponents = exponents.swapaxes(2, 3)
 
-    half = bits[0]
-    far, near = list(range(half, owners)), list(range(1, half))
+    half, low = bits[0], low_bits("expert")[0] * 2
+    far = [(d, 0, per_owner) for d in sorted(range(half, owners), key=lambda d: d % low)]
     first, second, third, fourth = (far[i * half // 4 : (i + 1) * half // 4] for i in range(4))
-    begin, rest = near[: (half - 1) // 3], near[(half - 1) // 3 :]
-    late = rest + fourth
-
-    def block(partner, learner_rows, exponents):
-        return encode(
-            learner_rows, exponents, me, partner, 0, per_owner, unit_rows, lambda m: 0
-        )
+    begin = [(d, 0, per_owner) for d in range(low, half) if d % low]
+    rest = [(d, 0, per_owner) for d in range(1, half) if d < low or not d % low]
+    fourth = [(d, k, 1) for k in range(per_owner) for d, _, _ in fourth]
+    soon, late = fourth[: half // 4], fourth[half // 4 :]
+
+    def block(key, learner_rows, exponents):
+        return encode(learner_rows, exponents, me, *key, unit_rows, lambda m: 0)
 
     sent, arrived = {}, {}
-    for d in first + second + third + begin:
-        sent[d] = block(d, learner_rows, exponents)
+    for key in first + second + third + begin:
+        sent[key] = block(key, learner_rows, exponents)
 
     def after(value, keys, table):
         value, *blocks = together(value, *[table[key] for key in keys])
@@ -246,43 +246,47 @@
 
     def send(keys):
         for key in keys:
-            arrived[key] = swap(sent[key], "expert", key)
+            arrived[key] = swap(sent[key], "expert", key[0])
 
     table = gather(share_table(expert_ids, route_probs, experts), "expert", z_bits[:1])
-    held = gather(tokens, "expert", z_bits[:1])
+    held = after(tokens, first, sent)
+    held = gather(held, "expert", z_bits[:1])
+    held = after(held, second, sent)
     held = jnp.concatenate([held, table], axis=1)
-    held = after(held, first + second, sent)
-    send(first + second)
     held = gather(held, "expert", z_bits[1:])
     held = after(held, third + begin, sent)
-    send(third + begin)
+    send(first + second + third + begin)
 
     def serve(held, learner_rows, exponents):
-        makes = [functools.partial(block, d, learner_rows, exponents) for d in late]
+        makes = [functools.partial(block, d, learner_rows, exponents) for d in soon + late + rest]
         return layer(held, learner_rows, exponents, makes)
 
     def idle(held, learner_rows, exponents):
         out = jnp.zeros((groups, held.shape[0], width), jnp.float32)
-        return out, *[block(d, learner_rows, exponents) for d in late]
+        return out, *[block(d, learner_rows, exponents) for d in soon + late + rest]
 
     out, *blocks = lax.cond(
         expert_ids[0, 0] >= 0, serve, idle, held, learner_rows, exponents
     )
-    sent.update(zip(late, blocks))
+    sent.update(zip(soon + late + rest, blocks))
     out = after(out, first, arrived)
 
     out = out.reshape(groups, -1, tok_rows, width).swapaxes(0, 1)
-    for bit, there in zip(reversed(z_bits), (second + begin, third, [], [])):
-        out = halve(out, "expert", [bit])
-        out = after(out, there, arrived)
+    out = halve(out, "expert", z_bits[1:])
+    out = after(out, second + begin, arrived)
+    out = after(out, soon + rest, sent)
+    send(soon + rest)
+    out = halve(out, "expert", z_bits[:1])
+    out = after(out, third, arrived)
+    out = after(out, late, sent)
     send(late)
     mixed = uncolumns(out.astype(jnp.bfloat16).reshape(groups * tok_rows, width), group_bits)
 
     elements = encode(
         learner_rows, exponents, me, 0, 0, per_owner, owners * unit_rows, lambda m: m
     )
-    for key in first + second + begin + third + rest + fourth:
-        elements = place(elements, arrived[key], me, key)
+    for key in first + second + begin + third + rest + soon + late:
+        elements = place(elements, arrived[key], me, *key[:2])
     return elements, mixed
 
 

time: 265 us -> 235 us (0.89)
  waiting for transfers between devices: 140 us -> 110 us
    ppermute x23 -> x24, waiting for transfers between devices: 140 us -> 110 us  [swap(): lax.ppermute(value, axis, [(i, i ^ bit) for i in range(lax.axis_size(axis...]
    pallas_call x8 -> x9, Pallas kernels: 25.1 us -> 27 us  [encode(): pl.pallas_call(encode_kernel, out_shape=jax.ShapeDtypeStruct((count, part...]
    ppermute x23 -> x24, starting transfers between devices: 28.4 us -> 27.1 us  [swap(): lax.ppermute(value, axis, [(i, i ^ bit) for i in range(lax.axis_size(axis...]
    dynamic_update_slice x7 -> x8, local copies, waits for them, and re-layouts: 11.8 us -> 12.4 us  [place(): return lax.dynamic_update_slice(elements, block, (first, 0, row, 0))]
  transfers between devices with their start and end apart: 23 -> 24, of which waited for: 10 -> 13; matrix products, arithmetic and copies ran while one was open for 14% -> 15% of each run, Pallas kernels for 20% -> 22%
where the time goes in v3:
time: 235 us; the launch traced here: 231 us
  waiting for transfers between devices  110 us (47%)
  Pallas kernels  54.1 us (23%)
  starting transfers between devices  27.1 us (12%)
  local copies, waits for them, and re-layouts  22.2 us (9%)
  matrix products  9.57 us (4%)
  other arithmetic  6.83 us (3%)
    ppermute x24, waiting for transfers between devices, swap(): lax.ppermute(value, axis, [(i, i ^ bit) for i in range(lax.axis_size(axis...  110 us
    ppermute x24, starting transfers between devices, swap(): lax.ppermute(value, axis, [(i, i ^ bit) for i in range(lax.axis_size(axis...  27.1 us
    pallas_call x9, Pallas kernels, encode(): pl.pallas_call(encode_kernel, out_shape=jax.ShapeDtypeStruct((count, part...  27 us
    pallas_call x2, Pallas kernels, dequantize(): pl.pallas_call(functools.partial(weights_kernel, first), out_shape=jax.Sh...  27 us
    dynamic_update_slice x8, local copies, waits for them, and re-layouts, place(): return lax.dynamic_update_slice(elements, block, (first, 0, row, 0))  12.4 us
    dot_general x1, matrix products, layer(): lax.dot_general(held.reshape(groups * slots, width), pair.reshape(-1, wid...  6.46 us
  transfers between devices with their start and end apart: 24, of which 13 were waited for; matrix products, arithmetic and copies ran while one was open for 15% of the time, Pallas kernels for 22%

profile of v3, /device:TPU:8, one launch (start us, length us, event | category | flops | bytes accessed | tf_op | source)
XLA Modules:
  0.0 231.3 jit_solution(18098684243546369754)
XLA Ops:
  0.7 3.2 %shard_map.69 = bf16[2,3,96,1024]{3,2,1,0:T(8,128)(2,1)} custom-call(s32[1]{0:T(128)} %bitcast.8.me, bf16[16,3,96,1024]{3,2,1,0:T(8,128)(2,1)} %rows_ref.9, s32[16,3,32,96]{3,2,1,0:T(8,128)} %bitcast.25), custom_call_target="tpu_custom_call" | custom-call | flops 11796480 | bytes 2359296 | tf_op jit(solution)/shard_map/pallas_call | solution.py:53
  3.9 2.6 %collective-permute-start.9 = (bf16[16,4096]{1,0:T(8,128)(2,1)S(1)}, bf16[16,4096]{1,0:T(8,128)(2,1)S(1)}, u32[]{:S(2)}, u32[]{:S(2)}) collective-permute-start(bf16[16,4096]{1,0:T(8,128)(2,1)S(1)} %copy-done.9), channel_id=1, source_target_pairs={{0,4},{1,5},{2,6},{3,7},{4,0},{5,1},{6,2},{7,3},{8,12},{9,13},{10,... | collective-permute-start | bytes 393224 | tf_op jit(solution)/shard_map/ppermute | solution.py:108
  7.3 3.1 %shard_map.70 = bf16[2,3,96,1024]{3,2,1,0:T(8,128)(2,1)} custom-call(s32[1]{0:T(128)} %bitcast.8.me, bf16[16,3,96,1024]{3,2,1,0:T(8,128)(2,1)} %rows_ref.9, s32[16,3,32,96]{3,2,1,0:T(8,128)S(1)} %bitcast.26), custom_call_target="tpu_custom_call" | custom-call | flops 11796480 | bytes 2359296 | tf_op jit(solution)/shard_map/pallas_call | solution.py:53
  10.4 1.7 collective-permute-done.9
  12.2 1.3 collective-permute-start.11
  13.5 2.2 collective-permute-start.12
  15.7 3.1 %shard_map.71 = bf16[2,3,96,1024]{3,2,1,0:T(8,128)(2,1)} custom-call(s32[1]{0:T(128)} %bitcast.8.me, bf16[16,3,96,1024]{3,2,1,0:T(8,128)(2,1)} %rows_ref.9, s32[16,3,32,96]{3,2,1,0:T(8,128)S(1)} %bitcast.27), custom_call_target="tpu_custom_call" | custom-call | flops 11796480 | bytes 2359296 | tf_op jit(solution)/shard_map/pallas_call | solution.py:53
  18.8 3.1 %shard_map.72 = bf16[2,3,96,1024]{3,2,1,0:T(8,128)(2,1)} custom-call(s32[1]{0:T(128)} %bitcast.8.me, bf16[16,3,96,1024]{3,2,1,0:T(8,128)(2,1)} %rows_ref.9, s32[16,3,32,96]{3,2,1,0:T(8,128)S(1)} %bitcast.28), custom_call_target="tpu_custom_call" | custom-call | flops 11796480 | bytes 2359296 | tf_op jit(solution)/shard_map/pallas_call | solution.py:53
  21.9 0.5 collective-permute-start.14
  22.4 1.6 collective-permute-done.11
  24.1 3.2 %collective-permute-start.15 = (bf16[2,3,96,1024]{3,2,1,0:T(8,128)(2,1)}, bf16[2,3,96,1024]{3,2,1,0:T(8,128)(2,1)}, u32[]{:S(2)}, u32[]{:S(2)}) collective-permute-start(bf16[2,3,96,1024]{3,2,1,0:T(8,128)(2,1)} %shard_map.72), channel_id=1, source_target_pairs={{0,3},{1,2},{2,1},{3,0},{4,7},{5,6},{6,5},{7,4},{8,11},{9,10},{10,... | collective-permute-start | bytes 3538952 | tf_op jit(solution)/shard_map/ppermute | solution.py:108
  27.3 1.5 collective-permute-start.17
  28.8 0.5 slice.82
  29.9 107.2 %conditional.1 = (f32[4,64,1024]{2,1,0:T(8,128)S(1)}, bf16[1,3,96,1024]{3,2,1,0:T(8,128)(2,1)}, bf16[1,3,96,1024]{3,2,1,0:T(8,128)(2,1)}, bf16[2,3,96,1024]{3,2,1,0:T(8,128)(2,1)}, bf16[2,3,96,1024]{3,2,1,0:T(8,128)(2,1)}) conditional(s32[]{:T(128)} %bitcast.10, (s32[1]{0:T(128)}, bf16[16,3,96,1024]{3,2,1,0:T(8,128)(2,1)}, ...), branch_computations={%region_2.3_spmd, %region_3.5_spmd} | conditional | flops 5003421696 | bytes 123851288 | solution.py:268
  30.2 1.6 collective-permute-start
  31.8 5.6 %collective-permute-done = bf16[64,2048]{1,0:T(8,128)(2,1)S(1)} collective-permute-done((bf16[64,2048]{1,0:T(8,128)(2,1)S(1)}, bf16[64,2048]{1,0:T(8,128)(2,1)S(1)}, u32[]{:S(2)}, u32[]{:S(2)}) %collective-permute-start) | collective-permute-done | bytes 262176 | tf_op jit(solution)/shard_map/cond/branch_1_fun/ppermute | solution.py:108
  37.6 1.5 collective-permute-done.1
  39.1 0.7 collective-permute-start.2
  39.8 1.4 copy.21
  41.2 0.8 slice.95
  42.0 14.8 %branch_1_fun.6 = bf16[2,16,96,1024]{3,2,1,0:T(8,128)(2,1)} custom-call(bf16[16,3,96,1024]{3,2,1,0:T(8,128)(2,1)} %get-tuple-element.18.rows_ref, s32[16,3,32,96]{3,2,1,0:T(8,128)S(1)} %get-tuple-element.19.exponent_ref), custom_call_target="tpu_custom_call" | custom-call | flops 78643200 | bytes 12582912 | tf_op jit(solution)/shard_map/cond/branch_1_fun/pallas_call | solution.py:87
  56.8 1.4 collective-permute-start.3
  58.2 6.5 %convolution_convert_fusion = bf16[512,3072]{1,0:T(8,128)(2,1)S(1)} fusion(bf16[512,1024]{1,0:T(8,128)(2,1)S(1)} %bitcast.41, bf16[3072,1024]{1,0:T(8,128)(2,1)} %bitcast.32), kind=kOutput, calls=%fused_computation | convolution fusion | flops 3222798336 | bytes 10485760 | tf_op jit(solution)/shard_map/cond/branch_1_fun/dot_general | solution.py:189
  65.0 3.4 %collective-permute-done.4 = bf16[256,3072]{1,0:T(8,128)(2,1)S(1)} collective-permute-done((bf16[256,3072]{1,0:T(8,128)(2,1)S(1)}, bf16[256,3072]{1,0:T(8,128)(2,1)S(1)}, u32[]{:S(2)}, u32[]{:S(2)}) %collective-permute-start.4) | collective-permute-done | bytes 1572896 | tf_op jit(solution)/shard_map/cond/branch_1_fun/ppermute | solution.py:108
  68.9 1.7 copy-done.1
  70.5 1.0 slice.142
  71.5 1.5 collective-permute-start.5
  73.0 12.3 %branch_1_fun.7 = bf16[1,16,96,1024]{3,2,1,0:T(8,128)(2,1)} custom-call(bf16[16,3,96,1024]{3,2,1,0:T(8,128)(2,1)} %get-tuple-element.18.rows_ref, s32[16,3,32,96]{3,2,1,0:T(8,128)S(1)} %get-tuple-element.19.exponent_ref), custom_call_target="tpu_custom_call" | custom-call | flops 39321600 | bytes 6291456 | tf_op jit(solution)/shard_map/cond/branch_1_fun/pallas_call | solution.py:87
  85.6 5.8 %collective-permute-done.5 = bf16[128,3072]{1,0:T(8,128)(2,1)} collective-permute-done((bf16[128,3072]{1,0:T(8,128)(2,1)}, bf16[128,3072]{1,0:T(8,128)(2,1)}, u32[]{:S(2)}, u32[]{:S(2)}) %collective-permute-start.5) | collective-permute-done | bytes 786464 | tf_op jit(solution)/shard_map/cond/branch_1_fun/ppermute | solution.py:108
  91.4 1.8 slice_add_fusion
  93.5 1.6 collective-permute-start.6
  95.1 8.8 %collective-permute-done.6 = bf16[128,1536]{1,0:T(8,128)(2,1)S(1)} collective-permute-done((bf16[128,1536]{1,0:T(8,128)(2,1)S(1)}, bf16[128,1536]{1,0:T(8,128)(2,1)S(1)}, u32[]{:S(2)}, u32[]{:S(2)}) %collective-permute-start.6) | collective-permute-done | bytes 393248 | tf_op jit(solution)/shard_map/cond/branch_1_fun/ppermute | solution.py:108
  104.0 2.5 %branch_1_fun.8 = bf16[1,3,96,1024]{3,2,1,0:T(8,128)(2,1)} custom-call(s32[1]{0:T(128)} %get-tuple-element.26.me, bf16[16,3,96,1024]{3,2,1,0:T(8,128)(2,1)} %get-tuple-element.18.rows_ref, s32[16,3,32,96]{3,2,1,0:T(8,128)S(1)} %get-tuple-element.19.exponent_ref), custom_call_target="tpu_custom_call" | custom-call | flops 5898240 | bytes 1179648 | tf_op jit(solution)/shard_map/cond/branch_1_fun/pallas_call | solution.py:53
  106.5 2.5 %branch_1_fun.9 = bf16[1,3,96,1024]{3,2,1,0:T(8,128)(2,1)} custom-call(s32[1]{0:T(128)} %get-tuple-element.26.me, bf16[16,3,96,1024]{3,2,1,0:T(8,128)(2,1)} %get-tuple-element.18.rows_ref, s32[16,3,32,96]{3,2,1,0:T(8,128)S(1)} %get-tuple-element.19.exponent_ref), custom_call_target="tpu_custom_call" | custom-call | flops 5898240 | bytes 1179648 | tf_op jit(solution)/shard_map/cond/branch_1_fun/pallas_call | solution.py:53
  109.0 1.4 pad_maximum_fusion
  110.4 0.7 copy-done.2
  111.1 3.1 %fusion.10 = f32[4,128,1024]{2,1,0:T(8,128)} fusion(bf16[4,128,1536]{2,1,0:T(8,128)(2,1)S(1)} %bitcast.40, bf16[1536,1024,1]{1,0,2:T(8,128)(2,1)S(1)} %bitcast.37), kind=kOutput, calls=%fused_computation.62 | convolution fusion | flops 1610612736 | bytes 6815744 | tf_op jit(solution)/shard_map/cond/branch_1_fun/dot_general | solution.py:207
  114.3 1.3 slice.143
  115.6 0.8 collective-permute-start.8
  116.3 3.1 %branch_1_fun.10 = bf16[2,3,96,1024]{3,2,1,0:T(8,128)(2,1)} custom-call(s32[1]{0:T(128)} %get-tuple-element.26.me, bf16[16,3,96,1024]{3,2,1,0:T(8,128)(2,1)} %get-tuple-element.18.rows_ref, s32[16,3,32,96]{3,2,1,0:T(8,128)S(1)} %get-tuple-element.19.exponent_ref), custom_call_target="tpu_custom_call" | custom-call | flops 11796480 | bytes 2359296 | tf_op jit(solution)/shard_map/cond/branch_1_fun/pallas_call | solution.py:53
  119.4 3.1 %branch_1_fun.11 = bf16[2,3,96,1024]{3,2,1,0:T(8,128)(2,1)} custom-call(s32[1]{0:T(128)} %get-tuple-element.26.me, bf16[16,3,96,1024]{3,2,1,0:T(8,128)(2,1)} %get-tuple-element.18.rows_ref, s32[16,3,32,96]{3,2,1,0:T(8,128)S(1)} %get-tuple-element.19.exponent_ref), custom_call_target="tpu_custom_call" | custom-call | flops 11796480 | bytes 2359296 | tf_op jit(solution)/shard_map/cond/branch_1_fun/pallas_call | solution.py:53
  122.5 13.2 %collective-permute-done.8 = bf16[4,64,1024]{2,1,0:T(8,128)(2,1)S(1)} collective-permute-done((bf16[4,64,1024]{2,1,0:T(8,128)(2,1)S(1)}, bf16[4,64,1024]{2,1,0:T(8,128)(2,1)S(1)}, u32[]{:S(2)}, u32[]{:S(2)}) %collective-permute-start.8) | collective-permute-done | bytes 524320 | tf_op jit(solution)/shard_map/cond/branch_1_fun/ppermute | solution.py:108
  135.8 1.4 slice_add_fusion.1
  137.2 1.0 copy-done.3
  138.3 0.8 slice.144
  139.1 3.2 %shard_map.68 = bf16[2,3,768,1024]{3,2,1,0:T(8,128)(2,1)} custom-call(s32[1]{0:T(128)} %bitcast.8.me, bf16[16,3,96,1024]{3,2,1,0:T(8,128)(2,1)} %rows_ref.9, s32[16,3,32,96]{3,2,1,0:T(8,128)S(1)} %bitcast.31), custom_call_target="tpu_custom_call" | custom-call | flops 11796480 | bytes 2359296 | tf_op jit(solution)/shard_map/pallas_call | solution.py:53
  142.3 1.1 constant_dynamic-update-slice_fusion.7
  143.4 27.5 %collective-permute-done.13 = bf16[2,4,16,1024]{3,2,1,0:T(8,128)(2,1)S(1)} collective-permute-done((bf16[2,4,16,1024]{3,2,1,0:T(8,128)(2,1)}, bf16[2,4,16,1024]{3,2,1,0:T(8,128)(2,1)S(1)}, u32[]{:S(2)}, u32[]{:S(2)}) %collective-permute-start.13) | collective-permute-done | bytes 262176 | tf_op jit(solution)/shard_map/ppermute | solution.py:108
  171.0 2.3 %collective-permute-start.16 = (bf16[1,4,16,1024]{3,2,1,0:T(8,128)(2,1)S(1)}, bf16[1,4,16,1024]{3,2,1,0:T(8,128)(2,1)S(1)}, u32[]{:S(2)}, u32[]{:S(2)}) collective-permute-start(bf16[1,4,16,1024]{3,2,1,0:T(8,128)(2,1)S(1)} %slice.145), channel_id=1, source_target_pairs={{0,4},{1,5},{2,6},{3,7},{4,0},{5,1},{6,2},{7,3},{8,12},{9,13},{10,... | collective-permute-start | bytes 393224 | tf_op jit(solution)/shard_map/ppermute | solution.py:108
  173.3 0.5 collective-permute-start.18
  174.0 2.4 %collective-permute-start.20 = (bf16[1,3,96,1024]{3,2,1,0:T(8,128)(2,1)S(1)}, bf16[1,3,96,1024]{3,2,1,0:T(8,128)(2,1)S(1)}, u32[]{:S(2)}, u32[]{:S(2)}) collective-permute-start(bf16[1,3,96,1024]{3,2,1,0:T(8,128)(2,1)S(1)} %copy-done.7), channel_id=1, source_target_pairs={{0,7},{1,6},{2,5},{3,4},{4,3},{5,2},{6,1},{7,0},{8,15},{9,14},{10,... | collective-permute-start | bytes 1769480 | tf_op jit(solution)/shard_map/ppermute | solution.py:108
  176.4 2.4 %constant_dynamic-update-slice_fusion.6 = bf16[2,3,768,1024]{3,2,1,0:T(8,128)(2,1)} fusion(bf16[2,3,768,1024]{3,2,1,0:T(8,128)(2,1)} %constant_dynamic-update-slice_fusion.7, bf16[2,3,96,1024]{3,2,1,0:T(8,128)(2,1)} %collective-permute-done.14, s32[]{:T(128)S(6)} %select_n.76), kind=kLoop, calls=%fused_computation.58 | loop fusion | bytes 2359300 | tf_op jit(solution)/shard_map/dynamic_update_slice | solution.py:104
  179.0 2.5 %constant_dynamic-update-slice_fusion.5 = bf16[2,3,768,1024]{3,2,1,0:T(8,128)(2,1)} fusion(bf16[2,3,768,1024]{3,2,1,0:T(8,128)(2,1)} %constant_dynamic-update-slice_fusion.6, bf16[2,3,96,1024]{3,2,1,0:T(8,128)(2,1)} %collective-permute-done.15, s32[]{:T(128)S(6)} %select_n.77), kind=kLoop, calls=%fused_computation.57 | loop fusion | bytes 2359300 | tf_op jit(solution)/shard_map/dynamic_update_slice | solution.py:104
  181.4 0.6 collective-permute-start.21
  182.1 1.6 collective-permute-start.23
  183.7 2.4 %constant_dynamic-update-slice_fusion.4 = bf16[2,3,768,1024]{3,2,1,0:T(8,128)(2,1)} fusion(bf16[2,3,768,1024]{3,2,1,0:T(8,128)(2,1)} %constant_dynamic-update-slice_fusion.5, bf16[2,3,96,1024]{3,2,1,0:T(8,128)(2,1)} %collective-permute-done.17, s32[]{:T(128)S(6)} %select_n.78), kind=kLoop, calls=%fused_computation.56 | loop fusion | bytes 2359300 | tf_op jit(solution)/shard_map/dynamic_update_slice | solution.py:104
  186.4 0.7 pad_maximum_fusion.8
  187.1 36.4 %collective-permute-done.18 = bf16[2,3,96,1024]{3,2,1,0:T(8,128)(2,1)S(1)} collective-permute-done((bf16[2,3,96,1024]{3,2,1,0:T(8,128)(2,1)S(1)}, bf16[2,3,96,1024]{3,2,1,0:T(8,128)(2,1)S(1)}, u32[]{:S(2)}, u32[]{:S(2)}) %collective-permute-start.18) | collective-permute-done | bytes 1179680 | tf_op jit(solution)/shard_map/ppermute | solution.py:108
  223.5 1.1 constant_dynamic-update-slice_fusion.3
  224.7 2.3 collective-permute-done.19
  226.9 1.1 constant_dynamic-update-slice_fusion.2
  228.1 0.9 constant_dynamic-update-slice_fusion.1
  228.9 1.5 collective-permute-done.21
  230.4 0.9 constant_dynamic-update-slice_fusion
  (71 shorter events, 3.5 us)
Async XLA Ops:
  0.6 3.3 %copy-start.9 = (bf16[16,4096]{1,0:T(8,128)(2,1)S(1)}, bf16[16,4096]{1,0:T(8,128)(2,1)}, u32[]{:S(2)}) copy-start(bf16[16,4096]{1,0:T(8,128)(2,1)} %param.7) | copy-start | bytes 393220
  0.6 5.9 %copy-start.10 = (f32[16,8]{0,1:T(8,128)S(1)}, f32[16,8]{0,1:T(8,128)}, u32[]{:S(2)}) copy-start(f32[16,8]{0,1:T(8,128)} %param.11) | copy-start | bytes 1540
  0.7 6.0 %copy-start.11 = (s32[16,8]{0,1:T(8,128)S(1)}, s32[16,8]{0,1:T(8,128)}, u32[]{:S(2)}) copy-start(s32[16,8]{0,1:T(8,128)} %param.10) | copy-start | bytes 1540
  0.7 6.6 %copy-start = (s32[16,3,96,32]{2,3,1,0:T(8,128)S(1)}, s32[16,3,96,32]{2,3,1,0:T(8,128)}, u32[]{:S(2)}) copy-start(s32[16,3,96,32]{2,3,1,0:T(8,128)} %param.9) | copy-start | bytes 1769476
  3.9 8.2 %collective-permute-start.9 = (bf16[16,4096]{1,0:T(8,128)(2,1)S(1)}, bf16[16,4096]{1,0:T(8,128)(2,1)S(1)}, u32[]{:S(2)}, u32[]{:S(2)}) collective-permute-start(bf16[16,4096]{1,0:T(8,128)(2,1)S(1)} %copy-done.9), channel_id=1, source_target_pairs={{0,4},{1,5},{2,6},{3,7},{4,0},{5,1},{6,2},{7,3},{8,12},{9,13},{10,... | collective-permute-start | bytes 393224 | tf_op jit(solution)/shard_map/ppermute | solution.py:108
  6.9 5.3 %collective-permute-start.10 = (bf16[16,128]{1,0:T(8,128)(2,1)S(1)}, bf16[16,128]{1,0:T(8,128)(2,1)S(1)}, u32[]{:S(2)}, u32[]{:S(2)}) collective-permute-start(bf16[16,128]{1,0:T(8,128)(2,1)S(1)} %fusion.8), channel_id=1, source_target_pairs={{0,4},{1,5},{2,6},{3,7},{4,0},{5,1},{6,2},{7,3},{8,12},{9,13},{10,... | collective-permute-start | bytes 12296 | tf_op jit(solution)/shard_map/ppermute | solution.py:108
  12.2 11.8 %collective-permute-start.11 = (bf16[32,4224]{1,0:T(8,128)(2,1)S(1)}, bf16[32,4224]{1,0:T(8,128)(2,1)S(1)}, u32[]{:S(2)}, u32[]{:S(2)}) collective-permute-start(bf16[32,4224]{1,0:T(8,128)(2,1)S(1)} %maximum_maximum_fusion), channel_id=1, source_target_pairs={{0,2},{1,3},{2,0},{3,1},{4,6},{5,7},{6,4},{7,5},{8,10},{9,11},{10,... | collective-permute-start | bytes 811016 | tf_op jit(solution)/shard_map/ppermute | solution.py:108
  13.5 123.6 %collective-permute-start.12 = (bf16[2,3,96,1024]{3,2,1,0:T(8,128)(2,1)}, bf16[2,3,96,1024]{3,2,1,0:T(8,128)(2,1)S(1)}, u32[]{:S(2)}, u32[]{:S(2)}) collective-permute-start(bf16[2,3,96,1024]{3,2,1,0:T(8,128)(2,1)} %shard_map.69), channel_id=1, source_target_pairs={{0,4},{1,5},{2,6},{3,7},{4,0},{5,1},{6,2},{7,3},{8,12},{9,13},{10,... | collective-permute-start | bytes 3538952 | tf_op jit(solution)/shard_map/ppermute | solution.py:108
  21.9 149.0 %collective-permute-start.14 = (bf16[2,3,96,1024]{3,2,1,0:T(8,128)(2,1)}, bf16[2,3,96,1024]{3,2,1,0:T(8,128)(2,1)}, u32[]{:S(2)}, u32[]{:S(2)}) collective-permute-start(bf16[2,3,96,1024]{3,2,1,0:T(8,128)(2,1)} %shard_map.70), channel_id=1, source_target_pairs={{0,6},{1,7},{2,4},{3,5},{4,2},{5,3},{6,0},{7,1},{8,14},{9,15},{10,... | collective-permute-start | bytes 3538952 | tf_op jit(solution)/shard_map/ppermute | solution.py:108
  24.1 146.8 %collective-permute-start.15 = (bf16[2,3,96,1024]{3,2,1,0:T(8,128)(2,1)}, bf16[2,3,96,1024]{3,2,1,0:T(8,128)(2,1)}, u32[]{:S(2)}, u32[]{:S(2)}) collective-permute-start(bf16[2,3,96,1024]{3,2,1,0:T(8,128)(2,1)} %shard_map.72), channel_id=1, source_target_pairs={{0,3},{1,2},{2,1},{3,0},{4,7},{5,6},{6,5},{7,4},{8,11},{9,10},{10,... | collective-permute-start | bytes 3538952 | tf_op jit(solution)/shard_map/ppermute | solution.py:108
  27.3 151.6 %collective-permute-start.17 = (bf16[2,3,96,1024]{3,2,1,0:T(8,128)(2,1)}, bf16[2,3,96,1024]{3,2,1,0:T(8,128)(2,1)}, u32[]{:S(2)}, u32[]{:S(2)}) collective-permute-start(bf16[2,3,96,1024]{3,2,1,0:T(8,128)(2,1)} %shard_map.71), channel_id=1, source_target_pairs={{0,5},{1,4},{2,7},{3,6},{4,1},{5,0},{6,3},{7,2},{8,13},{9,12},{10,... | collective-permute-start | bytes 3538952 | tf_op jit(solution)/shard_map/ppermute | solution.py:108
  30.2 7.2 %collective-permute-start = (bf16[64,2048]{1,0:T(8,128)(2,1)S(1)}, bf16[64,2048]{1,0:T(8,128)(2,1)S(1)}, u32[]{:S(2)}, u32[]{:S(2)}) collective-permute-start(bf16[64,2048]{1,0:T(8,128)(2,1)S(1)} %get-tuple-element.87), channel_id=1, source_target_pairs={{0,16},{8,24},{16,0},{24,8},{1,17},{9,25},{17,1},{25,9},{2,18},{10... | collective-permute-start | bytes 786440 | tf_op jit(solution)/shard_map/cond/branch_1_fun/ppermute | solution.py:108
  37.5 1.6 collective-permute-start.1
  39.1 17.6 %collective-permute-start.2 = (bf16[4,64,1024]{2,1,0:T(8,128)(2,1)S(1)}, bf16[4,64,1024]{2,1,0:T(8,128)(2,1)S(1)}, u32[]{:S(2)}, u32[]{:S(2)}) collective-permute-start(bf16[4,64,1024]{2,1,0:T(8,128)(2,1)S(1)} %bitcast.38), channel_id=1, source_target_pairs={{0,1},{1,0},{2,3},{3,2},{4,5},{5,4},{6,7},{7,6},{8,9},{9,8},{10,11... | collective-permute-start | bytes 1572872 | tf_op jit(solution)/shard_map/cond/branch_1_fun/ppermute | solution.py:108
  56.8 7.9 %collective-permute-start.3 = (bf16[64,128]{0,1:T(8,128)(2,1)S(1)}, bf16[64,128]{0,1:T(8,128)(2,1)S(1)}, u32[]{:S(2)}, u32[]{:S(2)}) collective-permute-start(bf16[64,128]{0,1:T(8,128)(2,1)S(1)} %slice.95), channel_id=1, source_target_pairs={{0,1},{1,0},{2,3},{3,2},{4,5},{5,4},{6,7},{7,6},{8,9},{9,8},{10,11... | collective-permute-start | bytes 49160 | tf_op jit(solution)/shard_map/cond/branch_1_fun/ppermute | solution.py:108
  64.9 3.5 %collective-permute-start.4 = (bf16[256,3072]{1,0:T(8,128)(2,1)S(1)}, bf16[256,3072]{1,0:T(8,128)(2,1)S(1)}, u32[]{:S(2)}, u32[]{:S(2)}) collective-permute-start(bf16[256,3072]{1,0:T(8,128)(2,1)S(1)} %slice.63), channel_id=1, source_target_pairs={{0,8},{8,0},{16,24},{24,16},{1,9},{9,1},{17,25},{25,17},{2,10},{10... | collective-permute-start | bytes 4718600 | tf_op jit(solution)/shard_map/cond/branch_1_fun/ppermute | solution.py:108
  68.9 1.7 copy-start.1
  71.5 19.9 %collective-permute-start.5 = (bf16[128,3072]{1,0:T(8,128)(2,1)}, bf16[128,3072]{1,0:T(8,128)(2,1)}, u32[]{:S(2)}, u32[]{:S(2)}) collective-permute-start(bf16[128,3072]{1,0:T(8,128)(2,1)} %slice.142), channel_id=1, source_target_pairs={{0,16},{8,24},{16,0},{24,8},{1,17},{9,25},{17,1},{25,9},{2,18},{10... | collective-permute-start | bytes 2359304 | tf_op jit(solution)/shard_map/cond/branch_1_fun/ppermute | solution.py:108
  93.5 10.4 %collective-permute-start.6 = (bf16[128,1536]{1,0:T(8,128)(2,1)S(1)}, bf16[128,1536]{1,0:T(8,128)(2,1)S(1)}, u32[]{:S(2)}, u32[]{:S(2)}) collective-permute-start(bf16[128,1536]{1,0:T(8,128)(2,1)S(1)} %multiply_convert_fusion), channel_id=1, source_target_pairs={{0,16},{8,24},{16,0},{24,8},{1,17},{9,25},{17,1},{25,9},{2,18},{10... | collective-permute-start | bytes 1179656 | tf_op jit(solution)/shard_map/cond/branch_1_fun/ppermute | solution.py:108
  103.9 5.1 %collective-permute-start.7 = (bf16[256,1536]{1,0:T(8,128)(2,1)S(1)}, bf16[256,1536]{1,0:T(8,128)(2,1)}, u32[]{:S(2)}, u32[]{:S(2)}) collective-permute-start(bf16[256,1536]{1,0:T(8,128)(2,1)S(1)} %pad_maximum_fusion.2), channel_id=1, source_target_pairs={{0,8},{8,0},{16,24},{24,16},{1,9},{9,1},{17,25},{25,17},{2,10},{10... | collective-permute-start | bytes 2359304 | tf_op jit(solution)/shard_map/cond/branch_1_fun/ppermute | solution.py:108
  109.0 2.1 copy-start.2
  115.6 20.2 %collective-permute-start.8 = (bf16[4,64,1024]{2,1,0:T(8,128)(2,1)S(1)}, bf16[4,64,1024]{2,1,0:T(8,128)(2,1)S(1)}, u32[]{:S(2)}, u32[]{:S(2)}) collective-permute-start(bf16[4,64,1024]{2,1,0:T(8,128)(2,1)S(1)} %slice.143), channel_id=1, source_target_pairs={{0,1},{1,0},{2,3},{3,2},{4,5},{5,4},{6,7},{7,6},{8,9},{9,8},{10,11... | collective-permute-start | bytes 1572872 | tf_op jit(solution)/shard_map/cond/branch_1_fun/ppermute | solution.py:108
  137.2 1.0 copy-start.3
  139.1 31.8 %collective-permute-start.13 = (bf16[2,4,16,1024]{3,2,1,0:T(8,128)(2,1)}, bf16[2,4,16,1024]{3,2,1,0:T(8,128)(2,1)S(1)}, u32[]{:S(2)}, u32[]{:S(2)}) collective-permute-start(bf16[2,4,16,1024]{3,2,1,0:T(8,128)(2,1)} %slice.144), channel_id=1, source_target_pairs={{0,2},{1,3},{2,0},{3,1},{4,6},{5,7},{6,4},{7,5},{8,10},{9,11},{10,... | collective-permute-start | bytes 786440 | tf_op jit(solution)/shard_map/ppermute | solution.py:108
  139.1 3.2 %copy-start.4 = (bf16[2,3,96,1024]{3,2,1,0:T(8,128)(2,1)S(1)}, bf16[2,3,96,1024]{3,2,1,0:T(8,128)(2,1)}, u32[]{:S(2)}) copy-start(bf16[2,3,96,1024]{3,2,1,0:T(8,128)(2,1)} %copy-done.3) | copy-start | bytes 3538948
  142.3 31.0 %copy-start.5 = (bf16[2,3,96,1024]{3,2,1,0:T(8,128)(2,1)S(1)}, bf16[2,3,96,1024]{3,2,1,0:T(8,128)(2,1)}, u32[]{:S(2)}) copy-start(bf16[2,3,96,1024]{3,2,1,0:T(8,128)(2,1)} %get-tuple-element.79) | copy-start | bytes 3538948
  142.3 31.6 %copy-start.6 = (bf16[2,3,96,1024]{3,2,1,0:T(8,128)(2,1)S(1)}, bf16[2,3,96,1024]{3,2,1,0:T(8,128)(2,1)}, u32[]{:S(2)}) copy-start(bf16[2,3,96,1024]{3,2,1,0:T(8,128)(2,1)} %get-tuple-element.80) | copy-start | bytes 3538948
  142.3 31.8 %copy-start.7 = (bf16[1,3,96,1024]{3,2,1,0:T(8,128)(2,1)S(1)}, bf16[1,3,96,1024]{3,2,1,0:T(8,128)(2,1)}, u32[]{:S(2)}) copy-start(bf16[1,3,96,1024]{3,2,1,0:T(8,128)(2,1)} %get-tuple-element.81) | copy-start | bytes 1769476
  171.0 7.9 %collective-permute-start.16 = (bf16[1,4,16,1024]{3,2,1,0:T(8,128)(2,1)S(1)}, bf16[1,4,16,1024]{3,2,1,0:T(8,128)(2,1)S(1)}, u32[]{:S(2)}, u32[]{:S(2)}) collective-permute-start(bf16[1,4,16,1024]{3,2,1,0:T(8,128)(2,1)S(1)} %slice.145), channel_id=1, source_target_pairs={{0,4},{1,5},{2,6},{3,7},{4,0},{5,1},{6,2},{7,3},{8,12},{9,13},{10,... | collective-permute-start | bytes 393224 | tf_op jit(solution)/shard_map/ppermute | solution.py:108
  173.3 50.2 %collective-permute-start.18 = (bf16[2,3,96,1024]{3,2,1,0:T(8,128)(2,1)S(1)}, bf16[2,3,96,1024]{3,2,1,0:T(8,128)(2,1)S(1)}, u32[]{:S(2)}, u32[]{:S(2)}) collective-permute-start(bf16[2,3,96,1024]{3,2,1,0:T(8,128)(2,1)S(1)} %copy-done.5), channel_id=1, source_target_pairs={{0,1},{1,0},{2,3},{3,2},{4,5},{5,4},{6,7},{7,6},{8,9},{9,8},{10,11... | collective-permute-start | bytes 3538952 | tf_op jit(solution)/shard_map/ppermute | solution.py:108
  173.8 53.1 %collective-permute-start.19 = (bf16[2,3,96,1024]{3,2,1,0:T(8,128)(2,1)S(1)}, bf16[2,3,96,1024]{3,2,1,0:T(8,128)(2,1)S(1)}, u32[]{:S(2)}, u32[]{:S(2)}) collective-permute-start(bf16[2,3,96,1024]{3,2,1,0:T(8,128)(2,1)S(1)} %copy-done.6), channel_id=1, source_target_pairs={{0,2},{1,3},{2,0},{3,1},{4,6},{5,7},{6,4},{7,5},{8,10},{9,11},{10,... | collective-permute-start | bytes 3538952 | tf_op jit(solution)/shard_map/ppermute | solution.py:108
  174.0 54.0 %collective-permute-start.20 = (bf16[1,3,96,1024]{3,2,1,0:T(8,128)(2,1)S(1)}, bf16[1,3,96,1024]{3,2,1,0:T(8,128)(2,1)S(1)}, u32[]{:S(2)}, u32[]{:S(2)}) collective-permute-start(bf16[1,3,96,1024]{3,2,1,0:T(8,128)(2,1)S(1)} %copy-done.7), channel_id=1, source_target_pairs={{0,7},{1,6},{2,5},{3,4},{4,3},{5,2},{6,1},{7,0},{8,15},{9,14},{10,... | collective-permute-start | bytes 1769480 | tf_op jit(solution)/shard_map/ppermute | solution.py:108
  178.8 2.6 %copy-start.8 = (bf16[1,3,96,1024]{3,2,1,0:T(8,128)(2,1)S(1)}, bf16[1,3,96,1024]{3,2,1,0:T(8,128)(2,1)}, u32[]{:S(2)}) copy-start(bf16[1,3,96,1024]{3,2,1,0:T(8,128)(2,1)} %get-tuple-element.84) | copy-start | bytes 1769476
  178.9 3.1 %collective-permute-start.22 = (bf16[32,1024]{1,0:T(8,128)(2,1)S(1)}, bf16[32,1024]{1,0:T(8,128)(2,1)S(1)}, u32[]{:S(2)}, u32[]{:S(2)}) collective-permute-start(bf16[32,1024]{1,0:T(8,128)(2,1)S(1)} %bitcast.42), channel_id=1, source_target_pairs={{0,8},{8,0},{16,24},{24,16},{1,9},{9,1},{17,25},{25,17},{2,10},{10... | collective-permute-start | bytes 196616 | tf_op jit(solution)/shard_map/ppermute | solution.py:108
  181.4 49.0 %collective-permute-start.21 = (bf16[1,3,96,1024]{3,2,1,0:T(8,128)(2,1)S(1)}, bf16[1,3,96,1024]{3,2,1,0:T(8,128)(2,1)S(1)}, u32[]{:S(2)}, u32[]{:S(2)}) collective-permute-start(bf16[1,3,96,1024]{3,2,1,0:T(8,128)(2,1)S(1)} %copy-done.8), channel_id=1, source_target_pairs={{0,7},{1,6},{2,5},{3,4},{4,3},{5,2},{6,1},{7,0},{8,15},{9,14},{10,... | collective-permute-start | bytes 1769480 | tf_op jit(solution)/shard_map/ppermute | solution.py:108
  182.1 4.3 %collective-permute-start.23 = (bf16[16,2048]{1,0:T(8,128)(2,1)S(1)}, bf16[16,2048]{1,0:T(8,128)(2,1)S(1)}, u32[]{:S(2)}, u32[]{:S(2)}) collective-permute-start(bf16[16,2048]{1,0:T(8,128)(2,1)S(1)} %fusion.1), channel_id=1, source_target_pairs={{0,16},{8,24},{16,0},{24,8},{1,17},{9,25},{17,1},{25,9},{2,18},{10... | collective-permute-start | bytes 196616 | tf_op jit(solution)/shard_map/ppermute | solution.py:108

commit v4 on v3

--- a/solution.py
+++ b/solution.py
@@ -42,34 +42,35 @@
         out_ref[0, part] = value.astype(out_ref.dtype)
 
 
-def encode(learner_rows, exponents, me, partner, first, count, out_rows, out_block):
+def encode(learner_rows, exponents, me, partner, out_rows, out_block):
     experts, parts, unit_rows, width = learner_rows.shape
     blocks = exponents.shape[2]
     per_owner = experts // lax.axis_size("expert")
 
-    def place(i, s):
-        return ((s[0] ^ partner) * per_owner + first + i, 0, 0, 0)
-
-    return pl.pallas_call(
+    def expert(i, s):
+        return ((s[0] ^ partner) * per_owner + i, 0, 0, 0)
+
+    value = pl.pallas_call(
         encode_kernel,
-        out_shape=jax.ShapeDtypeStruct((count, parts, out_rows, width), learner_rows.dtype),
+        out_shape=jax.ShapeDtypeStruct((per_owner, parts, out_rows, width), learner_rows.dtype),
         grid_spec=pltpu.PrefetchScalarGridSpec(
             num_scalar_prefetch=1,
-            grid=(count,),
+            grid=(per_owner,),
             in_specs=[
-                pl.BlockSpec((1, parts, unit_rows, width), place),
-                pl.BlockSpec((1, parts, blocks, unit_rows), place),
+                pl.BlockSpec((1, parts, unit_rows, width), expert),
+                pl.BlockSpec((1, parts, blocks, unit_rows), expert),
             ],
             out_specs=pl.BlockSpec(
                 (1, parts, unit_rows, width), lambda i, s: (i, 0, out_block(s[0]), 0)
             ),
         ),
         cost_estimate=pl.CostEstimate(
-            flops=20 * count * parts * unit_rows * width,
-            bytes_accessed=4 * count * parts * unit_rows * width,
+            flops=20 * per_owner * parts * unit_rows * width,
+            bytes_accessed=4 * per_owner * parts * unit_rows * width,
             transcendentals=0,
         ),
     )(me, learner_rows, exponents)
+    return value.reshape(per_owner * parts, out_rows, width)
 
 
 def weights_kernel(first, rows_ref, exponent_ref, out_ref):
@@ -99,9 +100,8 @@
     )(learner_rows, exponents)
 
 
-def place(elements, block, me, partner, first):
-    row = (me[0] ^ partner) * block.shape[2]
-    return lax.dynamic_update_slice(elements, block, (first, 0, row, 0))
+def place(elements, block, me, partner):
+    return lax.dynamic_update_slice(elements, block, (0, (me[0] ^ partner) * block.shape[1], 0))
 
 
 def swap(value, axis, bit):
@@ -182,10 +182,21 @@
     table = held[:, groups * width :]
     held = columns(held[:, : groups * width], group_bits).reshape(groups, rows, width)
     pair = dequantize(learner_rows, exponents, 0, 2)
+
+    def swap_all(values, bit):
+        rows = [value.reshape(-1, width) for value in values]
+        got = swap(jnp.concatenate(rows, axis=0), "expert", bit)
+        ends = [sum(part.shape[0] for part in rows[:i]) for i in range(len(rows) + 1)]
+        return [
+            got[start:end].reshape(value.shape)
+            for start, end, value in zip(ends, ends[1:], values)
+        ]
+
     for bit in x_bits:
-        held = jnp.concatenate([held, swap(held, "expert", bit)], axis=1)
+        got, got_table = swap_all([held, table], bit)
+        held = jnp.concatenate([held, got], axis=1)
+        table = jnp.concatenate([table, got_table], axis=0)
     held, pair, table = together(held, pair, table)
-    table = gather(table, "expert", x_bits)
     partial = lax.dot_general(
         held.reshape(groups * slots, width),
         pair.reshape(-1, width),
@@ -201,16 +212,13 @@
     hidden = jax.nn.silu(partial[:, :units]) * partial[:, units:]
     shared = hidden.reshape(-1, experts, unit_rows) * table[:, :, None]
     shared = shared.astype(jnp.bfloat16).reshape(-1, units)
-    middle = len(encode_more) // 2
-    more = [make() for make in encode_more]
-    shared, *first = together(gather(shared, "fsdp", group_bits), *more[:middle])
+    shared, *more = together(gather(shared, "fsdp", group_bits), *encode_more())
     out = jnp.dot(shared, down.reshape(-1, width), preferred_element_type=jnp.float32)
     out = out.reshape(groups, slots, width)
     for bit in reversed(x_bits):
         kept = out.shape[1] // 2
         out = out[:, :kept] + swap(out[:, kept:].astype(jnp.bfloat16), "expert", bit)
-    out, *second = together(out, *more[middle:])
-    return out, *first, *second
+    return out, *more
 
 
 def body(tokens, learner_rows, exponents, expert_ids, route_probs):
@@ -225,19 +233,21 @@
     exponents = exponents.swapaxes(2, 3)
 
     half, low = bits[0], low_bits("expert")[0] * 2
-    far = [(d, 0, per_owner) for d in sorted(range(half, owners), key=lambda d: d % low)]
+    straight = list(range(half, owners, low))
+    turning = [d for d in range(half, owners) if d % low]
+    far = turning[: half // 4] + straight + turning[half // 4 :]
     first, second, third, fourth = (far[i * half // 4 : (i + 1) * half // 4] for i in range(4))
-    begin = [(d, 0, per_owner) for d in range(low, half) if d % low]
-    rest = [(d, 0, per_owner) for d in range(1, half) if d < low or not d % low]
-    fourth = [(d, k, 1) for k in range(per_owner) for d, _, _ in fourth]
-    soon, late = fourth[: half // 4], fourth[half // 4 :]
-
-    def block(key, learner_rows, exponents):
-        return encode(learner_rows, exponents, me, *key, unit_rows, lambda m: 0)
-
-    sent, arrived = {}, {}
-    for key in first + second + third + begin:
-        sent[key] = block(key, learner_rows, exponents)
+    begin = [d for d in range(low, half) if d % low]
+    late = fourth + [d for d in range(1, half) if d not in begin]
+
+    def blocks(partners, learner_rows, exponents):
+        unit_rows = learner_rows.shape[2]
+        return [
+            encode(learner_rows, exponents, me, d, unit_rows, lambda m: 0) for d in partners
+        ]
+
+    early = first + second + third + begin
+    sent, arrived = dict(zip(early, blocks(early, learner_rows, exponents))), {}
 
     def after(value, keys, table):
         value, *blocks = together(value, *[table[key] for key in keys])
@@ -246,7 +256,7 @@
 
     def send(keys):
         for key in keys:
-            arrived[key] = swap(sent[key], "expert", key[0])
+            arrived[key] = swap(sent[key], "expert", key)
 
     table = gather(share_table(expert_ids, route_probs, experts), "expert", z_bits[:1])
     held = after(tokens, first, sent)
@@ -255,39 +265,34 @@
     held = jnp.concatenate([held, table], axis=1)
     held = gather(held, "expert", z_bits[1:])
     held = after(held, third + begin, sent)
-    send(first + second + third + begin)
+    send(early)
 
     def serve(held, learner_rows, exponents):
-        makes = [functools.partial(block, d, learner_rows, exponents) for d in soon + late + rest]
-        return layer(held, learner_rows, exponents, makes)
+        return layer(
+            held, learner_rows, exponents, lambda: blocks(late, learner_rows, exponents)
+        )
 
     def idle(held, learner_rows, exponents):
         out = jnp.zeros((groups, held.shape[0], width), jnp.float32)
-        return out, *[block(d, learner_rows, exponents) for d in soon + late + rest]
-
-    out, *blocks = lax.cond(
-        expert_ids[0, 0] >= 0, serve, idle, held, learner_rows, exponents
-    )
-    sent.update(zip(soon + late + rest, blocks))
+        return out, *blocks(late, learner_rows, exponents)
+
+    out, *got = lax.cond(expert_ids[0, 0] >= 0, serve, idle, held, learner_rows, exponents)
+    sent.update(zip(late, got))
     out = after(out, first, arrived)
 
     out = out.reshape(groups, -1, tok_rows, width).swapaxes(0, 1)
     out = halve(out, "expert", z_bits[1:])
     out = after(out, second + begin, arrived)
-    out = after(out, soon + rest, sent)
-    send(soon + rest)
+    out = after(out, late, sent)
+    send(late)
     out = halve(out, "expert", z_bits[:1])
     out = after(out, third, arrived)
-    out = after(out, late, sent)
-    send(late)
     mixed = uncolumns(out.astype(jnp.bfloat16).reshape(groups * tok_rows, width), group_bits)
 
-    elements = encode(
-        learner_rows, exponents, me, 0, 0, per_owner, owners * unit_rows, lambda m: m
-    )
-    for key in first + second + begin + third + rest + soon + late:
-        elements = place(elements, arrived[key], me, *key[:2])
-    return elements, mixed
+    elements = encode(learner_rows, exponents, me, 0, owners * unit_rows, lambda m: m)
+    for partner in first + second + begin + third + late[len(fourth) :] + fourth:
+        elements = place(elements, arrived[partner], me, partner)
+    return elements.reshape(per_owner, parts, owners * unit_rows, width), mixed
 
 
 def solution(mesh):

time: 235 us -> 228 us (0.970); the launches traced: 231 us -> 227 us
  waiting for transfers between devices: 110 us -> 103 us
  starting transfers between devices: 27.1 us -> 32.1 us
    ppermute x24 -> x22, waiting for transfers between devices: 110 us -> 103 us  [swap(): lax.ppermute(value, axis, [(i, i ^ bit) for i in range(lax.axis_size(axis...]
    ppermute x24 -> x22, starting transfers between devices: 27.1 us -> 32.1 us  [swap(): lax.ppermute(value, axis, [(i, i ^ bit) for i in range(lax.axis_size(axis...]
    pallas_call x9 -> x8, Pallas kernels: 27 us -> 25.2 us  [encode(): pl.pallas_call(encode_kernel, out_shape=jax.ShapeDtypeStruct((per_owner,...]
    dynamic_update_slice x8 -> x7, local copies, waits for them, and re-layouts: 12.4 us -> 11.8 us  [place(): lax.dynamic_update_slice(elements, block, (0, (me[0] ^ partner) * block.s...]
  transfers between devices with their start and end apart: 24 -> 22, of which waited for: 13 -> 14; matrix products, arithmetic and copies ran while one was open for 15% -> 15% of each run, Pallas kernels for 22% -> 22%
where the time goes in v4:
time: 228 us; the launch traced here: 227 us
  waiting for transfers between devices  103 us (45%)
  Pallas kernels  52.2 us (23%)
  starting transfers between devices  32.1 us (14%)
  local copies, waits for them, and re-layouts  22.4 us (10%)
  matrix products  8.27 us (4%)
  other arithmetic  7.05 us (3%)
    ppermute x22, waiting for transfers between devices, swap(): lax.ppermute(value, axis, [(i, i ^ bit) for i in range(lax.axis_size(axis...  103 us
    ppermute x22, starting transfers between devices, swap(): lax.ppermute(value, axis, [(i, i ^ bit) for i in range(lax.axis_size(axis...  32.1 us
    pallas_call x2, Pallas kernels, dequantize(): pl.pallas_call(functools.partial(weights_kernel, first), out_shape=jax.Sh...  27 us
    pallas_call x8, Pallas kernels, encode(): pl.pallas_call(encode_kernel, out_shape=jax.ShapeDtypeStruct((per_owner,...  25.2 us
    dynamic_update_slice x7, local copies, waits for them, and re-layouts, place(): lax.dynamic_update_slice(elements, block, (0, (me[0] ^ partner) * block.s...  11.8 us
    dot_general x1, matrix products, layer(): lax.dot_general(held.reshape(groups * slots, width), pair.reshape(-1, wid...  6.48 us
  transfers between devices with their start and end apart: 22, of which 14 were waited for; matrix products, arithmetic and copies ran while one was open for 15% of the time, Pallas kernels for 22%

profile of v4, /device:TPU:8, one launch (start us, length us, event | category | flops | bytes accessed | tf_op | source)
XLA Modules:
  0.0 227.0 jit_solution(6709475550476801293)
XLA Ops:
  0.7 3.2 %shard_map.69 = bf16[2,3,96,1024]{3,2,1,0:T(8,128)(2,1)} custom-call(s32[1]{0:T(128)} %bitcast.15.me, bf16[16,3,96,1024]{3,2,1,0:T(8,128)(2,1)} %rows_ref.9, s32[16,3,32,96]{3,2,1,0:T(8,128)} %bitcast.38), custom_call_target="tpu_custom_call" | custom-call | flops 11796480 | bytes 2359296 | tf_op jit(solution)/shard_map/pallas_call | solution.py:53
  3.9 2.6 %collective-permute-start.8 = (bf16[16,4096]{1,0:T(8,128)(2,1)S(1)}, bf16[16,4096]{1,0:T(8,128)(2,1)S(1)}, u32[]{:S(2)}, u32[]{:S(2)}) collective-permute-start(bf16[16,4096]{1,0:T(8,128)(2,1)S(1)} %copy-done.8), channel_id=1, source_target_pairs={{0,4},{1,5},{2,6},{3,7},{4,0},{5,1},{6,2},{7,3},{8,12},{9,13},{10,... | collective-permute-start | bytes 393224 | tf_op jit(solution)/shard_map/ppermute | solution.py:108
  6.9 0.3 collective-permute-start.9
  7.3 3.2 %shard_map.70 = bf16[2,3,96,1024]{3,2,1,0:T(8,128)(2,1)} custom-call(s32[1]{0:T(128)} %bitcast.15.me, bf16[16,3,96,1024]{3,2,1,0:T(8,128)(2,1)} %rows_ref.9, s32[16,3,32,96]{3,2,1,0:T(8,128)S(1)} %bitcast.39), custom_call_target="tpu_custom_call" | custom-call | flops 11796480 | bytes 2359296 | tf_op jit(solution)/shard_map/pallas_call | solution.py:53
  10.4 1.7 collective-permute-done.8
  12.2 1.3 collective-permute-start.10
  13.5 3.1 %collective-permute-start.11 = (bf16[6,96,1024]{2,1,0:T(8,128)(2,1)}, bf16[6,96,1024]{2,1,0:T(8,128)(2,1)S(1)}, u32[]{:S(2)}, u32[]{:S(2)}) collective-permute-start(bf16[6,96,1024]{2,1,0:T(8,128)(2,1)} %bitcast.59), channel_id=1, source_target_pairs={{0,5},{1,4},{2,7},{3,6},{4,1},{5,0},{6,3},{7,2},{8,13},{9,12},{10,... | collective-permute-start | bytes 3538952 | tf_op jit(solution)/shard_map/ppermute | solution.py:108
  16.6 3.1 %shard_map.71 = bf16[2,3,96,1024]{3,2,1,0:T(8,128)(2,1)} custom-call(s32[1]{0:T(128)} %bitcast.15.me, bf16[16,3,96,1024]{3,2,1,0:T(8,128)(2,1)} %rows_ref.9, s32[16,3,32,96]{3,2,1,0:T(8,128)S(1)} %bitcast.40), custom_call_target="tpu_custom_call" | custom-call | flops 11796480 | bytes 2359296 | tf_op jit(solution)/shard_map/pallas_call | solution.py:53
  19.7 3.1 %shard_map.72 = bf16[2,3,96,1024]{3,2,1,0:T(8,128)(2,1)} custom-call(s32[1]{0:T(128)} %bitcast.15.me, bf16[16,3,96,1024]{3,2,1,0:T(8,128)(2,1)} %rows_ref.9, s32[16,3,32,96]{3,2,1,0:T(8,128)S(1)} %bitcast.41), custom_call_target="tpu_custom_call" | custom-call | flops 11796480 | bytes 2359296 | tf_op jit(solution)/shard_map/pallas_call | solution.py:53
  22.8 0.8 collective-permute-start.13
  23.9 3.4 %collective-permute-start.14 = (bf16[6,96,1024]{2,1,0:T(8,128)(2,1)}, bf16[6,96,1024]{2,1,0:T(8,128)(2,1)}, u32[]{:S(2)}, u32[]{:S(2)}) collective-permute-start(bf16[6,96,1024]{2,1,0:T(8,128)(2,1)} %bitcast.58), channel_id=1, source_target_pairs={{0,3},{1,2},{2,1},{3,0},{4,7},{5,6},{6,5},{7,4},{8,11},{9,10},{10,... | collective-permute-start | bytes 3538952 | tf_op jit(solution)/shard_map/ppermute | solution.py:108
  27.3 2.0 collective-permute-start.16
  29.3 0.5 slice.88
  30.4 106.1 %conditional.1 = (f32[4,64,1024]{2,1,0:T(8,128)S(1)}, bf16[6,96,1024]{2,1,0:T(8,128)(2,1)}, bf16[6,96,1024]{2,1,0:T(8,128)(2,1)}, bf16[6,96,1024]{2,1,0:T(8,128)(2,1)}) conditional(s32[]{:T(128)} %bitcast.18, (s32[1]{0:T(128)}, bf16[16,3,96,1024]{3,2,1,0:T(8,128)(2,1)}, s32[16,3,32,96]{3,2,1,0:T(8,128)S(1)}) %tuple.47, ...), branch_computations={%region_2.3_spmd, %region_3.5_spmd} | conditional | flops 5005043712 | bytes 126157312 | solution.py:279
  30.7 1.6 collective-permute-start
  32.3 5.3 %collective-permute-done = bf16[64,2048]{1,0:T(8,128)(2,1)S(1)} collective-permute-done((bf16[64,2048]{1,0:T(8,128)(2,1)S(1)}, bf16[64,2048]{1,0:T(8,128)(2,1)S(1)}, u32[]{:S(2)}, u32[]{:S(2)}) %collective-permute-start) | collective-permute-done | bytes 262176 | tf_op jit(solution)/shard_map/cond/branch_1_fun/ppermute | solution.py:108
  37.8 1.4 copy.44
  39.2 0.8 slice.101
  40.1 0.8 pad_maximum_fusion.3
  40.9 14.8 %branch_1_fun.5 = bf16[2,16,96,1024]{3,2,1,0:T(8,128)(2,1)} custom-call(bf16[16,3,96,1024]{3,2,1,0:T(8,128)(2,1)} %get-tuple-element.18.rows_ref, s32[16,3,32,96]{3,2,1,0:T(8,128)S(1)} %get-tuple-element.19.exponent_ref), custom_call_target="tpu_custom_call" | custom-call | flops 78643200 | bytes 12582912 | tf_op jit(solution)/shard_map/cond/branch_1_fun/pallas_call | solution.py:88
  55.7 4.5 %collective-permute-done.2 = bf16[264,1024]{1,0:T(8,128)(2,1)} collective-permute-done((bf16[264,1024]{1,0:T(8,128)(2,1)}, bf16[264,1024]{1,0:T(8,128)(2,1)}, u32[]{:S(2)}, u32[]{:S(2)}) %collective-permute-start.2) | collective-permute-done | bytes 540704 | tf_op jit(solution)/shard_map/cond/branch_1_fun/ppermute | solution.py:108
  60.3 0.7 slice.103
  61.1 0.7 pad_maximum_fusion.6
  61.8 1.1 slice.102
  63.0 6.5 %convolution_convert_fusion = bf16[512,3072]{1,0:T(8,128)(2,1)S(1)} fusion(bf16[512,1024]{1,0:T(8,128)(2,1)S(1)} %bitcast.66, bf16[3072,1024]{1,0:T(8,128)(2,1)} %bitcast.47), kind=kOutput, calls=%fused_computation | convolution fusion | flops 3222798336 | bytes 10485760 | tf_op jit(solution)/shard_map/cond/branch_1_fun/dot_general | solution.py:200
  69.7 3.3 %collective-permute-done.3 = bf16[256,3072]{1,0:T(8,128)(2,1)S(1)} collective-permute-done((bf16[256,3072]{1,0:T(8,128)(2,1)S(1)}, bf16[256,3072]{1,0:T(8,128)(2,1)S(1)}, u32[]{:S(2)}, u32[]{:S(2)}) %collective-permute-start.3) | collective-permute-done | bytes 1572896 | tf_op jit(solution)/shard_map/cond/branch_1_fun/ppermute | solution.py:108
  73.1 0.5 convert_add_fusion
  73.6 1.7 copy-done.1
  75.3 1.0 slice.150
  76.3 1.5 collective-permute-start.4
  77.8 12.2 %branch_1_fun.6 = bf16[1,16,96,1024]{3,2,1,0:T(8,128)(2,1)} custom-call(bf16[16,3,96,1024]{3,2,1,0:T(8,128)(2,1)} %get-tuple-element.18.rows_ref, s32[16,3,32,96]{3,2,1,0:T(8,128)S(1)} %get-tuple-element.19.exponent_ref), custom_call_target="tpu_custom_call" | custom-call | flops 39321600 | bytes 6291456 | tf_op jit(solution)/shard_map/cond/branch_1_fun/pallas_call | solution.py:88
  90.4 5.8 %collective-permute-done.4 = bf16[128,3072]{1,0:T(8,128)(2,1)} collective-permute-done((bf16[128,3072]{1,0:T(8,128)(2,1)}, bf16[128,3072]{1,0:T(8,128)(2,1)}, u32[]{:S(2)}, u32[]{:S(2)}) %collective-permute-start.4) | collective-permute-done | bytes 786464 | tf_op jit(solution)/shard_map/cond/branch_1_fun/ppermute | solution.py:108
  96.2 1.8 slice_add_fusion
  98.2 1.6 collective-permute-start.5
  99.8 8.8 %collective-permute-done.5 = bf16[128,1536]{1,0:T(8,128)(2,1)S(1)} collective-permute-done((bf16[128,1536]{1,0:T(8,128)(2,1)S(1)}, bf16[128,1536]{1,0:T(8,128)(2,1)S(1)}, u32[]{:S(2)}, u32[]{:S(2)}) %collective-permute-start.5) | collective-permute-done | bytes 393248 | tf_op jit(solution)/shard_map/cond/branch_1_fun/ppermute | solution.py:108
  108.7 3.1 %branch_1_fun.8 = bf16[2,3,96,1024]{3,2,1,0:T(8,128)(2,1)} custom-call(s32[1]{0:T(128)} %get-tuple-element.26.me, bf16[16,3,96,1024]{3,2,1,0:T(8,128)(2,1)} %get-tuple-element.18.rows_ref, s32[16,3,32,96]{3,2,1,0:T(8,128)S(1)} %get-tuple-element.19.exponent_ref), custom_call_target="tpu_custom_call" | custom-call | flops 11796480 | bytes 2359296 | tf_op jit(solution)/shard_map/cond/branch_1_fun/pallas_call | solution.py:53
  111.9 3.1 %branch_1_fun.9 = bf16[2,3,96,1024]{3,2,1,0:T(8,128)(2,1)} custom-call(s32[1]{0:T(128)} %get-tuple-element.26.me, bf16[16,3,96,1024]{3,2,1,0:T(8,128)(2,1)} %get-tuple-element.18.rows_ref, s32[16,3,32,96]{3,2,1,0:T(8,128)S(1)} %get-tuple-element.19.exponent_ref), custom_call_target="tpu_custom_call" | custom-call | flops 11796480 | bytes 2359296 | tf_op jit(solution)/shard_map/cond/branch_1_fun/pallas_call | solution.py:53
  115.0 3.1 %branch_1_fun.7 = bf16[2,3,96,1024]{3,2,1,0:T(8,128)(2,1)} custom-call(s32[1]{0:T(128)} %get-tuple-element.26.me, bf16[16,3,96,1024]{3,2,1,0:T(8,128)(2,1)} %get-tuple-element.18.rows_ref, s32[16,3,32,96]{3,2,1,0:T(8,128)S(1)} %get-tuple-element.19.exponent_ref), custom_call_target="tpu_custom_call" | custom-call | flops 11796480 | bytes 2359296 | tf_op jit(solution)/shard_map/cond/branch_1_fun/pallas_call | solution.py:53
  118.1 1.4 pad_maximum_fusion
  119.5 0.7 copy-done.2
  120.2 1.8 fusion.10
  122.1 0.6 collective-permute-start.7
  122.7 13.8 %collective-permute-done.7 = bf16[4,64,1024]{2,1,0:T(8,128)(2,1)S(1)} collective-permute-done((bf16[4,64,1024]{2,1,0:T(8,128)(2,1)S(1)}, bf16[4,64,1024]{2,1,0:T(8,128)(2,1)S(1)}, u32[]{:S(2)}, u32[]{:S(2)}) %collective-permute-start.7) | collective-permute-done | bytes 524320 | tf_op jit(solution)/shard_map/cond/branch_1_fun/ppermute | solution.py:108
  136.6 1.0 copy-done.3
  137.7 0.7 slice.152
  138.5 5.2 %collective-permute-start.12 = (bf16[2,4,16,1024]{3,2,1,0:T(8,128)(2,1)}, bf16[2,4,16,1024]{3,2,1,0:T(8,128)(2,1)S(1)}, u32[]{:S(2)}, u32[]{:S(2)}) collective-permute-start(bf16[2,4,16,1024]{3,2,1,0:T(8,128)(2,1)} %slice.152), channel_id=1, source_target_pairs={{0,2},{1,3},{2,0},{3,1},{4,6},{5,7},{6,4},{7,5},{8,10},{9,11},{10,... | collective-permute-start | bytes 786440 | tf_op jit(solution)/shard_map/ppermute | solution.py:108
  143.7 3.2 %shard_map.68 = bf16[2,3,768,1024]{3,2,1,0:T(8,128)(2,1)} custom-call(s32[1]{0:T(128)} %bitcast.15.me, bf16[16,3,96,1024]{3,2,1,0:T(8,128)(2,1)} %rows_ref.9, s32[16,3,32,96]{3,2,1,0:T(8,128)S(1)} %bitcast.44), custom_call_target="tpu_custom_call" | custom-call | flops 11796480 | bytes 2359296 | tf_op jit(solution)/shard_map/pallas_call | solution.py:53
  146.9 1.1 constant_dynamic-update-slice_fusion.6
  148.0 2.2 collective-permute-done.12
  150.3 4.0 %collective-permute-start.15 = (bf16[1,4,16,1024]{3,2,1,0:T(8,128)(2,1)S(1)}, bf16[1,4,16,1024]{3,2,1,0:T(8,128)(2,1)S(1)}, u32[]{:S(2)}, u32[]{:S(2)}) collective-permute-start(bf16[1,4,16,1024]{3,2,1,0:T(8,128)(2,1)S(1)} %slice.153), channel_id=1, source_target_pairs={{0,4},{1,5},{2,6},{3,7},{4,0},{5,1},{6,2},{7,3},{8,12},{9,13},{10,... | collective-permute-start | bytes 393224 | tf_op jit(solution)/shard_map/ppermute | solution.py:108
  154.2 1.5 collective-permute-start.17
  156.3 2.4 %constant_dynamic-update-slice_fusion.5 = bf16[6,768,1024]{2,1,0:T(8,128)(2,1)} fusion(bf16[6,768,1024]{2,1,0:T(8,128)(2,1)} %constant_dynamic-update-slice_fusion.6, bf16[6,96,1024]{2,1,0:T(8,128)(2,1)} %collective-permute-done.13, s32[]{:T(128)S(6)} %select_n.75), kind=kLoop, calls=%fused_computation.59 | loop fusion | bytes 2359300 | tf_op jit(solution)/shard_map/dynamic_update_slice | solution.py:104
  158.8 16.5 %collective-permute-done.15 = bf16[1,4,16,1024]{3,2,1,0:T(8,128)(2,1)S(1)} collective-permute-done((bf16[1,4,16,1024]{3,2,1,0:T(8,128)(2,1)S(1)}, bf16[1,4,16,1024]{3,2,1,0:T(8,128)(2,1)S(1)}, u32[]{:S(2)}, u32[]{:S(2)}) %collective-permute-start.15) | collective-permute-done | bytes 131104 | tf_op jit(solution)/shard_map/ppermute | solution.py:108
  175.4 2.4 %constant_dynamic-update-slice_fusion.4 = bf16[6,768,1024]{2,1,0:T(8,128)(2,1)} fusion(bf16[6,768,1024]{2,1,0:T(8,128)(2,1)} %constant_dynamic-update-slice_fusion.5, bf16[6,96,1024]{2,1,0:T(8,128)(2,1)} %collective-permute-done.14, s32[]{:T(128)S(6)} %select_n.76), kind=kLoop, calls=%fused_computation.58 | loop fusion | bytes 2359300 | tf_op jit(solution)/shard_map/dynamic_update_slice | solution.py:104
  177.9 1.6 collective-permute-start.21
  179.4 2.4 %constant_dynamic-update-slice_fusion.3 = bf16[6,768,1024]{2,1,0:T(8,128)(2,1)} fusion(bf16[6,768,1024]{2,1,0:T(8,128)(2,1)} %constant_dynamic-update-slice_fusion.4, bf16[6,96,1024]{2,1,0:T(8,128)(2,1)} %collective-permute-done.16, s32[]{:T(128)S(6)} %select_n.77), kind=kLoop, calls=%fused_computation.57 | loop fusion | bytes 2359300 | tf_op jit(solution)/shard_map/dynamic_update_slice | solution.py:104
  181.9 0.5 collective-permute-done.21
  182.4 0.7 pad_maximum_fusion.9
  183.1 5.8 %collective-permute-done.17 = bf16[6,96,1024]{2,1,0:T(8,128)(2,1)S(1)} collective-permute-done((bf16[6,96,1024]{2,1,0:T(8,128)(2,1)S(1)}, bf16[6,96,1024]{2,1,0:T(8,128)(2,1)S(1)}, u32[]{:S(2)}, u32[]{:S(2)}) %collective-permute-start.17) | collective-permute-done | bytes 1179680 | tf_op jit(solution)/shard_map/ppermute | solution.py:108
  188.9 1.1 constant_dynamic-update-slice_fusion.2
  190.0 18.3 %collective-permute-done.18 = bf16[6,96,1024]{2,1,0:T(8,128)(2,1)S(1)} collective-permute-done((bf16[6,96,1024]{2,1,0:T(8,128)(2,1)S(1)}, bf16[6,96,1024]{2,1,0:T(8,128)(2,1)S(1)}, u32[]{:S(2)}, u32[]{:S(2)}) %collective-permute-start.18) | collective-permute-done | bytes 1179680 | tf_op jit(solution)/shard_map/ppermute | solution.py:108
  208.3 1.1 constant_dynamic-update-slice_fusion.1
  209.5 16.4 %collective-permute-done.19 = bf16[6,96,1024]{2,1,0:T(8,128)(2,1)S(1)} collective-permute-done((bf16[6,96,1024]{2,1,0:T(8,128)(2,1)S(1)}, bf16[6,96,1024]{2,1,0:T(8,128)(2,1)S(1)}, u32[]{:S(2)}, u32[]{:S(2)}) %collective-permute-start.19) | collective-permute-done | bytes 1179680 | tf_op jit(solution)/shard_map/ppermute | solution.py:108
  225.9 1.1 constant_dynamic-update-slice_fusion
  (71 shorter events, 3.4 us)
Async XLA Ops:
  0.6 3.3 %copy-start.8 = (bf16[16,4096]{1,0:T(8,128)(2,1)S(1)}, bf16[16,4096]{1,0:T(8,128)(2,1)}, u32[]{:S(2)}) copy-start(bf16[16,4096]{1,0:T(8,128)(2,1)} %param.7) | copy-start | bytes 393220
  0.6 5.9 %copy-start.9 = (f32[16,8]{0,1:T(8,128)S(1)}, f32[16,8]{0,1:T(8,128)}, u32[]{:S(2)}) copy-start(f32[16,8]{0,1:T(8,128)} %param.11) | copy-start | bytes 1540
  0.7 6.0 %copy-start.10 = (s32[16,8]{0,1:T(8,128)S(1)}, s32[16,8]{0,1:T(8,128)}, u32[]{:S(2)}) copy-start(s32[16,8]{0,1:T(8,128)} %param.10) | copy-start | bytes 1540
  0.7 6.6 %copy-start = (s32[16,3,96,32]{2,3,1,0:T(8,128)S(1)}, s32[16,3,96,32]{2,3,1,0:T(8,128)}, u32[]{:S(2)}) copy-start(s32[16,3,96,32]{2,3,1,0:T(8,128)} %param.9) | copy-start | bytes 1769476
  3.9 8.2 %collective-permute-start.8 = (bf16[16,4096]{1,0:T(8,128)(2,1)S(1)}, bf16[16,4096]{1,0:T(8,128)(2,1)S(1)}, u32[]{:S(2)}, u32[]{:S(2)}) collective-permute-start(bf16[16,4096]{1,0:T(8,128)(2,1)S(1)} %copy-done.8), channel_id=1, source_target_pairs={{0,4},{1,5},{2,6},{3,7},{4,0},{5,1},{6,2},{7,3},{8,12},{9,13},{10,... | collective-permute-start | bytes 393224 | tf_op jit(solution)/shard_map/ppermute | solution.py:108
  6.9 5.3 %collective-permute-start.9 = (bf16[16,128]{1,0:T(8,128)(2,1)S(1)}, bf16[16,128]{1,0:T(8,128)(2,1)S(1)}, u32[]{:S(2)}, u32[]{:S(2)}) collective-permute-start(bf16[16,128]{1,0:T(8,128)(2,1)S(1)} %fusion.8), channel_id=1, source_target_pairs={{0,4},{1,5},{2,6},{3,7},{4,0},{5,1},{6,2},{7,3},{8,12},{9,13},{10,... | collective-permute-start | bytes 12296 | tf_op jit(solution)/shard_map/ppermute | solution.py:108
  12.2 11.7 %collective-permute-start.10 = (bf16[32,4224]{1,0:T(8,128)(2,1)S(1)}, bf16[32,4224]{1,0:T(8,128)(2,1)S(1)}, u32[]{:S(2)}, u32[]{:S(2)}) collective-permute-start(bf16[32,4224]{1,0:T(8,128)(2,1)S(1)} %maximum_maximum_fusion), channel_id=1, source_target_pairs={{0,2},{1,3},{2,0},{3,1},{4,6},{5,7},{6,4},{7,5},{8,10},{9,11},{10,... | collective-permute-start | bytes 811016 | tf_op jit(solution)/shard_map/ppermute | solution.py:108
  13.5 123.1 %collective-permute-start.11 = (bf16[6,96,1024]{2,1,0:T(8,128)(2,1)}, bf16[6,96,1024]{2,1,0:T(8,128)(2,1)S(1)}, u32[]{:S(2)}, u32[]{:S(2)}) collective-permute-start(bf16[6,96,1024]{2,1,0:T(8,128)(2,1)} %bitcast.59), channel_id=1, source_target_pairs={{0,5},{1,4},{2,7},{3,6},{4,1},{5,0},{6,3},{7,2},{8,13},{9,12},{10,... | collective-permute-start | bytes 3538952 | tf_op jit(solution)/shard_map/ppermute | solution.py:108
  22.8 127.4 %collective-permute-start.13 = (bf16[6,96,1024]{2,1,0:T(8,128)(2,1)}, bf16[6,96,1024]{2,1,0:T(8,128)(2,1)}, u32[]{:S(2)}, u32[]{:S(2)}) collective-permute-start(bf16[6,96,1024]{2,1,0:T(8,128)(2,1)} %bitcast.57), channel_id=1, source_target_pairs={{0,4},{1,5},{2,6},{3,7},{4,0},{5,1},{6,2},{7,3},{8,12},{9,13},{10,... | collective-permute-start | bytes 3538952 | tf_op jit(solution)/shard_map/ppermute | solution.py:108
  23.9 126.3 %collective-permute-start.14 = (bf16[6,96,1024]{2,1,0:T(8,128)(2,1)}, bf16[6,96,1024]{2,1,0:T(8,128)(2,1)}, u32[]{:S(2)}, u32[]{:S(2)}) collective-permute-start(bf16[6,96,1024]{2,1,0:T(8,128)(2,1)} %bitcast.58), channel_id=1, source_target_pairs={{0,3},{1,2},{2,1},{3,0},{4,7},{5,6},{6,5},{7,4},{8,11},{9,10},{10,... | collective-permute-start | bytes 3538952 | tf_op jit(solution)/shard_map/ppermute | solution.py:108
  27.3 148.0 %collective-permute-start.16 = (bf16[6,96,1024]{2,1,0:T(8,128)(2,1)}, bf16[6,96,1024]{2,1,0:T(8,128)(2,1)}, u32[]{:S(2)}, u32[]{:S(2)}) collective-permute-start(bf16[6,96,1024]{2,1,0:T(8,128)(2,1)} %bitcast.56), channel_id=1, source_target_pairs={{0,6},{1,7},{2,4},{3,5},{4,2},{5,3},{6,0},{7,1},{8,14},{9,15},{10,... | collective-permute-start | bytes 3538952 | tf_op jit(solution)/shard_map/ppermute | solution.py:108
  30.7 6.9 %collective-permute-start = (bf16[64,2048]{1,0:T(8,128)(2,1)S(1)}, bf16[64,2048]{1,0:T(8,128)(2,1)S(1)}, u32[]{:S(2)}, u32[]{:S(2)}) collective-permute-start(bf16[64,2048]{1,0:T(8,128)(2,1)S(1)} %get-tuple-element.83), channel_id=1, source_target_pairs={{0,16},{8,24},{16,0},{24,8},{1,17},{9,25},{17,1},{25,9},{2,18},{10... | collective-permute-start | bytes 786440 | tf_op jit(solution)/shard_map/cond/branch_1_fun/ppermute | solution.py:108
  37.7 2.4 %collective-permute-start.1 = (bf16[128,1024]{1,0:T(8,128)(2,1)S(1)}, bf16[128,1024]{1,0:T(8,128)(2,1)S(1)}, u32[]{:S(2)}, u32[]{:S(2)}) collective-permute-start(bf16[128,1024]{1,0:T(8,128)(2,1)S(1)} %get-tuple-element.85), channel_id=1, source_target_pairs={{0,8},{8,0},{16,24},{24,16},{1,9},{9,1},{17,25},{25,17},{2,10},{10... | collective-permute-start | bytes 786440 | tf_op jit(solution)/shard_map/cond/branch_1_fun/ppermute | solution.py:108
  40.9 19.4 %collective-permute-start.2 = (bf16[264,1024]{1,0:T(8,128)(2,1)}, bf16[264,1024]{1,0:T(8,128)(2,1)}, u32[]{:S(2)}, u32[]{:S(2)}) collective-permute-start(bf16[264,1024]{1,0:T(8,128)(2,1)} %pad_maximum_fusion.3), channel_id=1, source_target_pairs={{0,1},{1,0},{2,3},{3,2},{4,5},{5,4},{6,7},{7,6},{8,9},{9,8},{10,11... | collective-permute-start | bytes 1622024 | tf_op jit(solution)/shard_map/cond/branch_1_fun/ppermute | solution.py:108
  69.6 3.5 %collective-permute-start.3 = (bf16[256,3072]{1,0:T(8,128)(2,1)S(1)}, bf16[256,3072]{1,0:T(8,128)(2,1)S(1)}, u32[]{:S(2)}, u32[]{:S(2)}) collective-permute-start(bf16[256,3072]{1,0:T(8,128)(2,1)S(1)} %slice.69), channel_id=1, source_target_pairs={{0,8},{8,0},{16,24},{24,16},{1,9},{9,1},{17,25},{25,17},{2,10},{10... | collective-permute-start | bytes 4718600 | tf_op jit(solution)/shard_map/cond/branch_1_fun/ppermute | solution.py:108
  73.6 1.7 copy-start.1
  76.3 13.8 %slice-start = ((bf16[128,128]{0,1:T(8,128)(2,1)}), bf16[128,48]{0,1:T(8,128)(2,1)S(1)}, s32[]{:S(2)}) async-start(bf16[128,128]{0,1:T(8,128)(2,1)} %pad_maximum_fusion.6), calls=%async_computation | async-start | bytes 24576 | tf_op jit(solution)/shard_map/cond/branch_1_fun/slice | solution.py:207
  76.3 19.9 %collective-permute-start.4 = (bf16[128,3072]{1,0:T(8,128)(2,1)}, bf16[128,3072]{1,0:T(8,128)(2,1)}, u32[]{:S(2)}, u32[]{:S(2)}) collective-permute-start(bf16[128,3072]{1,0:T(8,128)(2,1)} %slice.150), channel_id=1, source_target_pairs={{0,16},{8,24},{16,0},{24,8},{1,17},{9,25},{17,1},{25,9},{2,18},{10... | collective-permute-start | bytes 2359304 | tf_op jit(solution)/shard_map/cond/branch_1_fun/ppermute | solution.py:108
  98.2 10.4 %collective-permute-start.5 = (bf16[128,1536]{1,0:T(8,128)(2,1)S(1)}, bf16[128,1536]{1,0:T(8,128)(2,1)S(1)}, u32[]{:S(2)}, u32[]{:S(2)}) collective-permute-start(bf16[128,1536]{1,0:T(8,128)(2,1)S(1)} %multiply_convert_fusion), channel_id=1, source_target_pairs={{0,16},{8,24},{16,0},{24,8},{1,17},{9,25},{17,1},{25,9},{2,18},{10... | collective-permute-start | bytes 1179656 | tf_op jit(solution)/shard_map/cond/branch_1_fun/ppermute | solution.py:108
  108.7 9.4 %collective-permute-start.6 = (bf16[256,1536]{1,0:T(8,128)(2,1)S(1)}, bf16[256,1536]{1,0:T(8,128)(2,1)}, u32[]{:S(2)}, u32[]{:S(2)}) collective-permute-start(bf16[256,1536]{1,0:T(8,128)(2,1)S(1)} %pad_maximum_fusion.2), channel_id=1, source_target_pairs={{0,8},{8,0},{16,24},{24,16},{1,9},{9,1},{17,25},{25,17},{2,10},{10... | collective-permute-start | bytes 2359304 | tf_op jit(solution)/shard_map/cond/branch_1_fun/ppermute | solution.py:108
  118.1 2.1 copy-start.2
  122.1 14.4 %collective-permute-start.7 = (bf16[4,64,1024]{2,1,0:T(8,128)(2,1)S(1)}, bf16[4,64,1024]{2,1,0:T(8,128)(2,1)S(1)}, u32[]{:S(2)}, u32[]{:S(2)}) collective-permute-start(bf16[4,64,1024]{2,1,0:T(8,128)(2,1)S(1)} %slice.151), channel_id=1, source_target_pairs={{0,1},{1,0},{2,3},{3,2},{4,5},{5,4},{6,7},{7,6},{8,9},{9,8},{10,11... | collective-permute-start | bytes 1572872 | tf_op jit(solution)/shard_map/cond/branch_1_fun/ppermute | solution.py:108
  136.6 1.0 copy-start.3
  138.5 11.7 %collective-permute-start.12 = (bf16[2,4,16,1024]{3,2,1,0:T(8,128)(2,1)}, bf16[2,4,16,1024]{3,2,1,0:T(8,128)(2,1)S(1)}, u32[]{:S(2)}, u32[]{:S(2)}) collective-permute-start(bf16[2,4,16,1024]{3,2,1,0:T(8,128)(2,1)} %slice.152), channel_id=1, source_target_pairs={{0,2},{1,3},{2,0},{3,1},{4,6},{5,7},{6,4},{7,5},{8,10},{9,11},{10,... | collective-permute-start | bytes 786440 | tf_op jit(solution)/shard_map/ppermute | solution.py:108
  143.7 3.2 %copy-start.4 = (bf16[6,96,1024]{2,1,0:T(8,128)(2,1)S(1)}, bf16[6,96,1024]{2,1,0:T(8,128)(2,1)}, u32[]{:S(2)}) copy-start(bf16[6,96,1024]{2,1,0:T(8,128)(2,1)} %copy-done.3) | copy-start | bytes 3538948
  146.9 7.4 %copy-start.6 = (bf16[6,96,1024]{2,1,0:T(8,128)(2,1)S(1)}, bf16[6,96,1024]{2,1,0:T(8,128)(2,1)}, u32[]{:S(2)}) copy-start(bf16[6,96,1024]{2,1,0:T(8,128)(2,1)} %get-tuple-element.74) | copy-start | bytes 3538948
  146.9 8.9 %copy-start.7 = (bf16[6,96,1024]{2,1,0:T(8,128)(2,1)S(1)}, bf16[6,96,1024]{2,1,0:T(8,128)(2,1)}, u32[]{:S(2)}) copy-start(bf16[6,96,1024]{2,1,0:T(8,128)(2,1)} %get-tuple-element.75) | copy-start | bytes 3538948
  146.9 9.2 %copy-start.5 = (bf16[6,96,1024]{2,1,0:T(8,128)(2,1)S(1)}, bf16[6,96,1024]{2,1,0:T(8,128)(2,1)}, u32[]{:S(2)}) copy-start(bf16[6,96,1024]{2,1,0:T(8,128)(2,1)} %get-tuple-element.76) | copy-start | bytes 3538948
  150.3 25.0 %collective-permute-start.15 = (bf16[1,4,16,1024]{3,2,1,0:T(8,128)(2,1)S(1)}, bf16[1,4,16,1024]{3,2,1,0:T(8,128)(2,1)S(1)}, u32[]{:S(2)}, u32[]{:S(2)}) collective-permute-start(bf16[1,4,16,1024]{3,2,1,0:T(8,128)(2,1)S(1)} %slice.153), channel_id=1, source_target_pairs={{0,4},{1,5},{2,6},{3,7},{4,0},{5,1},{6,2},{7,3},{8,12},{9,13},{10,... | collective-permute-start | bytes 393224 | tf_op jit(solution)/shard_map/ppermute | solution.py:108
  154.2 34.7 %collective-permute-start.17 = (bf16[6,96,1024]{2,1,0:T(8,128)(2,1)S(1)}, bf16[6,96,1024]{2,1,0:T(8,128)(2,1)S(1)}, u32[]{:S(2)}, u32[]{:S(2)}) collective-permute-start(bf16[6,96,1024]{2,1,0:T(8,128)(2,1)S(1)} %copy-done.6), channel_id=1, source_target_pairs={{0,1},{1,0},{2,3},{3,2},{4,5},{5,4},{6,7},{7,6},{8,9},{9,8},{10,11... | collective-permute-start | bytes 3538952 | tf_op jit(solution)/shard_map/ppermute | solution.py:108
  155.8 52.6 %collective-permute-start.18 = (bf16[6,96,1024]{2,1,0:T(8,128)(2,1)S(1)}, bf16[6,96,1024]{2,1,0:T(8,128)(2,1)S(1)}, u32[]{:S(2)}, u32[]{:S(2)}) collective-permute-start(bf16[6,96,1024]{2,1,0:T(8,128)(2,1)S(1)} %copy-done.7), channel_id=1, source_target_pairs={{0,2},{1,3},{2,0},{3,1},{4,6},{5,7},{6,4},{7,5},{8,10},{9,11},{10,... | collective-permute-start | bytes 3538952 | tf_op jit(solution)/shard_map/ppermute | solution.py:108
  156.0 69.8 %collective-permute-start.19 = (bf16[6,96,1024]{2,1,0:T(8,128)(2,1)S(1)}, bf16[6,96,1024]{2,1,0:T(8,128)(2,1)S(1)}, u32[]{:S(2)}, u32[]{:S(2)}) collective-permute-start(bf16[6,96,1024]{2,1,0:T(8,128)(2,1)S(1)} %copy-done.5), channel_id=1, source_target_pairs={{0,7},{1,6},{2,5},{3,4},{4,3},{5,2},{6,1},{7,0},{8,15},{9,14},{10,... | collective-permute-start | bytes 3538952 | tf_op jit(solution)/shard_map/ppermute | solution.py:108
  175.3 2.5 %collective-permute-start.20 = (bf16[32,1024]{1,0:T(8,128)(2,1)S(1)}, bf16[32,1024]{1,0:T(8,128)(2,1)S(1)}, u32[]{:S(2)}, u32[]{:S(2)}) collective-permute-start(bf16[32,1024]{1,0:T(8,128)(2,1)S(1)} %bitcast.67), channel_id=1, source_target_pairs={{0,8},{8,0},{16,24},{24,16},{1,9},{9,1},{17,25},{25,17},{2,10},{10... | collective-permute-start | bytes 196616 | tf_op jit(solution)/shard_map/ppermute | solution.py:108
  177.9 4.6 %collective-permute-start.21 = (bf16[16,2048]{1,0:T(8,128)(2,1)S(1)}, bf16[16,2048]{1,0:T(8,128)(2,1)S(1)}, u32[]{:S(2)}, u32[]{:S(2)}) collective-permute-start(bf16[16,2048]{1,0:T(8,128)(2,1)S(1)} %fusion.1), channel_id=1, source_target_pairs={{0,16},{8,24},{16,0},{24,8},{1,17},{9,25},{17,1},{25,9},{2,18},{10... | collective-permute-start | bytes 196616 | tf_op jit(solution)/shard_map/ppermute | solution.py:108

commit v5 on v4

--- a/solution.py
+++ b/solution.py
@@ -258,9 +258,9 @@
         for key in keys:
             arrived[key] = swap(sent[key], "expert", key)
 
-    table = gather(share_table(expert_ids, route_probs, experts), "expert", z_bits[:1])
-    held = after(tokens, first, sent)
-    held = gather(held, "expert", z_bits[:1])
+    table = after(share_table(expert_ids, route_probs, experts), first, sent)
+    table = gather(table, "expert", z_bits[:1])
+    held = gather(tokens, "expert", z_bits[:1])
     held = after(held, second, sent)
     held = jnp.concatenate([held, table], axis=1)
     held = gather(held, "expert", z_bits[1:])

time: 228 us -> 227 us (level)
  transfers between devices with their start and end apart: 22 -> 22, of which waited for: 14 -> 13; matrix products, arithmetic and copies ran while one was open for 15% -> 16% of each run, Pallas kernels for 22% -> 23%
where the time goes in v5:
time: 227 us; the launch traced here: 226 us
  waiting for transfers between devices  101 us (44%)
  Pallas kernels  52 us (23%)
  starting transfers between devices  30.3 us (13%)
  local copies, waits for them, and re-layouts  23.8 us (10%)
  other arithmetic  8.4 us (4%)
  matrix products  8.27 us (4%)
    ppermute x22, waiting for transfers between devices, swap(): lax.ppermute(value, axis, [(i, i ^ bit) for i in range(lax.axis_size(axis...  101 us
    ppermute x22, starting transfers between devices, swap(): lax.ppermute(value, axis, [(i, i ^ bit) for i in range(lax.axis_size(axis...  30.3 us
    pallas_call x2, Pallas kernels, dequantize(): pl.pallas_call(functools.partial(weights_kernel, first), out_shape=jax.Sh...  26.9 us
    pallas_call x8, Pallas kernels, encode(): pl.pallas_call(encode_kernel, out_shape=jax.ShapeDtypeStruct((per_owner,...  25.1 us
    dynamic_update_slice x7, local copies, waits for them, and re-layouts, place(): lax.dynamic_update_slice(elements, block, (0, (me[0] ^ partner) * block.s...  11.8 us
    dot_general x1, matrix products, layer(): lax.dot_general(held.reshape(groups * slots, width), pair.reshape(-1, wid...  6.48 us
  transfers between devices with their start and end apart: 22, of which 13 were waited for; matrix products, arithmetic and copies ran while one was open for 16% of the time, Pallas kernels for 23%

profile of v5, /device:TPU:8, one launch (start us, length us, event | category | flops | bytes accessed | tf_op | source)
XLA Modules:
  0.0 225.9 jit_solution(4580074297806623713)
XLA Ops:
  0.6 2.7 %collective-permute-start.8 = (bf16[16,4096]{1,0:T(8,128)(2,1)}, bf16[16,4096]{1,0:T(8,128)(2,1)S(1)}, u32[]{:S(2)}, u32[]{:S(2)}) collective-permute-start(bf16[16,4096]{1,0:T(8,128)(2,1)} %param.7), channel_id=1, source_target_pairs={{0,4},{1,5},{2,6},{3,7},{4,0},{5,1},{6,2},{7,3},{8,12},{9,13},{10,... | collective-permute-start | bytes 393224 | tf_op jit(solution)/shard_map/ppermute | solution.py:108
  3.3 0.7 reduce_sum.27
  4.0 0.7 broadcast_divide_fusion
  4.8 0.8 copy.42
  5.7 3.2 %shard_map.70 = bf16[2,3,96,1024]{3,2,1,0:T(8,128)(2,1)} custom-call(s32[1]{0:T(128)} %bitcast.15.me, bf16[16,3,96,1024]{3,2,1,0:T(8,128)(2,1)} %rows_ref.9, s32[16,3,32,96]{3,2,1,0:T(8,128)} %bitcast.38), custom_call_target="tpu_custom_call" | custom-call | flops 11796480 | bytes 2359296 | tf_op jit(solution)/shard_map/pallas_call | solution.py:53
  9.3 3.1 %shard_map.69 = bf16[2,3,96,1024]{3,2,1,0:T(8,128)(2,1)} custom-call(s32[1]{0:T(128)} %bitcast.15.me, bf16[16,3,96,1024]{3,2,1,0:T(8,128)(2,1)} %rows_ref.9, s32[16,3,32,96]{3,2,1,0:T(8,128)S(1)} %bitcast.39), custom_call_target="tpu_custom_call" | custom-call | flops 11796480 | bytes 2359296 | tf_op jit(solution)/shard_map/pallas_call | solution.py:53
  12.5 1.0 collective-permute-done.9
  14.0 2.5 %collective-permute-start.11 = (bf16[6,96,1024]{2,1,0:T(8,128)(2,1)}, bf16[6,96,1024]{2,1,0:T(8,128)(2,1)S(1)}, u32[]{:S(2)}, u32[]{:S(2)}) collective-permute-start(bf16[6,96,1024]{2,1,0:T(8,128)(2,1)} %bitcast.59), channel_id=1, source_target_pairs={{0,5},{1,4},{2,7},{3,6},{4,1},{5,0},{6,3},{7,2},{8,13},{9,12},{10,... | collective-permute-start | bytes 3538952 | tf_op jit(solution)/shard_map/ppermute | solution.py:108
  16.5 3.1 %shard_map.71 = bf16[2,3,96,1024]{3,2,1,0:T(8,128)(2,1)} custom-call(s32[1]{0:T(128)} %bitcast.15.me, bf16[16,3,96,1024]{3,2,1,0:T(8,128)(2,1)} %rows_ref.9, s32[16,3,32,96]{3,2,1,0:T(8,128)S(1)} %bitcast.40), custom_call_target="tpu_custom_call" | custom-call | flops 11796480 | bytes 2359296 | tf_op jit(solution)/shard_map/pallas_call | solution.py:53
  19.6 3.1 %shard_map.72 = bf16[2,3,96,1024]{3,2,1,0:T(8,128)(2,1)} custom-call(s32[1]{0:T(128)} %bitcast.15.me, bf16[16,3,96,1024]{3,2,1,0:T(8,128)(2,1)} %rows_ref.9, s32[16,3,32,96]{3,2,1,0:T(8,128)S(1)} %bitcast.41), custom_call_target="tpu_custom_call" | custom-call | flops 11796480 | bytes 2359296 | tf_op jit(solution)/shard_map/pallas_call | solution.py:53
  22.8 1.3 collective-permute-start.13
  24.1 3.1 %collective-permute-start.14 = (bf16[6,96,1024]{2,1,0:T(8,128)(2,1)}, bf16[6,96,1024]{2,1,0:T(8,128)(2,1)}, u32[]{:S(2)}, u32[]{:S(2)}) collective-permute-start(bf16[6,96,1024]{2,1,0:T(8,128)(2,1)} %bitcast.58), channel_id=1, source_target_pairs={{0,3},{1,2},{2,1},{3,0},{4,7},{5,6},{6,5},{7,4},{8,11},{9,10},{10,... | collective-permute-start | bytes 3538952 | tf_op jit(solution)/shard_map/ppermute | solution.py:108
  27.2 1.9 collective-permute-start.16
  29.1 1.2 slice.88
  31.0 104.6 %conditional.1 = (f32[4,64,1024]{2,1,0:T(8,128)S(1)}, bf16[6,96,1024]{2,1,0:T(8,128)(2,1)}, bf16[6,96,1024]{2,1,0:T(8,128)(2,1)}, bf16[6,96,1024]{2,1,0:T(8,128)(2,1)}) conditional(s32[]{:T(128)} %bitcast.18, (s32[1]{0:T(128)}, bf16[16,3,96,1024]{3,2,1,0:T(8,128)(2,1)}, s32[16,3,32,96]{3,2,1,0:T(8,128)S(1)}) %tuple.47, ...), branch_computations={%region_2.3_spmd, %region_3.5_spmd} | conditional | flops 5005043712 | bytes 126157312 | solution.py:279
  31.2 1.6 collective-permute-start
  32.8 4.9 %collective-permute-done = bf16[64,2048]{1,0:T(8,128)(2,1)S(1)} collective-permute-done((bf16[64,2048]{1,0:T(8,128)(2,1)S(1)}, bf16[64,2048]{1,0:T(8,128)(2,1)S(1)}, u32[]{:S(2)}, u32[]{:S(2)}) %collective-permute-start) | collective-permute-done | bytes 262176 | tf_op jit(solution)/shard_map/cond/branch_1_fun/ppermute | solution.py:108
  37.9 1.4 copy.44
  39.3 0.8 slice.101
  40.2 0.8 pad_maximum_fusion.3
  41.0 14.7 %branch_1_fun.5 = bf16[2,16,96,1024]{3,2,1,0:T(8,128)(2,1)} custom-call(bf16[16,3,96,1024]{3,2,1,0:T(8,128)(2,1)} %get-tuple-element.18.rows_ref, s32[16,3,32,96]{3,2,1,0:T(8,128)S(1)} %get-tuple-element.19.exponent_ref), custom_call_target="tpu_custom_call" | custom-call | flops 78643200 | bytes 12582912 | tf_op jit(solution)/shard_map/cond/branch_1_fun/pallas_call | solution.py:88
  55.7 3.5 %collective-permute-done.2 = bf16[264,1024]{1,0:T(8,128)(2,1)} collective-permute-done((bf16[264,1024]{1,0:T(8,128)(2,1)}, bf16[264,1024]{1,0:T(8,128)(2,1)}, u32[]{:S(2)}, u32[]{:S(2)}) %collective-permute-start.2) | collective-permute-done | bytes 540704 | tf_op jit(solution)/shard_map/cond/branch_1_fun/ppermute | solution.py:108
  59.2 0.7 slice.103
  60.1 0.7 pad_maximum_fusion.6
  60.8 1.1 slice.102
  62.0 6.5 %convolution_convert_fusion = bf16[512,3072]{1,0:T(8,128)(2,1)S(1)} fusion(bf16[512,1024]{1,0:T(8,128)(2,1)S(1)} %bitcast.66, bf16[3072,1024]{1,0:T(8,128)(2,1)} %bitcast.47), kind=kOutput, calls=%fused_computation | convolution fusion | flops 3222798336 | bytes 10485760 | tf_op jit(solution)/shard_map/cond/branch_1_fun/dot_general | solution.py:200
  68.7 3.3 %collective-permute-done.3 = bf16[256,3072]{1,0:T(8,128)(2,1)S(1)} collective-permute-done((bf16[256,3072]{1,0:T(8,128)(2,1)S(1)}, bf16[256,3072]{1,0:T(8,128)(2,1)S(1)}, u32[]{:S(2)}, u32[]{:S(2)}) %collective-permute-start.3) | collective-permute-done | bytes 1572896 | tf_op jit(solution)/shard_map/cond/branch_1_fun/ppermute | solution.py:108
  72.6 1.7 copy-done.1
  74.2 1.0 slice.150
  75.2 1.5 collective-permute-start.4
  76.8 12.2 %branch_1_fun.6 = bf16[1,16,96,1024]{3,2,1,0:T(8,128)(2,1)} custom-call(bf16[16,3,96,1024]{3,2,1,0:T(8,128)(2,1)} %get-tuple-element.18.rows_ref, s32[16,3,32,96]{3,2,1,0:T(8,128)S(1)} %get-tuple-element.19.exponent_ref), custom_call_target="tpu_custom_call" | custom-call | flops 39321600 | bytes 6291456 | tf_op jit(solution)/shard_map/cond/branch_1_fun/pallas_call | solution.py:88
  89.3 5.8 %collective-permute-done.4 = bf16[128,3072]{1,0:T(8,128)(2,1)} collective-permute-done((bf16[128,3072]{1,0:T(8,128)(2,1)}, bf16[128,3072]{1,0:T(8,128)(2,1)}, u32[]{:S(2)}, u32[]{:S(2)}) %collective-permute-start.4) | collective-permute-done | bytes 786464 | tf_op jit(solution)/shard_map/cond/branch_1_fun/ppermute | solution.py:108
  95.1 1.8 slice_add_fusion
  97.2 1.6 collective-permute-start.5
  98.8 8.8 %collective-permute-done.5 = bf16[128,1536]{1,0:T(8,128)(2,1)S(1)} collective-permute-done((bf16[128,1536]{1,0:T(8,128)(2,1)S(1)}, bf16[128,1536]{1,0:T(8,128)(2,1)S(1)}, u32[]{:S(2)}, u32[]{:S(2)}) %collective-permute-start.5) | collective-permute-done | bytes 393248 | tf_op jit(solution)/shard_map/cond/branch_1_fun/ppermute | solution.py:108
  107.7 3.1 %branch_1_fun.8 = bf16[2,3,96,1024]{3,2,1,0:T(8,128)(2,1)} custom-call(s32[1]{0:T(128)} %get-tuple-element.26.me, bf16[16,3,96,1024]{3,2,1,0:T(8,128)(2,1)} %get-tuple-element.18.rows_ref, s32[16,3,32,96]{3,2,1,0:T(8,128)S(1)} %get-tuple-element.19.exponent_ref), custom_call_target="tpu_custom_call" | custom-call | flops 11796480 | bytes 2359296 | tf_op jit(solution)/shard_map/cond/branch_1_fun/pallas_call | solution.py:53
  110.8 3.1 %branch_1_fun.9 = bf16[2,3,96,1024]{3,2,1,0:T(8,128)(2,1)} custom-call(s32[1]{0:T(128)} %get-tuple-element.26.me, bf16[16,3,96,1024]{3,2,1,0:T(8,128)(2,1)} %get-tuple-element.18.rows_ref, s32[16,3,32,96]{3,2,1,0:T(8,128)S(1)} %get-tuple-element.19.exponent_ref), custom_call_target="tpu_custom_call" | custom-call | flops 11796480 | bytes 2359296 | tf_op jit(solution)/shard_map/cond/branch_1_fun/pallas_call | solution.py:53
  113.9 3.1 %branch_1_fun.7 = bf16[2,3,96,1024]{3,2,1,0:T(8,128)(2,1)} custom-call(s32[1]{0:T(128)} %get-tuple-element.26.me, bf16[16,3,96,1024]{3,2,1,0:T(8,128)(2,1)} %get-tuple-element.18.rows_ref, s32[16,3,32,96]{3,2,1,0:T(8,128)S(1)} %get-tuple-element.19.exponent_ref), custom_call_target="tpu_custom_call" | custom-call | flops 11796480 | bytes 2359296 | tf_op jit(solution)/shard_map/cond/branch_1_fun/pallas_call | solution.py:53
  117.0 1.4 pad_maximum_fusion
  118.4 0.7 copy-done.2
  119.2 1.8 fusion.10
  121.0 0.6 collective-permute-start.7
  121.6 13.8 %collective-permute-done.7 = bf16[4,64,1024]{2,1,0:T(8,128)(2,1)S(1)} collective-permute-done((bf16[4,64,1024]{2,1,0:T(8,128)(2,1)S(1)}, bf16[4,64,1024]{2,1,0:T(8,128)(2,1)S(1)}, u32[]{:S(2)}, u32[]{:S(2)}) %collective-permute-start.7) | collective-permute-done | bytes 524320 | tf_op jit(solution)/shard_map/cond/branch_1_fun/ppermute | solution.py:108
  135.6 1.0 copy-done.3
  136.7 0.7 slice.152
  137.4 4.8 %collective-permute-start.12 = (bf16[2,4,16,1024]{3,2,1,0:T(8,128)(2,1)}, bf16[2,4,16,1024]{3,2,1,0:T(8,128)(2,1)S(1)}, u32[]{:S(2)}, u32[]{:S(2)}) collective-permute-start(bf16[2,4,16,1024]{3,2,1,0:T(8,128)(2,1)} %slice.152), channel_id=1, source_target_pairs={{0,2},{1,3},{2,0},{3,1},{4,6},{5,7},{6,4},{7,5},{8,10},{9,11},{10,... | collective-permute-start | bytes 786440 | tf_op jit(solution)/shard_map/ppermute | solution.py:108
  142.3 3.2 %shard_map.68 = bf16[2,3,768,1024]{3,2,1,0:T(8,128)(2,1)} custom-call(s32[1]{0:T(128)} %bitcast.15.me, bf16[16,3,96,1024]{3,2,1,0:T(8,128)(2,1)} %rows_ref.9, s32[16,3,32,96]{3,2,1,0:T(8,128)S(1)} %bitcast.44), custom_call_target="tpu_custom_call" | custom-call | flops 11796480 | bytes 2359296 | tf_op jit(solution)/shard_map/pallas_call | solution.py:53
  145.5 1.1 constant_dynamic-update-slice_fusion.6
  146.6 2.8 %collective-permute-done.12 = bf16[2,4,16,1024]{3,2,1,0:T(8,128)(2,1)S(1)} collective-permute-done((bf16[2,4,16,1024]{3,2,1,0:T(8,128)(2,1)}, bf16[2,4,16,1024]{3,2,1,0:T(8,128)(2,1)S(1)}, u32[]{:S(2)}, u32[]{:S(2)}) %collective-permute-start.12) | collective-permute-done | bytes 262176 | tf_op jit(solution)/shard_map/ppermute | solution.py:108
  149.6 3.8 %collective-permute-start.15 = (bf16[1,4,16,1024]{3,2,1,0:T(8,128)(2,1)S(1)}, bf16[1,4,16,1024]{3,2,1,0:T(8,128)(2,1)S(1)}, u32[]{:S(2)}, u32[]{:S(2)}) collective-permute-start(bf16[1,4,16,1024]{3,2,1,0:T(8,128)(2,1)S(1)} %slice.153), channel_id=1, source_target_pairs={{0,4},{1,5},{2,6},{3,7},{4,0},{5,1},{6,2},{7,3},{8,12},{9,13},{10,... | collective-permute-start | bytes 393224 | tf_op jit(solution)/shard_map/ppermute | solution.py:108
  153.3 1.5 collective-permute-start.17
  155.5 2.4 %constant_dynamic-update-slice_fusion.5 = bf16[6,768,1024]{2,1,0:T(8,128)(2,1)} fusion(bf16[6,768,1024]{2,1,0:T(8,128)(2,1)} %constant_dynamic-update-slice_fusion.6, bf16[6,96,1024]{2,1,0:T(8,128)(2,1)} %collective-permute-done.13, s32[]{:T(128)S(6)} %select_n.75), kind=kLoop, calls=%fused_computation.59 | loop fusion | bytes 2359300 | tf_op jit(solution)/shard_map/dynamic_update_slice | solution.py:104
  157.9 16.8 %collective-permute-done.15 = bf16[1,4,16,1024]{3,2,1,0:T(8,128)(2,1)S(1)} collective-permute-done((bf16[1,4,16,1024]{3,2,1,0:T(8,128)(2,1)S(1)}, bf16[1,4,16,1024]{3,2,1,0:T(8,128)(2,1)S(1)}, u32[]{:S(2)}, u32[]{:S(2)}) %collective-permute-start.15) | collective-permute-done | bytes 131104 | tf_op jit(solution)/shard_map/ppermute | solution.py:108
  174.8 2.4 %constant_dynamic-update-slice_fusion.4 = bf16[6,768,1024]{2,1,0:T(8,128)(2,1)} fusion(bf16[6,768,1024]{2,1,0:T(8,128)(2,1)} %constant_dynamic-update-slice_fusion.5, bf16[6,96,1024]{2,1,0:T(8,128)(2,1)} %collective-permute-done.14, s32[]{:T(128)S(6)} %select_n.76), kind=kLoop, calls=%fused_computation.58 | loop fusion | bytes 2359300 | tf_op jit(solution)/shard_map/dynamic_update_slice | solution.py:104
  177.3 1.6 collective-permute-start.21
  178.9 2.4 %constant_dynamic-update-slice_fusion.3 = bf16[6,768,1024]{2,1,0:T(8,128)(2,1)} fusion(bf16[6,768,1024]{2,1,0:T(8,128)(2,1)} %constant_dynamic-update-slice_fusion.4, bf16[6,96,1024]{2,1,0:T(8,128)(2,1)} %collective-permute-done.16, s32[]{:T(128)S(6)} %select_n.77), kind=kLoop, calls=%fused_computation.57 | loop fusion | bytes 2359300 | tf_op jit(solution)/shard_map/dynamic_update_slice | solution.py:104
  181.3 0.5 collective-permute-done.21
  181.9 0.7 pad_maximum_fusion.9
  182.5 6.0 %collective-permute-done.17 = bf16[6,96,1024]{2,1,0:T(8,128)(2,1)S(1)} collective-permute-done((bf16[6,96,1024]{2,1,0:T(8,128)(2,1)S(1)}, bf16[6,96,1024]{2,1,0:T(8,128)(2,1)S(1)}, u32[]{:S(2)}, u32[]{:S(2)}) %collective-permute-start.17) | collective-permute-done | bytes 1179680 | tf_op jit(solution)/shard_map/ppermute | solution.py:108
  188.5 1.1 constant_dynamic-update-slice_fusion.2
  189.6 17.8 %collective-permute-done.18 = bf16[6,96,1024]{2,1,0:T(8,128)(2,1)S(1)} collective-permute-done((bf16[6,96,1024]{2,1,0:T(8,128)(2,1)S(1)}, bf16[6,96,1024]{2,1,0:T(8,128)(2,1)S(1)}, u32[]{:S(2)}, u32[]{:S(2)}) %collective-permute-start.18) | collective-permute-done | bytes 1179680 | tf_op jit(solution)/shard_map/ppermute | solution.py:108
  207.4 1.1 constant_dynamic-update-slice_fusion.1
  208.6 16.2 %collective-permute-done.19 = bf16[6,96,1024]{2,1,0:T(8,128)(2,1)S(1)} collective-permute-done((bf16[6,96,1024]{2,1,0:T(8,128)(2,1)S(1)}, bf16[6,96,1024]{2,1,0:T(8,128)(2,1)S(1)}, u32[]{:S(2)}, u32[]{:S(2)}) %collective-permute-start.19) | collective-permute-done | bytes 1179680 | tf_op jit(solution)/shard_map/ppermute | solution.py:108
  224.8 1.1 constant_dynamic-update-slice_fusion
  (67 shorter events, 4.4 us)
Async XLA Ops:
  0.6 11.8 %collective-permute-start.8 = (bf16[16,4096]{1,0:T(8,128)(2,1)}, bf16[16,4096]{1,0:T(8,128)(2,1)S(1)}, u32[]{:S(2)}, u32[]{:S(2)}) collective-permute-start(bf16[16,4096]{1,0:T(8,128)(2,1)} %param.7), channel_id=1, source_target_pairs={{0,4},{1,5},{2,6},{3,7},{4,0},{5,1},{6,2},{7,3},{8,12},{9,13},{10,... | collective-permute-start | bytes 393224 | tf_op jit(solution)/shard_map/ppermute | solution.py:108
  5.6 3.6 %copy-start = (s32[16,3,96,32]{2,3,1,0:T(8,128)S(1)}, s32[16,3,96,32]{2,3,1,0:T(8,128)}, u32[]{:S(2)}) copy-start(s32[16,3,96,32]{2,3,1,0:T(8,128)} %param.9) | copy-start | bytes 1769476
  8.9 3.5 %copy-start.8 = (bf16[16,4096]{1,0:T(8,128)(2,1)S(1)}, bf16[16,4096]{1,0:T(8,128)(2,1)}, u32[]{:S(2)}) copy-start(bf16[16,4096]{1,0:T(8,128)(2,1)} %param.7) | copy-start | bytes 393220
  8.9 4.5 %collective-permute-start.9 = (bf16[16,128]{1,0:T(8,128)(2,1)S(1)}, bf16[16,128]{1,0:T(8,128)(2,1)S(1)}, u32[]{:S(2)}, u32[]{:S(2)}) collective-permute-start(bf16[16,128]{1,0:T(8,128)(2,1)S(1)} %fusion.8), channel_id=1, source_target_pairs={{0,4},{1,5},{2,6},{3,7},{4,0},{5,1},{6,2},{7,3},{8,12},{9,13},{10,... | collective-permute-start | bytes 12296 | tf_op jit(solution)/shard_map/ppermute | solution.py:108
  13.5 10.6 %collective-permute-start.10 = (bf16[32,4224]{1,0:T(8,128)(2,1)S(1)}, bf16[32,4224]{1,0:T(8,128)(2,1)S(1)}, u32[]{:S(2)}, u32[]{:S(2)}) collective-permute-start(bf16[32,4224]{1,0:T(8,128)(2,1)S(1)} %maximum_maximum_fusion), channel_id=1, source_target_pairs={{0,2},{1,3},{2,0},{3,1},{4,6},{5,7},{6,4},{7,5},{8,10},{9,11},{10,... | collective-permute-start | bytes 811016 | tf_op jit(solution)/shard_map/ppermute | solution.py:108
  14.0 121.6 %collective-permute-start.11 = (bf16[6,96,1024]{2,1,0:T(8,128)(2,1)}, bf16[6,96,1024]{2,1,0:T(8,128)(2,1)S(1)}, u32[]{:S(2)}, u32[]{:S(2)}) collective-permute-start(bf16[6,96,1024]{2,1,0:T(8,128)(2,1)} %bitcast.59), channel_id=1, source_target_pairs={{0,5},{1,4},{2,7},{3,6},{4,1},{5,0},{6,3},{7,2},{8,13},{9,12},{10,... | collective-permute-start | bytes 3538952 | tf_op jit(solution)/shard_map/ppermute | solution.py:108
  22.8 126.8 %collective-permute-start.13 = (bf16[6,96,1024]{2,1,0:T(8,128)(2,1)}, bf16[6,96,1024]{2,1,0:T(8,128)(2,1)}, u32[]{:S(2)}, u32[]{:S(2)}) collective-permute-start(bf16[6,96,1024]{2,1,0:T(8,128)(2,1)} %bitcast.57), channel_id=1, source_target_pairs={{0,4},{1,5},{2,6},{3,7},{4,0},{5,1},{6,2},{7,3},{8,12},{9,13},{10,... | collective-permute-start | bytes 3538952 | tf_op jit(solution)/shard_map/ppermute | solution.py:108
  24.1 125.4 %collective-permute-start.14 = (bf16[6,96,1024]{2,1,0:T(8,128)(2,1)}, bf16[6,96,1024]{2,1,0:T(8,128)(2,1)}, u32[]{:S(2)}, u32[]{:S(2)}) collective-permute-start(bf16[6,96,1024]{2,1,0:T(8,128)(2,1)} %bitcast.58), channel_id=1, source_target_pairs={{0,3},{1,2},{2,1},{3,0},{4,7},{5,6},{6,5},{7,4},{8,11},{9,10},{10,... | collective-permute-start | bytes 3538952 | tf_op jit(solution)/shard_map/ppermute | solution.py:108
  27.2 147.5 %collective-permute-start.16 = (bf16[6,96,1024]{2,1,0:T(8,128)(2,1)}, bf16[6,96,1024]{2,1,0:T(8,128)(2,1)}, u32[]{:S(2)}, u32[]{:S(2)}) collective-permute-start(bf16[6,96,1024]{2,1,0:T(8,128)(2,1)} %bitcast.56), channel_id=1, source_target_pairs={{0,6},{1,7},{2,4},{3,5},{4,2},{5,3},{6,0},{7,1},{8,14},{9,15},{10,... | collective-permute-start | bytes 3538952 | tf_op jit(solution)/shard_map/ppermute | solution.py:108
  31.2 6.4 %collective-permute-start = (bf16[64,2048]{1,0:T(8,128)(2,1)S(1)}, bf16[64,2048]{1,0:T(8,128)(2,1)S(1)}, u32[]{:S(2)}, u32[]{:S(2)}) collective-permute-start(bf16[64,2048]{1,0:T(8,128)(2,1)S(1)} %get-tuple-element.83), channel_id=1, source_target_pairs={{0,16},{8,24},{16,0},{24,8},{1,17},{9,25},{17,1},{25,9},{2,18},{10... | collective-permute-start | bytes 786440 | tf_op jit(solution)/shard_map/cond/branch_1_fun/ppermute | solution.py:108
  37.8 2.4 %collective-permute-start.1 = (bf16[128,1024]{1,0:T(8,128)(2,1)S(1)}, bf16[128,1024]{1,0:T(8,128)(2,1)S(1)}, u32[]{:S(2)}, u32[]{:S(2)}) collective-permute-start(bf16[128,1024]{1,0:T(8,128)(2,1)S(1)} %get-tuple-element.85), channel_id=1, source_target_pairs={{0,8},{8,0},{16,24},{24,16},{1,9},{9,1},{17,25},{25,17},{2,10},{10... | collective-permute-start | bytes 786440 | tf_op jit(solution)/shard_map/cond/branch_1_fun/ppermute | solution.py:108
  41.0 18.2 %collective-permute-start.2 = (bf16[264,1024]{1,0:T(8,128)(2,1)}, bf16[264,1024]{1,0:T(8,128)(2,1)}, u32[]{:S(2)}, u32[]{:S(2)}) collective-permute-start(bf16[264,1024]{1,0:T(8,128)(2,1)} %pad_maximum_fusion.3), channel_id=1, source_target_pairs={{0,1},{1,0},{2,3},{3,2},{4,5},{5,4},{6,7},{7,6},{8,9},{9,8},{10,11... | collective-permute-start | bytes 1622024 | tf_op jit(solution)/shard_map/cond/branch_1_fun/ppermute | solution.py:108
  68.6 3.5 %collective-permute-start.3 = (bf16[256,3072]{1,0:T(8,128)(2,1)S(1)}, bf16[256,3072]{1,0:T(8,128)(2,1)S(1)}, u32[]{:S(2)}, u32[]{:S(2)}) collective-permute-start(bf16[256,3072]{1,0:T(8,128)(2,1)S(1)} %slice.69), channel_id=1, source_target_pairs={{0,8},{8,0},{16,24},{24,16},{1,9},{9,1},{17,25},{25,17},{2,10},{10... | collective-permute-start | bytes 4718600 | tf_op jit(solution)/shard_map/cond/branch_1_fun/ppermute | solution.py:108
  72.6 1.7 copy-start.1
  75.2 13.8 %slice-start = ((bf16[128,128]{0,1:T(8,128)(2,1)}), bf16[128,48]{0,1:T(8,128)(2,1)S(1)}, s32[]{:S(2)}) async-start(bf16[128,128]{0,1:T(8,128)(2,1)} %pad_maximum_fusion.6), calls=%async_computation | async-start | bytes 24576 | tf_op jit(solution)/shard_map/cond/branch_1_fun/slice | solution.py:207
  75.2 19.9 %collective-permute-start.4 = (bf16[128,3072]{1,0:T(8,128)(2,1)}, bf16[128,3072]{1,0:T(8,128)(2,1)}, u32[]{:S(2)}, u32[]{:S(2)}) collective-permute-start(bf16[128,3072]{1,0:T(8,128)(2,1)} %slice.150), channel_id=1, source_target_pairs={{0,16},{8,24},{16,0},{24,8},{1,17},{9,25},{17,1},{25,9},{2,18},{10... | collective-permute-start | bytes 2359304 | tf_op jit(solution)/shard_map/cond/branch_1_fun/ppermute | solution.py:108
  97.2 10.4 %collective-permute-start.5 = (bf16[128,1536]{1,0:T(8,128)(2,1)S(1)}, bf16[128,1536]{1,0:T(8,128)(2,1)S(1)}, u32[]{:S(2)}, u32[]{:S(2)}) collective-permute-start(bf16[128,1536]{1,0:T(8,128)(2,1)S(1)} %multiply_convert_fusion), channel_id=1, source_target_pairs={{0,16},{8,24},{16,0},{24,8},{1,17},{9,25},{17,1},{25,9},{2,18},{10... | collective-permute-start | bytes 1179656 | tf_op jit(solution)/shard_map/cond/branch_1_fun/ppermute | solution.py:108
  107.6 9.4 %collective-permute-start.6 = (bf16[256,1536]{1,0:T(8,128)(2,1)S(1)}, bf16[256,1536]{1,0:T(8,128)(2,1)}, u32[]{:S(2)}, u32[]{:S(2)}) collective-permute-start(bf16[256,1536]{1,0:T(8,128)(2,1)S(1)} %pad_maximum_fusion.2), channel_id=1, source_target_pairs={{0,8},{8,0},{16,24},{24,16},{1,9},{9,1},{17,25},{25,17},{2,10},{10... | collective-permute-start | bytes 2359304 | tf_op jit(solution)/shard_map/cond/branch_1_fun/ppermute | solution.py:108
  117.0 2.1 copy-start.2
  121.0 14.4 %collective-permute-start.7 = (bf16[4,64,1024]{2,1,0:T(8,128)(2,1)S(1)}, bf16[4,64,1024]{2,1,0:T(8,128)(2,1)S(1)}, u32[]{:S(2)}, u32[]{:S(2)}) collective-permute-start(bf16[4,64,1024]{2,1,0:T(8,128)(2,1)S(1)} %slice.151), channel_id=1, source_target_pairs={{0,1},{1,0},{2,3},{3,2},{4,5},{5,4},{6,7},{7,6},{8,9},{9,8},{10,11... | collective-permute-start | bytes 1572872 | tf_op jit(solution)/shard_map/cond/branch_1_fun/ppermute | solution.py:108
  135.6 1.0 copy-start.3
  137.4 12.0 %collective-permute-start.12 = (bf16[2,4,16,1024]{3,2,1,0:T(8,128)(2,1)}, bf16[2,4,16,1024]{3,2,1,0:T(8,128)(2,1)S(1)}, u32[]{:S(2)}, u32[]{:S(2)}) collective-permute-start(bf16[2,4,16,1024]{3,2,1,0:T(8,128)(2,1)} %slice.152), channel_id=1, source_target_pairs={{0,2},{1,3},{2,0},{3,1},{4,6},{5,7},{6,4},{7,5},{8,10},{9,11},{10,... | collective-permute-start | bytes 786440 | tf_op jit(solution)/shard_map/ppermute | solution.py:108
  142.3 3.2 %copy-start.4 = (bf16[6,96,1024]{2,1,0:T(8,128)(2,1)S(1)}, bf16[6,96,1024]{2,1,0:T(8,128)(2,1)}, u32[]{:S(2)}) copy-start(bf16[6,96,1024]{2,1,0:T(8,128)(2,1)} %copy-done.3) | copy-start | bytes 3538948
  145.5 7.8 %copy-start.6 = (bf16[6,96,1024]{2,1,0:T(8,128)(2,1)S(1)}, bf16[6,96,1024]{2,1,0:T(8,128)(2,1)}, u32[]{:S(2)}) copy-start(bf16[6,96,1024]{2,1,0:T(8,128)(2,1)} %get-tuple-element.74) | copy-start | bytes 3538948
  145.5 9.4 %copy-start.7 = (bf16[6,96,1024]{2,1,0:T(8,128)(2,1)S(1)}, bf16[6,96,1024]{2,1,0:T(8,128)(2,1)}, u32[]{:S(2)}) copy-start(bf16[6,96,1024]{2,1,0:T(8,128)(2,1)} %get-tuple-element.75) | copy-start | bytes 3538948
  145.5 9.7 %copy-start.5 = (bf16[6,96,1024]{2,1,0:T(8,128)(2,1)S(1)}, bf16[6,96,1024]{2,1,0:T(8,128)(2,1)}, u32[]{:S(2)}) copy-start(bf16[6,96,1024]{2,1,0:T(8,128)(2,1)} %get-tuple-element.76) | copy-start | bytes 3538948
  149.6 25.1 %collective-permute-start.15 = (bf16[1,4,16,1024]{3,2,1,0:T(8,128)(2,1)S(1)}, bf16[1,4,16,1024]{3,2,1,0:T(8,128)(2,1)S(1)}, u32[]{:S(2)}, u32[]{:S(2)}) collective-permute-start(bf16[1,4,16,1024]{3,2,1,0:T(8,128)(2,1)S(1)} %slice.153), channel_id=1, source_target_pairs={{0,4},{1,5},{2,6},{3,7},{4,0},{5,1},{6,2},{7,3},{8,12},{9,13},{10,... | collective-permute-start | bytes 393224 | tf_op jit(solution)/shard_map/ppermute | solution.py:108
  153.3 35.2 %collective-permute-start.17 = (bf16[6,96,1024]{2,1,0:T(8,128)(2,1)S(1)}, bf16[6,96,1024]{2,1,0:T(8,128)(2,1)S(1)}, u32[]{:S(2)}, u32[]{:S(2)}) collective-permute-start(bf16[6,96,1024]{2,1,0:T(8,128)(2,1)S(1)} %copy-done.6), channel_id=1, source_target_pairs={{0,1},{1,0},{2,3},{3,2},{4,5},{5,4},{6,7},{7,6},{8,9},{9,8},{10,11... | collective-permute-start | bytes 3538952 | tf_op jit(solution)/shard_map/ppermute | solution.py:108
  154.9 52.6 %collective-permute-start.18 = (bf16[6,96,1024]{2,1,0:T(8,128)(2,1)S(1)}, bf16[6,96,1024]{2,1,0:T(8,128)(2,1)S(1)}, u32[]{:S(2)}, u32[]{:S(2)}) collective-permute-start(bf16[6,96,1024]{2,1,0:T(8,128)(2,1)S(1)} %copy-done.7), channel_id=1, source_target_pairs={{0,2},{1,3},{2,0},{3,1},{4,6},{5,7},{6,4},{7,5},{8,10},{9,11},{10,... | collective-permute-start | bytes 3538952 | tf_op jit(solution)/shard_map/ppermute | solution.py:108
  155.2 69.6 %collective-permute-start.19 = (bf16[6,96,1024]{2,1,0:T(8,128)(2,1)S(1)}, bf16[6,96,1024]{2,1,0:T(8,128)(2,1)S(1)}, u32[]{:S(2)}, u32[]{:S(2)}) collective-permute-start(bf16[6,96,1024]{2,1,0:T(8,128)(2,1)S(1)} %copy-done.5), channel_id=1, source_target_pairs={{0,7},{1,6},{2,5},{3,4},{4,3},{5,2},{6,1},{7,0},{8,15},{9,14},{10,... | collective-permute-start | bytes 3538952 | tf_op jit(solution)/shard_map/ppermute | solution.py:108
  174.7 2.5 %collective-permute-start.20 = (bf16[32,1024]{1,0:T(8,128)(2,1)S(1)}, bf16[32,1024]{1,0:T(8,128)(2,1)S(1)}, u32[]{:S(2)}, u32[]{:S(2)}) collective-permute-start(bf16[32,1024]{1,0:T(8,128)(2,1)S(1)} %bitcast.67), channel_id=1, source_target_pairs={{0,8},{8,0},{16,24},{24,16},{1,9},{9,1},{17,25},{25,17},{2,10},{10... | collective-permute-start | bytes 196616 | tf_op jit(solution)/shard_map/ppermute | solution.py:108
  177.3 4.6 %collective-permute-start.21 = (bf16[16,2048]{1,0:T(8,128)(2,1)S(1)}, bf16[16,2048]{1,0:T(8,128)(2,1)S(1)}, u32[]{:S(2)}, u32[]{:S(2)}) collective-permute-start(bf16[16,2048]{1,0:T(8,128)(2,1)S(1)} %fusion.1), channel_id=1, source_target_pairs={{0,16},{8,24},{16,0},{24,8},{1,17},{9,25},{17,1},{25,9},{2,18},{10... | collective-permute-start | bytes 196616 | tf_op jit(solution)/shard_map/ppermute | solution.py:108

commit v6 on v5

--- a/solution.py
+++ b/solution.py
@@ -278,11 +278,11 @@
 
     out, *got = lax.cond(expert_ids[0, 0] >= 0, serve, idle, held, learner_rows, exponents)
     sent.update(zip(late, got))
-    out = after(out, first, arrived)
+    out = after(out, first + second, arrived)
 
     out = out.reshape(groups, -1, tok_rows, width).swapaxes(0, 1)
     out = halve(out, "expert", z_bits[1:])
-    out = after(out, second + begin, arrived)
+    out = after(out, begin, arrived)
     out = after(out, late, sent)
     send(late)
     out = halve(out, "expert", z_bits[:1])

time: 227 us -> 227 us (level)
  waiting for transfers between devices: 101 us -> 104 us
    ppermute x22, waiting for transfers between devices: 101 us -> 104 us  [swap(): lax.ppermute(value, axis, [(i, i ^ bit) for i in range(lax.axis_size(axis...]
where the time goes in v6:
time: 227 us; the launch traced here: 226 us
  waiting for transfers between devices  104 us (46%)
  Pallas kernels  51.9 us (23%)
  starting transfers between devices  28.3 us (12%)
  local copies, waits for them, and re-layouts  23.3 us (10%)
  other arithmetic  8.4 us (4%)
  matrix products  8.27 us (4%)
    ppermute x22, waiting for transfers between devices, swap(): lax.ppermute(value, axis, [(i, i ^ bit) for i in range(lax.axis_size(axis...  104 us
    ppermute x22, starting transfers between devices, swap(): lax.ppermute(value, axis, [(i, i ^ bit) for i in range(lax.axis_size(axis...  28.3 us
    pallas_call x2, Pallas kernels, dequantize(): pl.pallas_call(functools.partial(weights_kernel, first), out_shape=jax.Sh...  26.9 us
    pallas_call x8, Pallas kernels, encode(): pl.pallas_call(encode_kernel, out_shape=jax.ShapeDtypeStruct((per_owner,...  25 us
    dynamic_update_slice x7, local copies, waits for them, and re-layouts, place(): lax.dynamic_update_slice(elements, block, (0, (me[0] ^ partner) * block.s...  11.9 us
    dot_general x1, matrix products, layer(): lax.dot_general(held.reshape(groups * slots, width), pair.reshape(-1, wid...  6.48 us
  transfers between devices with their start and end apart: 22, of which 13 were waited for; matrix products, arithmetic and copies ran while one was open for 16% of the time, Pallas kernels for 23%

profile of v6, /device:TPU:8, one launch (start us, length us, event | category | flops | bytes accessed | tf_op | source)
XLA Modules:
  0.0 225.9 jit_solution(5721051118818555071)
XLA Ops:
  0.6 2.7 %collective-permute-start.8 = (bf16[16,4096]{1,0:T(8,128)(2,1)}, bf16[16,4096]{1,0:T(8,128)(2,1)S(1)}, u32[]{:S(2)}, u32[]{:S(2)}) collective-permute-start(bf16[16,4096]{1,0:T(8,128)(2,1)} %param.7), channel_id=1, source_target_pairs={{0,4},{1,5},{2,6},{3,7},{4,0},{5,1},{6,2},{7,3},{8,12},{9,13},{10,... | collective-permute-start | bytes 393224 | tf_op jit(solution)/shard_map/ppermute | solution.py:108
  3.3 0.7 reduce_sum.27
  4.0 0.7 broadcast_divide_fusion
  4.8 0.8 copy.42
  5.7 3.2 %shard_map.70 = bf16[2,3,96,1024]{3,2,1,0:T(8,128)(2,1)} custom-call(s32[1]{0:T(128)} %bitcast.15.me, bf16[16,3,96,1024]{3,2,1,0:T(8,128)(2,1)} %rows_ref.9, s32[16,3,32,96]{3,2,1,0:T(8,128)} %bitcast.38), custom_call_target="tpu_custom_call" | custom-call | flops 11796480 | bytes 2359296 | tf_op jit(solution)/shard_map/pallas_call | solution.py:53
  9.3 3.1 %shard_map.69 = bf16[2,3,96,1024]{3,2,1,0:T(8,128)(2,1)} custom-call(s32[1]{0:T(128)} %bitcast.15.me, bf16[16,3,96,1024]{3,2,1,0:T(8,128)(2,1)} %rows_ref.9, s32[16,3,32,96]{3,2,1,0:T(8,128)S(1)} %bitcast.39), custom_call_target="tpu_custom_call" | custom-call | flops 11796480 | bytes 2359296 | tf_op jit(solution)/shard_map/pallas_call | solution.py:53
  12.4 1.0 collective-permute-done.9
  14.0 2.5 %collective-permute-start.11 = (bf16[6,96,1024]{2,1,0:T(8,128)(2,1)}, bf16[6,96,1024]{2,1,0:T(8,128)(2,1)}, u32[]{:S(2)}, u32[]{:S(2)}) collective-permute-start(bf16[6,96,1024]{2,1,0:T(8,128)(2,1)} %bitcast.20), channel_id=1, source_target_pairs={{0,5},{1,4},{2,7},{3,6},{4,1},{5,0},{6,3},{7,2},{8,13},{9,12},{10,... | collective-permute-start | bytes 3538952 | tf_op jit(solution)/shard_map/ppermute | solution.py:108
  16.5 3.1 %shard_map.71 = bf16[2,3,96,1024]{3,2,1,0:T(8,128)(2,1)} custom-call(s32[1]{0:T(128)} %bitcast.15.me, bf16[16,3,96,1024]{3,2,1,0:T(8,128)(2,1)} %rows_ref.9, s32[16,3,32,96]{3,2,1,0:T(8,128)S(1)} %bitcast.40), custom_call_target="tpu_custom_call" | custom-call | flops 11796480 | bytes 2359296 | tf_op jit(solution)/shard_map/pallas_call | solution.py:53
  19.6 3.1 %shard_map.72 = bf16[2,3,96,1024]{3,2,1,0:T(8,128)(2,1)} custom-call(s32[1]{0:T(128)} %bitcast.15.me, bf16[16,3,96,1024]{3,2,1,0:T(8,128)(2,1)} %rows_ref.9, s32[16,3,32,96]{3,2,1,0:T(8,128)S(1)} %bitcast.41), custom_call_target="tpu_custom_call" | custom-call | flops 11796480 | bytes 2359296 | tf_op jit(solution)/shard_map/pallas_call | solution.py:53
  22.8 1.4 collective-permute-start.12
  24.2 3.0 %collective-permute-start.14 = (bf16[6,96,1024]{2,1,0:T(8,128)(2,1)}, bf16[6,96,1024]{2,1,0:T(8,128)(2,1)}, u32[]{:S(2)}, u32[]{:S(2)}) collective-permute-start(bf16[6,96,1024]{2,1,0:T(8,128)(2,1)} %bitcast.57), channel_id=1, source_target_pairs={{0,3},{1,2},{2,1},{3,0},{4,7},{5,6},{6,5},{7,4},{8,11},{9,10},{10,... | collective-permute-start | bytes 3538952 | tf_op jit(solution)/shard_map/ppermute | solution.py:108
  27.2 2.0 collective-permute-start.16
  29.1 1.2 slice.88
  31.0 104.6 %conditional.1 = (f32[4,64,1024]{2,1,0:T(8,128)S(1)}, bf16[6,96,1024]{2,1,0:T(8,128)(2,1)}, bf16[6,96,1024]{2,1,0:T(8,128)(2,1)}, bf16[6,96,1024]{2,1,0:T(8,128)(2,1)}) conditional(s32[]{:T(128)} %bitcast.18, (s32[1]{0:T(128)}, bf16[16,3,96,1024]{3,2,1,0:T(8,128)(2,1)}, s32[16,3,32,96]{3,2,1,0:T(8,128)S(1)}) %tuple.47, ...), branch_computations={%region_2.3_spmd, %region_3.5_spmd} | conditional | flops 5005043712 | bytes 126157312 | solution.py:279
  31.2 1.6 collective-permute-start
  32.8 4.9 %collective-permute-done = bf16[64,2048]{1,0:T(8,128)(2,1)S(1)} collective-permute-done((bf16[64,2048]{1,0:T(8,128)(2,1)S(1)}, bf16[64,2048]{1,0:T(8,128)(2,1)S(1)}, u32[]{:S(2)}, u32[]{:S(2)}) %collective-permute-start) | collective-permute-done | bytes 262176 | tf_op jit(solution)/shard_map/cond/branch_1_fun/ppermute | solution.py:108
  37.9 1.4 copy.44
  39.3 0.8 slice.101
  40.2 0.8 pad_maximum_fusion.3
  41.0 14.7 %branch_1_fun.5 = bf16[2,16,96,1024]{3,2,1,0:T(8,128)(2,1)} custom-call(bf16[16,3,96,1024]{3,2,1,0:T(8,128)(2,1)} %get-tuple-element.18.rows_ref, s32[16,3,32,96]{3,2,1,0:T(8,128)S(1)} %get-tuple-element.19.exponent_ref), custom_call_target="tpu_custom_call" | custom-call | flops 78643200 | bytes 12582912 | tf_op jit(solution)/shard_map/cond/branch_1_fun/pallas_call | solution.py:88
  55.7 3.5 %collective-permute-done.2 = bf16[264,1024]{1,0:T(8,128)(2,1)} collective-permute-done((bf16[264,1024]{1,0:T(8,128)(2,1)}, bf16[264,1024]{1,0:T(8,128)(2,1)}, u32[]{:S(2)}, u32[]{:S(2)}) %collective-permute-start.2) | collective-permute-done | bytes 540704 | tf_op jit(solution)/shard_map/cond/branch_1_fun/ppermute | solution.py:108
  59.2 0.7 slice.103
  60.1 0.7 pad_maximum_fusion.6
  60.8 1.1 slice.102
  61.9 6.5 %convolution_convert_fusion = bf16[512,3072]{1,0:T(8,128)(2,1)S(1)} fusion(bf16[512,1024]{1,0:T(8,128)(2,1)S(1)} %bitcast.65, bf16[3072,1024]{1,0:T(8,128)(2,1)} %bitcast.47), kind=kOutput, calls=%fused_computation | convolution fusion | flops 3222798336 | bytes 10485760 | tf_op jit(solution)/shard_map/cond/branch_1_fun/dot_general | solution.py:200
  68.7 3.3 %collective-permute-done.3 = bf16[256,3072]{1,0:T(8,128)(2,1)S(1)} collective-permute-done((bf16[256,3072]{1,0:T(8,128)(2,1)S(1)}, bf16[256,3072]{1,0:T(8,128)(2,1)S(1)}, u32[]{:S(2)}, u32[]{:S(2)}) %collective-permute-start.3) | collective-permute-done | bytes 1572896 | tf_op jit(solution)/shard_map/cond/branch_1_fun/ppermute | solution.py:108
  72.5 1.7 copy-done.1
  74.2 1.0 slice.150
  75.2 1.5 collective-permute-start.4
  76.7 12.2 %branch_1_fun.6 = bf16[1,16,96,1024]{3,2,1,0:T(8,128)(2,1)} custom-call(bf16[16,3,96,1024]{3,2,1,0:T(8,128)(2,1)} %get-tuple-element.18.rows_ref, s32[16,3,32,96]{3,2,1,0:T(8,128)S(1)} %get-tuple-element.19.exponent_ref), custom_call_target="tpu_custom_call" | custom-call | flops 39321600 | bytes 6291456 | tf_op jit(solution)/shard_map/cond/branch_1_fun/pallas_call | solution.py:88
  89.3 5.8 %collective-permute-done.4 = bf16[128,3072]{1,0:T(8,128)(2,1)} collective-permute-done((bf16[128,3072]{1,0:T(8,128)(2,1)}, bf16[128,3072]{1,0:T(8,128)(2,1)}, u32[]{:S(2)}, u32[]{:S(2)}) %collective-permute-start.4) | collective-permute-done | bytes 786464 | tf_op jit(solution)/shard_map/cond/branch_1_fun/ppermute | solution.py:108
  95.1 1.8 slice_add_fusion
  97.2 1.6 collective-permute-start.5
  98.7 8.8 %collective-permute-done.5 = bf16[128,1536]{1,0:T(8,128)(2,1)S(1)} collective-permute-done((bf16[128,1536]{1,0:T(8,128)(2,1)S(1)}, bf16[128,1536]{1,0:T(8,128)(2,1)S(1)}, u32[]{:S(2)}, u32[]{:S(2)}) %collective-permute-start.5) | collective-permute-done | bytes 393248 | tf_op jit(solution)/shard_map/cond/branch_1_fun/ppermute | solution.py:108
  107.7 3.1 %branch_1_fun.8 = bf16[2,3,96,1024]{3,2,1,0:T(8,128)(2,1)} custom-call(s32[1]{0:T(128)} %get-tuple-element.26.me, bf16[16,3,96,1024]{3,2,1,0:T(8,128)(2,1)} %get-tuple-element.18.rows_ref, s32[16,3,32,96]{3,2,1,0:T(8,128)S(1)} %get-tuple-element.19.exponent_ref), custom_call_target="tpu_custom_call" | custom-call | flops 11796480 | bytes 2359296 | tf_op jit(solution)/shard_map/cond/branch_1_fun/pallas_call | solution.py:53
  110.8 3.1 %branch_1_fun.9 = bf16[2,3,96,1024]{3,2,1,0:T(8,128)(2,1)} custom-call(s32[1]{0:T(128)} %get-tuple-element.26.me, bf16[16,3,96,1024]{3,2,1,0:T(8,128)(2,1)} %get-tuple-element.18.rows_ref, s32[16,3,32,96]{3,2,1,0:T(8,128)S(1)} %get-tuple-element.19.exponent_ref), custom_call_target="tpu_custom_call" | custom-call | flops 11796480 | bytes 2359296 | tf_op jit(solution)/shard_map/cond/branch_1_fun/pallas_call | solution.py:53
  113.9 3.1 %branch_1_fun.7 = bf16[2,3,96,1024]{3,2,1,0:T(8,128)(2,1)} custom-call(s32[1]{0:T(128)} %get-tuple-element.26.me, bf16[16,3,96,1024]{3,2,1,0:T(8,128)(2,1)} %get-tuple-element.18.rows_ref, s32[16,3,32,96]{3,2,1,0:T(8,128)S(1)} %get-tuple-element.19.exponent_ref), custom_call_target="tpu_custom_call" | custom-call | flops 11796480 | bytes 2359296 | tf_op jit(solution)/shard_map/cond/branch_1_fun/pallas_call | solution.py:53
  117.0 1.4 pad_maximum_fusion
  118.4 0.7 copy-done.2
  119.2 1.8 fusion.10
  121.0 0.6 collective-permute-start.7
  121.6 13.8 %collective-permute-done.7 = bf16[4,64,1024]{2,1,0:T(8,128)(2,1)S(1)} collective-permute-done((bf16[4,64,1024]{2,1,0:T(8,128)(2,1)S(1)}, bf16[4,64,1024]{2,1,0:T(8,128)(2,1)S(1)}, u32[]{:S(2)}, u32[]{:S(2)}) %collective-permute-start.7) | collective-permute-done | bytes 524320 | tf_op jit(solution)/shard_map/cond/branch_1_fun/ppermute | solution.py:108
  135.6 8.3 %collective-permute-done.12 = bf16[6,96,1024]{2,1,0:T(8,128)(2,1)S(1)} collective-permute-done((bf16[6,96,1024]{2,1,0:T(8,128)(2,1)}, bf16[6,96,1024]{2,1,0:T(8,128)(2,1)S(1)}, u32[]{:S(2)}, u32[]{:S(2)}) %collective-permute-start.12) | collective-permute-done | bytes 1179680 | tf_op jit(solution)/shard_map/ppermute | solution.py:108
  143.9 1.0 copy-done.3
  145.0 3.7 %collective-permute-start.13 = (bf16[2,4,16,1024]{3,2,1,0:T(8,128)(2,1)S(1)}, bf16[2,4,16,1024]{3,2,1,0:T(8,128)(2,1)S(1)}, u32[]{:S(2)}, u32[]{:S(2)}) collective-permute-start(bf16[2,4,16,1024]{3,2,1,0:T(8,128)(2,1)S(1)} %slice.152), channel_id=1, source_target_pairs={{0,2},{1,3},{2,0},{3,1},{4,6},{5,7},{6,4},{7,5},{8,10},{9,11},{10,... | collective-permute-start | bytes 786440 | tf_op jit(solution)/shard_map/ppermute | solution.py:108
  148.8 3.1 %shard_map.68 = bf16[2,3,768,1024]{3,2,1,0:T(8,128)(2,1)} custom-call(s32[1]{0:T(128)} %bitcast.15.me, bf16[16,3,96,1024]{3,2,1,0:T(8,128)(2,1)} %rows_ref.9, s32[16,3,32,96]{3,2,1,0:T(8,128)S(1)} %bitcast.44), custom_call_target="tpu_custom_call" | custom-call | flops 11796480 | bytes 2359296 | tf_op jit(solution)/shard_map/pallas_call | solution.py:53
  151.9 2.5 %constant_dynamic-update-slice_fusion.6 = bf16[6,768,1024]{2,1,0:T(8,128)(2,1)} fusion(bf16[6,768,1024]{2,1,0:T(8,128)(2,1)} %bitcast.45, bf16[6,96,1024]{2,1,0:T(8,128)(2,1)} %collective-permute-done.11, s32[]{:T(128)S(6)} %select_n.74), kind=kLoop, calls=%fused_computation.60 | loop fusion | bytes 2359300 | tf_op jit(solution)/shard_map/dynamic_update_slice | solution.py:104
  154.9 1.1 constant_dynamic-update-slice_fusion.5
  156.1 1.0 collective-permute-start.17
  157.1 1.3 collective-permute-start.18
  158.3 2.3 %collective-permute-start.19 = (bf16[6,96,1024]{2,1,0:T(8,128)(2,1)S(1)}, bf16[6,96,1024]{2,1,0:T(8,128)(2,1)S(1)}, u32[]{:S(2)}, u32[]{:S(2)}) collective-permute-start(bf16[6,96,1024]{2,1,0:T(8,128)(2,1)S(1)} %copy-done.5), channel_id=1, source_target_pairs={{0,7},{1,6},{2,5},{3,4},{4,3},{5,2},{6,1},{7,0},{8,15},{9,14},{10,... | collective-permute-start | bytes 3538952 | tf_op jit(solution)/shard_map/ppermute | solution.py:108
  160.7 14.0 %collective-permute-done.15 = bf16[1,4,16,1024]{3,2,1,0:T(8,128)(2,1)S(1)} collective-permute-done((bf16[1,4,16,1024]{3,2,1,0:T(8,128)(2,1)S(1)}, bf16[1,4,16,1024]{3,2,1,0:T(8,128)(2,1)S(1)}, u32[]{:S(2)}, u32[]{:S(2)}) %collective-permute-start.15) | collective-permute-done | bytes 131104 | tf_op jit(solution)/shard_map/ppermute | solution.py:108
  174.8 2.4 %constant_dynamic-update-slice_fusion.4 = bf16[6,768,1024]{2,1,0:T(8,128)(2,1)} fusion(bf16[6,768,1024]{2,1,0:T(8,128)(2,1)} %constant_dynamic-update-slice_fusion.5, bf16[6,96,1024]{2,1,0:T(8,128)(2,1)} %collective-permute-done.14, s32[]{:T(128)S(6)} %select_n.76), kind=kLoop, calls=%fused_computation.58 | loop fusion | bytes 2359300 | tf_op jit(solution)/shard_map/dynamic_update_slice | solution.py:104
  177.3 1.6 collective-permute-start.21
  178.9 2.4 %constant_dynamic-update-slice_fusion.3 = bf16[6,768,1024]{2,1,0:T(8,128)(2,1)} fusion(bf16[6,768,1024]{2,1,0:T(8,128)(2,1)} %constant_dynamic-update-slice_fusion.4, bf16[6,96,1024]{2,1,0:T(8,128)(2,1)} %collective-permute-done.16, s32[]{:T(128)S(6)} %select_n.77), kind=kLoop, calls=%fused_computation.57 | loop fusion | bytes 2359300 | tf_op jit(solution)/shard_map/dynamic_update_slice | solution.py:104
  181.3 0.5 collective-permute-done.21
  181.8 0.7 pad_maximum_fusion.9
  182.5 6.6 %collective-permute-done.17 = bf16[6,96,1024]{2,1,0:T(8,128)(2,1)S(1)} collective-permute-done((bf16[6,96,1024]{2,1,0:T(8,128)(2,1)S(1)}, bf16[6,96,1024]{2,1,0:T(8,128)(2,1)S(1)}, u32[]{:S(2)}, u32[]{:S(2)}) %collective-permute-start.17) | collective-permute-done | bytes 1179680 | tf_op jit(solution)/shard_map/ppermute | solution.py:108
  189.1 1.1 constant_dynamic-update-slice_fusion.2
  190.3 17.2 %collective-permute-done.18 = bf16[6,96,1024]{2,1,0:T(8,128)(2,1)S(1)} collective-permute-done((bf16[6,96,1024]{2,1,0:T(8,128)(2,1)S(1)}, bf16[6,96,1024]{2,1,0:T(8,128)(2,1)S(1)}, u32[]{:S(2)}, u32[]{:S(2)}) %collective-permute-start.18) | collective-permute-done | bytes 1179680 | tf_op jit(solution)/shard_map/ppermute | solution.py:108
  207.5 1.1 constant_dynamic-update-slice_fusion.1
  208.6 16.2 %collective-permute-done.19 = bf16[6,96,1024]{2,1,0:T(8,128)(2,1)S(1)} collective-permute-done((bf16[6,96,1024]{2,1,0:T(8,128)(2,1)S(1)}, bf16[6,96,1024]{2,1,0:T(8,128)(2,1)S(1)}, u32[]{:S(2)}, u32[]{:S(2)}) %collective-permute-start.19) | collective-permute-done | bytes 1179680 | tf_op jit(solution)/shard_map/ppermute | solution.py:108
  224.8 1.1 constant_dynamic-update-slice_fusion
  (67 shorter events, 4.3 us)
Async XLA Ops:
  0.6 11.8 %collective-permute-start.8 = (bf16[16,4096]{1,0:T(8,128)(2,1)}, bf16[16,4096]{1,0:T(8,128)(2,1)S(1)}, u32[]{:S(2)}, u32[]{:S(2)}) collective-permute-start(bf16[16,4096]{1,0:T(8,128)(2,1)} %param.7), channel_id=1, source_target_pairs={{0,4},{1,5},{2,6},{3,7},{4,0},{5,1},{6,2},{7,3},{8,12},{9,13},{10,... | collective-permute-start | bytes 393224 | tf_op jit(solution)/shard_map/ppermute | solution.py:108
  5.6 3.7 %copy-start = (s32[16,3,96,32]{2,3,1,0:T(8,128)S(1)}, s32[16,3,96,32]{2,3,1,0:T(8,128)}, u32[]{:S(2)}) copy-start(s32[16,3,96,32]{2,3,1,0:T(8,128)} %param.9) | copy-start | bytes 1769476
  8.9 3.5 %copy-start.8 = (bf16[16,4096]{1,0:T(8,128)(2,1)S(1)}, bf16[16,4096]{1,0:T(8,128)(2,1)}, u32[]{:S(2)}) copy-start(bf16[16,4096]{1,0:T(8,128)(2,1)} %param.7) | copy-start | bytes 393220
  9.0 4.5 %collective-permute-start.9 = (bf16[16,128]{1,0:T(8,128)(2,1)S(1)}, bf16[16,128]{1,0:T(8,128)(2,1)S(1)}, u32[]{:S(2)}, u32[]{:S(2)}) collective-permute-start(bf16[16,128]{1,0:T(8,128)(2,1)S(1)} %fusion.8), channel_id=1, source_target_pairs={{0,4},{1,5},{2,6},{3,7},{4,0},{5,1},{6,2},{7,3},{8,12},{9,13},{10,... | collective-permute-start | bytes 12296 | tf_op jit(solution)/shard_map/ppermute | solution.py:108
  13.5 10.6 %collective-permute-start.10 = (bf16[32,4224]{1,0:T(8,128)(2,1)S(1)}, bf16[32,4224]{1,0:T(8,128)(2,1)S(1)}, u32[]{:S(2)}, u32[]{:S(2)}) collective-permute-start(bf16[32,4224]{1,0:T(8,128)(2,1)S(1)} %maximum_maximum_fusion), channel_id=1, source_target_pairs={{0,2},{1,3},{2,0},{3,1},{4,6},{5,7},{6,4},{7,5},{8,10},{9,11},{10,... | collective-permute-start | bytes 811016 | tf_op jit(solution)/shard_map/ppermute | solution.py:108
  14.0 121.5 %collective-permute-start.11 = (bf16[6,96,1024]{2,1,0:T(8,128)(2,1)}, bf16[6,96,1024]{2,1,0:T(8,128)(2,1)}, u32[]{:S(2)}, u32[]{:S(2)}) collective-permute-start(bf16[6,96,1024]{2,1,0:T(8,128)(2,1)} %bitcast.20), channel_id=1, source_target_pairs={{0,5},{1,4},{2,7},{3,6},{4,1},{5,0},{6,3},{7,2},{8,13},{9,12},{10,... | collective-permute-start | bytes 3538952 | tf_op jit(solution)/shard_map/ppermute | solution.py:108
  22.8 121.1 %collective-permute-start.12 = (bf16[6,96,1024]{2,1,0:T(8,128)(2,1)}, bf16[6,96,1024]{2,1,0:T(8,128)(2,1)S(1)}, u32[]{:S(2)}, u32[]{:S(2)}) collective-permute-start(bf16[6,96,1024]{2,1,0:T(8,128)(2,1)} %bitcast.58), channel_id=1, source_target_pairs={{0,4},{1,5},{2,6},{3,7},{4,0},{5,1},{6,2},{7,3},{8,12},{9,13},{10,... | collective-permute-start | bytes 3538952 | tf_op jit(solution)/shard_map/ppermute | solution.py:108
  24.2 130.3 %collective-permute-start.14 = (bf16[6,96,1024]{2,1,0:T(8,128)(2,1)}, bf16[6,96,1024]{2,1,0:T(8,128)(2,1)}, u32[]{:S(2)}, u32[]{:S(2)}) collective-permute-start(bf16[6,96,1024]{2,1,0:T(8,128)(2,1)} %bitcast.57), channel_id=1, source_target_pairs={{0,3},{1,2},{2,1},{3,0},{4,7},{5,6},{6,5},{7,4},{8,11},{9,10},{10,... | collective-permute-start | bytes 3538952 | tf_op jit(solution)/shard_map/ppermute | solution.py:108
  27.2 147.5 %collective-permute-start.16 = (bf16[6,96,1024]{2,1,0:T(8,128)(2,1)}, bf16[6,96,1024]{2,1,0:T(8,128)(2,1)}, u32[]{:S(2)}, u32[]{:S(2)}) collective-permute-start(bf16[6,96,1024]{2,1,0:T(8,128)(2,1)} %bitcast.56), channel_id=1, source_target_pairs={{0,6},{1,7},{2,4},{3,5},{4,2},{5,3},{6,0},{7,1},{8,14},{9,15},{10,... | collective-permute-start | bytes 3538952 | tf_op jit(solution)/shard_map/ppermute | solution.py:108
  31.2 6.4 %collective-permute-start = (bf16[64,2048]{1,0:T(8,128)(2,1)S(1)}, bf16[64,2048]{1,0:T(8,128)(2,1)S(1)}, u32[]{:S(2)}, u32[]{:S(2)}) collective-permute-start(bf16[64,2048]{1,0:T(8,128)(2,1)S(1)} %get-tuple-element.83), channel_id=1, source_target_pairs={{0,16},{8,24},{16,0},{24,8},{1,17},{9,25},{17,1},{25,9},{2,18},{10... | collective-permute-start | bytes 786440 | tf_op jit(solution)/shard_map/cond/branch_1_fun/ppermute | solution.py:108
  37.8 2.4 %collective-permute-start.1 = (bf16[128,1024]{1,0:T(8,128)(2,1)S(1)}, bf16[128,1024]{1,0:T(8,128)(2,1)S(1)}, u32[]{:S(2)}, u32[]{:S(2)}) collective-permute-start(bf16[128,1024]{1,0:T(8,128)(2,1)S(1)} %get-tuple-element.85), channel_id=1, source_target_pairs={{0,8},{8,0},{16,24},{24,16},{1,9},{9,1},{17,25},{25,17},{2,10},{10... | collective-permute-start | bytes 786440 | tf_op jit(solution)/shard_map/cond/branch_1_fun/ppermute | solution.py:108
  41.0 18.2 %collective-permute-start.2 = (bf16[264,1024]{1,0:T(8,128)(2,1)}, bf16[264,1024]{1,0:T(8,128)(2,1)}, u32[]{:S(2)}, u32[]{:S(2)}) collective-permute-start(bf16[264,1024]{1,0:T(8,128)(2,1)} %pad_maximum_fusion.3), channel_id=1, source_target_pairs={{0,1},{1,0},{2,3},{3,2},{4,5},{5,4},{6,7},{7,6},{8,9},{9,8},{10,11... | collective-permute-start | bytes 1622024 | tf_op jit(solution)/shard_map/cond/branch_1_fun/ppermute | solution.py:108
  68.5 3.5 %collective-permute-start.3 = (bf16[256,3072]{1,0:T(8,128)(2,1)S(1)}, bf16[256,3072]{1,0:T(8,128)(2,1)S(1)}, u32[]{:S(2)}, u32[]{:S(2)}) collective-permute-start(bf16[256,3072]{1,0:T(8,128)(2,1)S(1)} %slice.69), channel_id=1, source_target_pairs={{0,8},{8,0},{16,24},{24,16},{1,9},{9,1},{17,25},{25,17},{2,10},{10... | collective-permute-start | bytes 4718600 | tf_op jit(solution)/shard_map/cond/branch_1_fun/ppermute | solution.py:108
  72.5 1.7 copy-start.1
  75.2 13.8 %slice-start = ((bf16[128,128]{0,1:T(8,128)(2,1)}), bf16[128,48]{0,1:T(8,128)(2,1)S(1)}, s32[]{:S(2)}) async-start(bf16[128,128]{0,1:T(8,128)(2,1)} %pad_maximum_fusion.6), calls=%async_computation | async-start | bytes 24576 | tf_op jit(solution)/shard_map/cond/branch_1_fun/slice | solution.py:207
  75.2 19.9 %collective-permute-start.4 = (bf16[128,3072]{1,0:T(8,128)(2,1)}, bf16[128,3072]{1,0:T(8,128)(2,1)}, u32[]{:S(2)}, u32[]{:S(2)}) collective-permute-start(bf16[128,3072]{1,0:T(8,128)(2,1)} %slice.150), channel_id=1, source_target_pairs={{0,16},{8,24},{16,0},{24,8},{1,17},{9,25},{17,1},{25,9},{2,18},{10... | collective-permute-start | bytes 2359304 | tf_op jit(solution)/shard_map/cond/branch_1_fun/ppermute | solution.py:108
  97.2 10.4 %collective-permute-start.5 = (bf16[128,1536]{1,0:T(8,128)(2,1)S(1)}, bf16[128,1536]{1,0:T(8,128)(2,1)S(1)}, u32[]{:S(2)}, u32[]{:S(2)}) collective-permute-start(bf16[128,1536]{1,0:T(8,128)(2,1)S(1)} %multiply_convert_fusion), channel_id=1, source_target_pairs={{0,16},{8,24},{16,0},{24,8},{1,17},{9,25},{17,1},{25,9},{2,18},{10... | collective-permute-start | bytes 1179656 | tf_op jit(solution)/shard_map/cond/branch_1_fun/ppermute | solution.py:108
  107.6 9.4 %collective-permute-start.6 = (bf16[256,1536]{1,0:T(8,128)(2,1)S(1)}, bf16[256,1536]{1,0:T(8,128)(2,1)}, u32[]{:S(2)}, u32[]{:S(2)}) collective-permute-start(bf16[256,1536]{1,0:T(8,128)(2,1)S(1)} %pad_maximum_fusion.2), channel_id=1, source_target_pairs={{0,8},{8,0},{16,24},{24,16},{1,9},{9,1},{17,25},{25,17},{2,10},{10... | collective-permute-start | bytes 2359304 | tf_op jit(solution)/shard_map/cond/branch_1_fun/ppermute | solution.py:108
  117.0 2.1 copy-start.2
  121.0 14.4 %collective-permute-start.7 = (bf16[4,64,1024]{2,1,0:T(8,128)(2,1)S(1)}, bf16[4,64,1024]{2,1,0:T(8,128)(2,1)S(1)}, u32[]{:S(2)}, u32[]{:S(2)}) collective-permute-start(bf16[4,64,1024]{2,1,0:T(8,128)(2,1)S(1)} %slice.151), channel_id=1, source_target_pairs={{0,1},{1,0},{2,3},{3,2},{4,5},{5,4},{6,7},{7,6},{8,9},{9,8},{10,11... | collective-permute-start | bytes 1572872 | tf_op jit(solution)/shard_map/cond/branch_1_fun/ppermute | solution.py:108
  143.9 1.0 copy-start.3
  145.0 9.3 %collective-permute-start.13 = (bf16[2,4,16,1024]{3,2,1,0:T(8,128)(2,1)S(1)}, bf16[2,4,16,1024]{3,2,1,0:T(8,128)(2,1)S(1)}, u32[]{:S(2)}, u32[]{:S(2)}) collective-permute-start(bf16[2,4,16,1024]{3,2,1,0:T(8,128)(2,1)S(1)} %slice.152), channel_id=1, source_target_pairs={{0,2},{1,3},{2,0},{3,1},{4,6},{5,7},{6,4},{7,5},{8,10},{9,11},{10,... | collective-permute-start | bytes 786440 | tf_op jit(solution)/shard_map/ppermute | solution.py:108
  151.9 3.1 %copy-start.4 = (bf16[6,96,1024]{2,1,0:T(8,128)(2,1)S(1)}, bf16[6,96,1024]{2,1,0:T(8,128)(2,1)}, u32[]{:S(2)}) copy-start(bf16[6,96,1024]{2,1,0:T(8,128)(2,1)} %copy-done.3) | copy-start | bytes 3538948
  154.4 2.7 %copy-start.7 = (bf16[6,96,1024]{2,1,0:T(8,128)(2,1)S(1)}, bf16[6,96,1024]{2,1,0:T(8,128)(2,1)}, u32[]{:S(2)}) copy-start(bf16[6,96,1024]{2,1,0:T(8,128)(2,1)} %get-tuple-element.75) | copy-start | bytes 3538948
  154.5 1.6 copy-start.6
  154.5 3.9 %copy-start.5 = (bf16[6,96,1024]{2,1,0:T(8,128)(2,1)S(1)}, bf16[6,96,1024]{2,1,0:T(8,128)(2,1)}, u32[]{:S(2)}) copy-start(bf16[6,96,1024]{2,1,0:T(8,128)(2,1)} %get-tuple-element.76) | copy-start | bytes 3538948
  154.5 20.1 %collective-permute-start.15 = (bf16[1,4,16,1024]{3,2,1,0:T(8,128)(2,1)S(1)}, bf16[1,4,16,1024]{3,2,1,0:T(8,128)(2,1)S(1)}, u32[]{:S(2)}, u32[]{:S(2)}) collective-permute-start(bf16[1,4,16,1024]{3,2,1,0:T(8,128)(2,1)S(1)} %slice.153), channel_id=1, source_target_pairs={{0,4},{1,5},{2,6},{3,7},{4,0},{5,1},{6,2},{7,3},{8,12},{9,13},{10,... | collective-permute-start | bytes 393224 | tf_op jit(solution)/shard_map/ppermute | solution.py:108
  156.1 33.0 %collective-permute-start.17 = (bf16[6,96,1024]{2,1,0:T(8,128)(2,1)S(1)}, bf16[6,96,1024]{2,1,0:T(8,128)(2,1)S(1)}, u32[]{:S(2)}, u32[]{:S(2)}) collective-permute-start(bf16[6,96,1024]{2,1,0:T(8,128)(2,1)S(1)} %copy-done.6), channel_id=1, source_target_pairs={{0,1},{1,0},{2,3},{3,2},{4,5},{5,4},{6,7},{7,6},{8,9},{9,8},{10,11... | collective-permute-start | bytes 3538952 | tf_op jit(solution)/shard_map/ppermute | solution.py:108
  157.1 50.4 %collective-permute-start.18 = (bf16[6,96,1024]{2,1,0:T(8,128)(2,1)S(1)}, bf16[6,96,1024]{2,1,0:T(8,128)(2,1)S(1)}, u32[]{:S(2)}, u32[]{:S(2)}) collective-permute-start(bf16[6,96,1024]{2,1,0:T(8,128)(2,1)S(1)} %copy-done.7), channel_id=1, source_target_pairs={{0,2},{1,3},{2,0},{3,1},{4,6},{5,7},{6,4},{7,5},{8,10},{9,11},{10,... | collective-permute-start | bytes 3538952 | tf_op jit(solution)/shard_map/ppermute | solution.py:108
  158.3 66.5 %collective-permute-start.19 = (bf16[6,96,1024]{2,1,0:T(8,128)(2,1)S(1)}, bf16[6,96,1024]{2,1,0:T(8,128)(2,1)S(1)}, u32[]{:S(2)}, u32[]{:S(2)}) collective-permute-start(bf16[6,96,1024]{2,1,0:T(8,128)(2,1)S(1)} %copy-done.5), channel_id=1, source_target_pairs={{0,7},{1,6},{2,5},{3,4},{4,3},{5,2},{6,1},{7,0},{8,15},{9,14},{10,... | collective-permute-start | bytes 3538952 | tf_op jit(solution)/shard_map/ppermute | solution.py:108
  174.7 2.5 %collective-permute-start.20 = (bf16[32,1024]{1,0:T(8,128)(2,1)S(1)}, bf16[32,1024]{1,0:T(8,128)(2,1)S(1)}, u32[]{:S(2)}, u32[]{:S(2)}) collective-permute-start(bf16[32,1024]{1,0:T(8,128)(2,1)S(1)} %bitcast.66), channel_id=1, source_target_pairs={{0,8},{8,0},{16,24},{24,16},{1,9},{9,1},{17,25},{25,17},{2,10},{10... | collective-permute-start | bytes 196616 | tf_op jit(solution)/shard_map/ppermute | solution.py:108
  177.3 4.6 %collective-permute-start.21 = (bf16[16,2048]{1,0:T(8,128)(2,1)S(1)}, bf16[16,2048]{1,0:T(8,128)(2,1)S(1)}, u32[]{:S(2)}, u32[]{:S(2)}) collective-permute-start(bf16[16,2048]{1,0:T(8,128)(2,1)S(1)} %fusion.1), channel_id=1, source_target_pairs={{0,16},{8,24},{16,0},{24,8},{1,17},{9,25},{17,1},{25,9},{2,18},{10... | collective-permute-start | bytes 196616 | tf_op jit(solution)/shard_map/ppermute | solution.py:108
